TPU v7x, 256 devices: a whole 4x4x8 slice. The times are simulated.
256 devices in a mesh: tile: 64 (over y, x_hi, z), mem: 4 (over x_lo, core).
Axes of the slice: x: 4 (x_hi: 2, x_lo: 2; x = x_hi * 2 + x_lo), y: 4, z: 8, core: 2. Of those that a mesh axis runs over, the one named last changes fastest.
Arguments:
- prior: float32 [64, 256, 48, 128], P('mem', 'tile'), may hold values from -1 to 1
- base_flow: float32 [256, 48, 128], P('tile'), may hold values from -4 to 4
- base_visc: float32 [256, 48, 128], P('tile'), may hold values from 0.02 to 0.05
- probe_cells: int32 [64, 4], P('tile'), may hold values from 0 to 24575
- obs_slot: int32 [256], replicated, may hold values from 0 to 255, each once
- obs_values: float32 [256], replicated, may hold values from -6 to 6
- obs_var: float32 [256], replicated, may hold values from 0.05 to 0.5
- obs_noise: float32 [64, 256], replicated, may hold values from -5 to 5
Outputs:
- velocity: float32 [64, 256, 48, 128], P('mem', 'tile')
- posterior: float32 [64, 256, 48, 128], P('mem', 'tile')
Inputs may be any that keep to these rules, and one draw needn't show every extreme that they name: `obs_slot`: each slot appears once.
All inputs are finite; a program needn't handle non-finite values.
Results may differ from a plain program's by a relative error of at most 0.00095.
The roundings to bfloat16 on the way count: a program that leaves them out, or rounds other values in their place, can miss the bound.
Values may be sent and summed in bfloat16 or wider, within the bound.
No kernel may reach another device: no remote copies, remote signals or barrier semaphores. Data moves between devices by JAX's collectives and lax.ppermute only.
A program may use at most 64 MiB of HBM per device.

v0:
```python
import jax
import jax.numpy as jnp
from jax import lax
from jax.sharding import PartitionSpec as P

ITERS = 4


def extended(cells, sides, width):
    for axis, dim in sides:
        count = lax.axis_size(axis)
        head = lax.slice_in_dim(cells, 0, width, axis=dim)
        tail = lax.slice_in_dim(cells, cells.shape[dim] - width, cells.shape[dim], axis=dim)
        cells = jnp.concatenate(
            [
                lax.ppermute(tail, axis, [(i, (i + 1) % count) for i in range(count)]),
                cells,
                lax.ppermute(head, axis, [((i + 1) % count, i) for i in range(count)]),
            ],
            axis=dim,
        )
    return cells


def relax_step(centre, behind, ahead, viscosity):
    spanwise = jnp.roll(centre, 1, -2) + jnp.roll(centre, -1, -2)
    widths = [(0, 0)] * (centre.ndim - 1) + [(1, 1)]
    padded = jnp.pad(centre, widths)
    normal = padded[..., 2:] + padded[..., :-2]
    laplace = behind + ahead + spanwise + normal - 6.0 * centre
    return centre + viscosity * laplace - 0.15 * (centre - behind) + 0.01


def per_device(prior, base_flow, base_visc, probe_cells, obs_slot, obs_values, obs_var, obs_noise):
    members_here = prior.shape[0]
    members = members_here * lax.axis_size("mem")
    viscosity = base_visc[None] * jnp.exp(prior)
    speed = jnp.broadcast_to(base_flow[None], prior.shape)
    for sweep in range(ITERS):
        padded = extended(speed, (("tile", 1),), 1)
        speed = relax_step(speed, padded[:, :-2], padded[:, 2:], viscosity)
    flat_speed = speed.reshape(members_here, -1)
    local_probes = flat_speed[:, probe_cells[0]]
    member_vals = lax.all_gather(local_probes, "mem", axis=0, tiled=True)
    identity = (members - 1.0) * jnp.eye(members, dtype=jnp.float32)
    all_vals = lax.all_gather(member_vals, "tile", axis=1, tiled=True)
    predicted = all_vals[:, obs_slot]
    spread_obs = predicted - jnp.sum(predicted, 0) / members
    scaled = spread_obs / obs_var[None, :]
    innovation = obs_values[None, :] + jnp.sqrt(obs_var)[None, :] * obs_noise - predicted
    gram = jnp.dot(scaled, spread_obs.T, precision=lax.Precision.HIGHEST) + identity
    rhs = jnp.dot(scaled, innovation.T, precision=lax.Precision.HIGHEST)
    factor = jnp.linalg.cholesky(gram)
    weights = jax.scipy.linalg.cho_solve((factor, True), rhs).astype(jnp.bfloat16)
    member_total = lax.psum(jnp.sum(prior, 0), "mem")
    anomaly = (prior - member_total[None] / members).astype(jnp.bfloat16)
    first_member = lax.axis_index("mem") * members_here
    my_cols = lax.dynamic_slice_in_dim(weights, first_member, members_here, 1)
    update = jnp.einsum(
        "km,kxzy->mxzy",
        my_cols,
        lax.all_gather(anomaly, "mem", axis=0, tiled=True),
        preferred_element_type=jnp.float32,
    )
    return (speed, prior + update)


def solution(mesh):
    placed = (
        P("mem", "tile", None, None),
        P("tile", None, None),
        P("tile", None, None),
        P("tile", None),
        P(),
        P(),
        P(),
        P(),
    )
    return jax.shard_map(
        per_device,
        mesh=mesh,
        in_specs=placed,
        out_specs=(P("mem", "tile", None, None), P("mem", "tile", None, None)),
        check_vma=False,
    )
```

profile of v0, /device:TPU:2, one launch (start us, length us, event | category | flops | bytes accessed | tf_op | source)
XLA Modules:
  0.0 353.1 jit_solution(582325917830929939)
XLA Ops:
  8.0 2.0 collective-permute-start
  10.0 8.0 %collective-permute-start.1 = (f32[16,1,48,128]{3,2,1,0:T(8,128)S(1)}, f32[16,1,48,128]{3,2,1,0:T(8,128)S(1)}, u32[]{:S(2)}, u32[]{:S(2)}) collective-permute-start(f32[16,1,48,128]{3,2,1,0:T(8,128)S(1)} %broadcast_in_dim.34), channel_id=1, source_target_pairs={{4,0},{8,4},{12,8},{16,12},{20,16},{24,20},{28,24},{32,28},{36,32}... | collective-permute-start | bytes 1179656 | tf_op jit(solution)/shard_map/ppermute | solution.py:18
  20.7 6.4 %collective-permute-done = f32[16,1,48,128]{3,2,1,0:T(8,128)S(1)} collective-permute-done((f32[16,1,48,128]{3,2,1,0:T(8,128)S(1)}, f32[16,1,48,128]{3,2,1,0:T(8,128)S(1)}, u32[]{:S(2)}, u32[]{:S(2)}) %collective-permute-start) | collective-permute-done | bytes 393248 | tf_op jit(solution)/shard_map/ppermute | solution.py:16
  28.6 1.5 fusion.27
  30.3 7.7 %collective-permute-start.3 = (f32[16,1,48,128]{3,2,1,0:T(8,128)S(1)}, f32[16,1,48,128]{3,2,1,0:T(8,128)S(1)}, u32[]{:S(2)}, u32[]{:S(2)}) collective-permute-start(f32[16,1,48,128]{3,2,1,0:T(8,128)S(1)} %get-tuple-element.27), channel_id=1, source_target_pairs={{4,0},{8,4},{12,8},{16,12},{20,16},{24,20},{28,24},{32,28},{36,32}... | collective-permute-start | bytes 1179656 | tf_op jit(solution)/shard_map/ppermute | solution.py:18
  38.4 7.9 %collective-permute-done.2 = f32[16,1,48,128]{3,2,1,0:T(8,128)S(1)} collective-permute-done((f32[16,1,48,128]{3,2,1,0:T(8,128)S(1)}, f32[16,1,48,128]{3,2,1,0:T(8,128)S(1)}, u32[]{:S(2)}, u32[]{:S(2)}) %collective-permute-start.2) | collective-permute-done | bytes 393248 | tf_op jit(solution)/shard_map/ppermute | solution.py:16
  46.3 2.2 fusion.68
  48.5 38.8 %all-reduce.6.cloned.1.call-done = f32[4,48,128]{2,1,0:T(8,128)} async-done(((f32[4,48,128]{2,1,0:T(8,128)}), f32[4,48,128]{2,1,0:T(8,128)}) %all-reduce.6.cloned.1.call-update) | async-done | bytes 98320 | tf_op jit(solution)/shard_map/psum | solution.py:55
  88.3 1.9 subtract_convert_fusion
  90.5 1.7 collective-permute-start.4
  92.1 6.1 %collective-permute-start.5 = (f32[16,1,48,128]{3,2,1,0:T(8,128)S(1)}, f32[16,1,48,128]{3,2,1,0:T(8,128)S(1)}, u32[]{:S(2)}, u32[]{:S(2)}) collective-permute-start(f32[16,1,48,128]{3,2,1,0:T(8,128)S(1)} %get-tuple-element.21), channel_id=1, source_target_pairs={{4,0},{8,4},{12,8},{16,12},{20,16},{24,20},{28,24},{32,28},{36,32}... | collective-permute-start | bytes 1179656 | tf_op jit(solution)/shard_map/ppermute | solution.py:18
  98.7 9.3 %collective-permute-done.4 = f32[16,1,48,128]{3,2,1,0:T(8,128)S(1)} collective-permute-done((f32[16,1,48,128]{3,2,1,0:T(8,128)S(1)}, f32[16,1,48,128]{3,2,1,0:T(8,128)S(1)}, u32[]{:S(2)}, u32[]{:S(2)}) %collective-permute-start.4) | collective-permute-done | bytes 393248 | tf_op jit(solution)/shard_map/ppermute | solution.py:16
  108.0 1.5 fusion.13
  109.6 7.8 %collective-permute-start.7 = (f32[16,1,48,128]{3,2,1,0:T(8,128)S(1)}, f32[16,1,48,128]{3,2,1,0:T(8,128)S(1)}, u32[]{:S(2)}, u32[]{:S(2)}) collective-permute-start(f32[16,1,48,128]{3,2,1,0:T(8,128)S(1)} %get-tuple-element.15), channel_id=1, source_target_pairs={{4,0},{8,4},{12,8},{16,12},{20,16},{24,20},{28,24},{32,28},{36,32}... | collective-permute-start | bytes 1179656 | tf_op jit(solution)/shard_map/ppermute | solution.py:18
  117.9 8.4 %collective-permute-done.6 = f32[16,1,48,128]{3,2,1,0:T(8,128)S(1)} collective-permute-done((f32[16,1,48,128]{3,2,1,0:T(8,128)S(1)}, f32[16,1,48,128]{3,2,1,0:T(8,128)S(1)}, u32[]{:S(2)}, u32[]{:S(2)}) %collective-permute-start.6) | collective-permute-done | bytes 393248 | tf_op jit(solution)/shard_map/ppermute | solution.py:16
  126.3 1.5 fusion.20
  127.8 6.6 %copy.23 = f32[16,4,48,128]{0,3,2,1:T(8,128)} copy(f32[16,4,48,128]{3,2,1,0:T(8,128)S(1)} %fusion.20) | data formatting | bytes 3145728 | tf_op jit(solution)/shard_map/add | solution.py:31
  134.5 5.1 %gather_fusion = f32[4,16]{1,0:T(4,128)S(1)} fusion(f32[16,24576]{0,1:T(8,128)} %bitcast.52, s32[1024]{0:T(1024)S(1)} %pad_clamp_fusion.1), kind=kCustom, calls=%fused_computation | custom fusion | bytes 528 | tf_op jit(solution)/shard_map/gather | solution.py:43
  139.6 5.2 %all-gather.2 = f32[4,16,4]{1,2,0:T(4,128)S(1)} all-gather(f32[1,16,4]{1,2,0:T(4,128)S(1)} %bitcast.54), channel_id=2, replica_groups=mesh['tile'=64,'mem'=4] {'mem'}, dimensions={0}, use_global_device_ids=true | all-gather | bytes 1280 | tf_op jit(solution)/shard_map/all_gather | solution.py:44
  144.9 182.1 %all-gather.3 = f32[64,4,64]{2,1,0:T(4,128)S(1)} all-gather(f32[1,4,64]{2,1,0:T(4,128)S(1)} %bitcast.55), channel_id=3, replica_groups=mesh['tile'=64,'mem'=4] {'tile'}, dimensions={0}, use_global_device_ids=true | all-gather | bytes 66560 | tf_op jit(solution)/shard_map/all_gather | solution.py:46
  328.4 5.8 %cholesky.16 = f32[64,64]{1,0:T(8,128)S(1)} custom-call(f32[64,64]{1,0:T(8,128)S(1)} %fusion.63), custom_call_target="Cholesky" | custom-call | tf_op jit(solution)/shard_map/jit(cholesky)/cholesky | solution.py:53
  335.6 4.9 %custom-call.10 = f32[1,64,64]{1,2,0:T(8,128)S(1)} custom-call(f32[1,64,64]{2,1,0:T(8,128)S(1)} %fusion.57), custom_call_target="InvertDiagBlocksLowerTriangular" | custom-call | tf_op jit(solution)/shard_map/jit(_cho_solve)/triangular_solve | solution.py:54
  341.6 3.0 convolution_add_fusion
  344.6 1.6 copy.29
  (70 shorter events, 11.6 us)
Async XLA Ops:
  7.2 80.2 %all-reduce.6.cloned.1.call-start = ((), (), s32[]{:S(2)}) async-start(), calls=%async_computation | async-start | bytes 196608 | tf_op jit(solution)/shard_map/psum | solution.py:55
  8.0 19.1 %collective-permute-start = (f32[16,1,48,128]{3,2,1,0:T(8,128)S(1)}, f32[16,1,48,128]{3,2,1,0:T(8,128)S(1)}, u32[]{:S(2)}, u32[]{:S(2)}) collective-permute-start(f32[16,1,48,128]{3,2,1,0:T(8,128)S(1)} %broadcast_in_dim.33), channel_id=1, source_target_pairs={{0,4},{4,8},{8,12},{12,16},{16,20},{20,24},{24,28},{28,32},{32,36}... | collective-permute-start | bytes 1179656 | tf_op jit(solution)/shard_map/ppermute | solution.py:16
  10.0 17.0 %collective-permute-start.1 = (f32[16,1,48,128]{3,2,1,0:T(8,128)S(1)}, f32[16,1,48,128]{3,2,1,0:T(8,128)S(1)}, u32[]{:S(2)}, u32[]{:S(2)}) collective-permute-start(f32[16,1,48,128]{3,2,1,0:T(8,128)S(1)} %broadcast_in_dim.34), channel_id=1, source_target_pairs={{4,0},{8,4},{12,8},{16,12},{20,16},{24,20},{28,24},{32,28},{36,32}... | collective-permute-start | bytes 1179656 | tf_op jit(solution)/shard_map/ppermute | solution.py:18
  27.1 0.9 copy-start.2
  27.2 1.4 copy-start
  27.2 1.4 copy-start.3
  30.2 16.1 %collective-permute-start.2 = (f32[16,1,48,128]{3,2,1,0:T(8,128)S(1)}, f32[16,1,48,128]{3,2,1,0:T(8,128)S(1)}, u32[]{:S(2)}, u32[]{:S(2)}) collective-permute-start(f32[16,1,48,128]{3,2,1,0:T(8,128)S(1)} %get-tuple-element.26), channel_id=1, source_target_pairs={{0,4},{4,8},{8,12},{12,16},{16,20},{20,24},{24,28},{28,32},{32,36}... | collective-permute-start | bytes 1179656 | tf_op jit(solution)/shard_map/ppermute | solution.py:16
  30.3 16.0 %collective-permute-start.3 = (f32[16,1,48,128]{3,2,1,0:T(8,128)S(1)}, f32[16,1,48,128]{3,2,1,0:T(8,128)S(1)}, u32[]{:S(2)}, u32[]{:S(2)}) collective-permute-start(f32[16,1,48,128]{3,2,1,0:T(8,128)S(1)} %get-tuple-element.27), channel_id=1, source_target_pairs={{4,0},{8,4},{12,8},{16,12},{20,16},{24,20},{28,24},{32,28},{36,32}... | collective-permute-start | bytes 1179656 | tf_op jit(solution)/shard_map/ppermute | solution.py:18
  46.3 2.2 copy-start.5
  48.5 293.1 %all-gather.6.cloned.1.call-start = ((), (), s32[]{:S(2)}) async-start(), calls=%async_computation.1 | async-start | bytes 3932160 | tf_op jit(solution)/shard_map/all_gather | solution.py:62
  88.3 1.9 copy-start.8
  88.3 2.0 copy-start.4
  88.3 2.1 copy-start.6
  90.5 17.5 %collective-permute-start.4 = (f32[16,1,48,128]{3,2,1,0:T(8,128)S(1)}, f32[16,1,48,128]{3,2,1,0:T(8,128)S(1)}, u32[]{:S(2)}, u32[]{:S(2)}) collective-permute-start(f32[16,1,48,128]{3,2,1,0:T(8,128)S(1)} %get-tuple-element.20), channel_id=1, source_target_pairs={{0,4},{4,8},{8,12},{12,16},{16,20},{20,24},{24,28},{28,32},{32,36}... | collective-permute-start | bytes 1179656 | tf_op jit(solution)/shard_map/ppermute | solution.py:16
  92.1 15.8 %collective-permute-start.5 = (f32[16,1,48,128]{3,2,1,0:T(8,128)S(1)}, f32[16,1,48,128]{3,2,1,0:T(8,128)S(1)}, u32[]{:S(2)}, u32[]{:S(2)}) collective-permute-start(f32[16,1,48,128]{3,2,1,0:T(8,128)S(1)} %get-tuple-element.21), channel_id=1, source_target_pairs={{4,0},{8,4},{12,8},{16,12},{20,16},{24,20},{28,24},{32,28},{36,32}... | collective-permute-start | bytes 1179656 | tf_op jit(solution)/shard_map/ppermute | solution.py:18
  109.5 16.8 %collective-permute-start.6 = (f32[16,1,48,128]{3,2,1,0:T(8,128)S(1)}, f32[16,1,48,128]{3,2,1,0:T(8,128)S(1)}, u32[]{:S(2)}, u32[]{:S(2)}) collective-permute-start(f32[16,1,48,128]{3,2,1,0:T(8,128)S(1)} %get-tuple-element.14), channel_id=1, source_target_pairs={{0,4},{4,8},{8,12},{12,16},{16,20},{20,24},{24,28},{28,32},{32,36}... | collective-permute-start | bytes 1179656 | tf_op jit(solution)/shard_map/ppermute | solution.py:16
  109.6 16.7 %collective-permute-start.7 = (f32[16,1,48,128]{3,2,1,0:T(8,128)S(1)}, f32[16,1,48,128]{3,2,1,0:T(8,128)S(1)}, u32[]{:S(2)}, u32[]{:S(2)}) collective-permute-start(f32[16,1,48,128]{3,2,1,0:T(8,128)S(1)} %get-tuple-element.15), channel_id=1, source_target_pairs={{4,0},{8,4},{12,8},{16,12},{20,16},{24,20},{28,24},{32,28},{36,32}... | collective-permute-start | bytes 1179656 | tf_op jit(solution)/shard_map/ppermute | solution.py:18
  127.8 6.7 %copy-start.1 = (f32[16,4,48,128]{3,2,1,0:T(8,128)}, f32[16,4,48,128]{3,2,1,0:T(8,128)S(1)}, u32[]{:S(2)}) copy-start(f32[16,4,48,128]{3,2,1,0:T(8,128)S(1)} %fusion.20) | copy-start | bytes 4718596
  134.5 206.1 %copy-start.7 = (f32[256]{0:T(256)S(1)}, f32[256]{0:T(256)}, u32[]{:S(2)}) copy-start(f32[256]{0:T(256)} %param.13) | copy-start | bytes 3076
Sparse Core Ops, SparseCore 0:
  48.6 38.7 all-reduce.5
  90.3 48.9 all-gather.5
where the time goes:
time: 354 us; the launch traced here: 353 us
  blocking collectives  187 us (53%)
  waiting for transfers between devices  70.8 us (20%)
  starting transfers between devices  33.7 us (10%)
  other arithmetic  22.5 us (6%)
  local copies, waits for them, and re-layouts  19.9 us (6%)
  between operations  14.4 us (4%)
  matrix products  4.6 us (1%)
    all_gather x1, blocking collectives, per_device(): all_vals = lax.all_gather(member_vals, 'tile', axis=1, tiled=True)  182 us
    psum x1, waiting for transfers between devices, per_device(): member_total = lax.psum(jnp.sum(prior, 0), 'mem')  38.8 us
    ppermute x4, waiting for transfers between devices, extended(): lax.ppermute(tail, axis, [(i, (i + 1) % count) for i in range(count)])  32 us
    ppermute x4, starting transfers between devices, extended(): lax.ppermute(head, axis, [((i + 1) % count, i) for i in range(count)])  29.8 us
  transfers between devices with their start and end apart: 10, of which 5 were waited for; matrix products, arithmetic and copies ran while one was open for 9% of the time, Pallas kernels for 0%

commit v1 on v0

v1 whole, which is shorter than its diff:
```python
import functools
import math

import jax
import jax.numpy as jnp
from jax import lax
from jax.experimental import pallas as pl
from jax.experimental.pallas import tpu as pltpu
from jax.sharding import PartitionSpec as P

ITERS = 4
CHUNKS = 2
GROUP = 4
LOG_MID = 0.5 * (math.log(0.02) + math.log(0.05))
LOG_HALF = 0.5 * (math.log(0.05) - math.log(0.02)) + 1.0
NU_SCALE = 124.0 / LOG_HALF
FLOW_SCALE = 31.0
LN2 = math.log(2.0)
VMEM = pl.BlockSpec(memory_space=pltpu.VMEM)
SMEM = pl.BlockSpec(memory_space=pltpu.SMEM)
F32 = jnp.float32
BF16 = jnp.bfloat16


def params(mib=48):
    return pltpu.CompilerParams(vmem_limit_bytes=mib * 1024 * 1024)


def power(x):
    return jnp.exp(x * LN2)


def log2_of(x):
    return jnp.log(x) * (1.0 / LN2)


def encode_kernel(base_slabs, prior_ref, flow_ref, visc_ref, sum_ref, right_ref, left_ref, total_ref, base):
    layers = prior_ref.shape[1]
    base[...] = jnp.log(visc_ref[...]) * NU_SCALE - LOG_MID * NU_SCALE
    if base_slabs:
        for l in range(layers):
            code = power(flow_ref[l] * FLOW_SCALE).astype(BF16)
            right_ref[l] = code
            left_ref[l] = code
    total_ref[...] = sum_ref[...] if sum_ref is not None else jnp.zeros_like(total_ref)

    def member(m, carry):
        for l in range(layers):
            field = prior_ref[m, l]
            total_ref[l] += field
            code = power(field * NU_SCALE + base[l]).astype(BF16)
            if l >= 1:
                right_ref[base_slabs + m * 3 + l - 1] = code
            if l < 3:
                left_ref[base_slabs + m * 3 + l] = code
        return carry

    lax.fori_loop(0, prior_ref.shape[0], member, 0)


def encode(prior, flow, visc, chunk, before):
    members, layers, nz, ny = prior.shape
    part = members // CHUNKS
    base_slabs = layers if chunk == 0 else 0
    slabs = base_slabs + 3 * part
    whole = lambda shape: pl.BlockSpec(shape, lambda i: (0,) * len(shape))
    args = [prior, flow, visc]
    specs = [
        pl.BlockSpec((part, layers, nz, ny), lambda i: (chunk, 0, 0, 0)),
        whole(flow.shape),
        whole(visc.shape),
    ]
    body = functools.partial(encode_kernel, base_slabs)
    if before is None:
        kernel = lambda p, f, v, *rest: body(p, f, v, None, *rest)
    else:
        kernel = body
        args.append(before)
        specs.append(whole(before.shape))
    return pl.pallas_call(
        kernel,
        grid=(1,),
        in_specs=specs,
        out_specs=[whole((slabs, nz, ny)), whole((slabs, nz, ny)), whole((layers, nz, ny))],
        out_shape=[
            jax.ShapeDtypeStruct((slabs, nz, ny), BF16),
            jax.ShapeDtypeStruct((slabs, nz, ny), BF16),
            jax.ShapeDtypeStruct((layers, nz, ny), F32),
        ],
        scratch_shapes=[pltpu.VMEM((layers, nz, ny), F32)],
        compiler_params=params(),
        name=f"encode{chunk}",
    )(*args)


def neighbours(buf, l, centre, nz, ny):
    lane = lax.broadcasted_iota(jnp.int32, centre.shape, 1)
    below = jnp.where(lane == 0, 0.0, pltpu.roll(centre, 1, 1))
    above = jnp.where(lane == ny - 1, 0.0, pltpu.roll(centre, ny - 1, 1))
    return (buf[l, 7 : 7 + nz] + buf[l, 9 : 9 + nz]) + (below + above)


def put(buf, l, value, nz):
    buf[l, 8 : 8 + nz] = value
    buf[l, 7:8] = value[nz - 1 : nz]
    buf[l, 8 + nz : 9 + nz] = value[0:1]


def sweep_kernel(
    chunk, base_slabs, devices, *refs
):
    cells_ref, prior_ref, flow_ref, visc_ref, behind_base, ahead_base, behind_ref, ahead_ref = refs[:8]
    rest = refs[8:]
    if chunk:
        rows_in, _, out_ref, rows_out, buf0, buf1, lap0, adv0, nu, rows = rest
    else:
        out_ref, rows_out, buf0, buf1, lap0, adv0, nu, rows = rest
    step = pl.program_id(0)
    group, layers, nz, ny = prior_ref.shape
    wide = layers + 2 * ITERS

    @pl.when(step == 0)
    def _():
        for l in range(ITERS):
            put(buf0, l, log2_of(behind_base[l].astype(F32)) * (1.0 / FLOW_SCALE), nz)
            put(buf0, ITERS + layers + l, log2_of(ahead_base[l].astype(F32)) * (1.0 / FLOW_SCALE), nz)
        for l in range(layers):
            put(buf0, ITERS + l, flow_ref[l], nz)
        for l in range(1, wide - 1):
            centre, back = buf0[l, 8 : 8 + nz], buf0[l - 1, 8 : 8 + nz]
            sides = back + buf0[l + 1, 8 : 8 + nz] + neighbours(buf0, l, centre, nz, ny)
            lap0[l - 1] = sides - 6.0 * centre
            adv0[l - 1] = centre - 0.15 * (centre - back) + 0.01

    def member(m, carry):
        first = base_slabs + (step * group + m) * 3
        for l in range(3):
            behind = behind_ref[first + l].astype(F32)
            nu[l] = jnp.exp(jnp.log(behind) * (1.0 / (LN2 * NU_SCALE)) + LOG_MID)
            ahead = ahead_ref[first + l].astype(F32)
            nu[3 + layers + l] = jnp.exp(jnp.log(ahead) * (1.0 / (LN2 * NU_SCALE)) + LOG_MID)
        for l in range(layers):
            nu[3 + l] = visc_ref[l] * jnp.exp(prior_ref[m, l])
        for l in range(1, wide - 1):
            put(buf1, l, adv0[l - 1] + nu[l - 1] * lap0[l - 1], nz)
        src, dst = buf1, buf0
        for sweep in range(1, ITERS):
            low, high = sweep + 1, wide - sweep - 1
            back, centre = src[low - 1, 8 : 8 + nz], src[low, 8 : 8 + nz]
            for l in range(low, high):
                front = src[l + 1, 8 : 8 + nz]
                lap = back + front + neighbours(src, l, centre, nz, ny) - 6.0 * centre
                value = centre + nu[l - 1] * lap - 0.15 * (centre - back) + 0.01
                if sweep == ITERS - 1:
                    out_ref[m, l - ITERS] = value
                else:
                    put(dst, l, value, nz)
                back, centre = centre, front
            src, dst = dst, src
        for s in range(4):
            cell = cells_ref[0, s]
            layer, z = cell // (nz * ny), lax.rem(cell, nz * ny) // ny
            rows[pl.ds(s * 16 + chunk * group * pl.num_programs(0) + step * group + m, 1), :] = out_ref[m, layer, pl.ds(z, 1), :]
        return carry

    if chunk:

        @pl.when(step == 0)
        def _():
            rows[...] = rows_in[...]

    lax.fori_loop(0, group, member, 0)

    @pl.when(step == pl.num_programs(0) - 1)
    def _():
        if chunk == 0:
            rows_out[...] = rows[...]
        else:
            lane = lax.broadcasted_iota(jnp.int32, (64, ny), 1)
            row = lax.broadcasted_iota(jnp.int32, (64, ny), 0)
            y = jnp.zeros((64, ny), jnp.int32)
            for s in range(4):
                y = jnp.where(row // 16 == s, lax.rem(cells_ref[0, s], ny), y)
            picked = jnp.sum(jnp.where(lane == y, rows[...], 0.0), axis=1, keepdims=True)
            line = jnp.sum(jnp.where(lane == row, picked, 0.0), axis=0, keepdims=True)
            rows_out[...] = jnp.broadcast_to(line, (devices, ny))


def sweeps(prior, flow, visc, cells, base, halo, chunk, before, devices):
    members, layers, nz, ny = prior.shape
    part = members // CHUNKS
    steps = part // GROUP
    base_slabs = layers if chunk == 0 else 0
    whole = lambda shape: pl.BlockSpec(shape, lambda i: (0,) * len(shape))
    block = pl.BlockSpec((GROUP, layers, nz, ny), lambda i: (chunk * steps + i, 0, 0, 0))
    args = [cells, prior, flow, visc, base[0], base[1], halo[0], halo[1]]
    specs = [SMEM, block, whole(flow.shape), whole(visc.shape)]
    specs += [whole((layers, nz, ny))] * 2 + [whole(halo[0].shape)] * 2
    alias = {}
    rows_shape = (64, ny) if chunk == 0 else (devices, ny)
    if chunk:
        args += [before[1], before[0]]
        specs += [whole((64, ny)), pl.BlockSpec(memory_space=pl.ANY)]
        alias = {len(args) - 1: 0}
    wide = layers + 2 * ITERS
    return pl.pallas_call(
        functools.partial(sweep_kernel, chunk, base_slabs, devices),
        grid=(steps,),
        in_specs=specs,
        out_specs=[block, whole(rows_shape)],
        out_shape=[
            jax.ShapeDtypeStruct(prior.shape, F32),
            jax.ShapeDtypeStruct(rows_shape, F32),
        ],
        input_output_aliases=alias,
        scratch_shapes=[
            pltpu.VMEM((wide, nz + 16, ny), F32),
            pltpu.VMEM((wide, nz + 16, ny), F32),
            pltpu.VMEM((wide - 2, nz, ny), F32),
            pltpu.VMEM((wide - 2, nz, ny), F32),
            pltpu.VMEM((wide - 2, nz, ny), F32),
            pltpu.VMEM((64, ny), F32),
        ],
        compiler_params=params(),
        name=f"sweeps{chunk}",
    )(*args)


def anomaly_kernel(members_all, prior_ref, a_ref, b_ref, c_ref, d_ref, out_ref):
    members, _, nz, ny = prior_ref.shape
    flat = prior_ref.reshape(members * nz, ny)
    mean = (a_ref[0] + b_ref[0] + c_ref[0] + d_ref[0]) / members_all
    for z in range(nz):
        rows = flat[pl.ds(z, members, stride=nz), :]
        out_ref[z] = (rows - mean[z : z + 1]).astype(BF16)


def anomalies(prior, totals, members_all):
    members, layers, nz, ny = prior.shape
    total = pl.BlockSpec((1, nz, ny), lambda l: (l, 0, 0))
    return pl.pallas_call(
        functools.partial(anomaly_kernel, members_all),
        grid=(layers,),
        in_specs=[pl.BlockSpec((members, 1, nz, ny), lambda l: (0, l, 0, 0))] + [total] * 4,
        out_specs=pl.BlockSpec((nz, members, ny), lambda l: (l, 0, 0)),
        out_shape=jax.ShapeDtypeStruct((layers * nz, members, ny), BF16),
        compiler_params=params(),
        name="anomalies",
    )(prior, *totals)


def slots_kernel(probes, slot_ref, value_ref, var_ref, noise_ref, seen_ref, weight_ref, stack):
    members, count = noise_ref.shape
    stack[...] = jnp.zeros_like(stack)
    stack[0:members] = noise_ref[...]
    stack[members : members + 1] = value_ref[...]
    stack[members + 1 : members + 2] = var_ref[...]
    slot = slot_ref[...]
    place = lax.rem(slot, probes) * (count // probes) + slot // probes
    row = lax.broadcasted_iota(jnp.int32, (count, count), 0)
    chosen = jnp.where(row == place, 1.0, 0.0)
    ordered = lax.dot_general(
        chosen, stack[...], (((1,), (1,)), ((), ())), precision=lax.Precision.HIGHEST, preferred_element_type=F32
    )
    value = ordered[:, members : members + 1]
    var = ordered[:, members + 1 : members + 2]
    seen_ref[...] = value + jnp.sqrt(var) * ordered
    weight_ref[...] = jnp.broadcast_to(1.0 / var, weight_ref.shape)


def in_slots(slot, value, var, noise, probes):
    count = slot.shape[0]
    shape = jax.ShapeDtypeStruct((count, 128), F32)
    return pl.pallas_call(
        functools.partial(slots_kernel, probes),
        in_specs=[VMEM] * 4,
        out_specs=[VMEM] * 2,
        out_shape=[shape, shape],
        scratch_shapes=[pltpu.VMEM((128, count), F32)],
        compiler_params=params(),
        name="slots",
    )(slot[None], value[None], var[None], noise)


def dot(a, b, dims):
    return lax.dot_general(a, b, (dims, ((), ())), precision=lax.Precision.HIGHEST, preferred_element_type=F32)


def solve_kernel(members, here, me_ref, vals_ref, seen_ref, weight_ref, out_ref, scr):
    devices, ny = vals_ref.shape
    groups = members // here
    tiles = devices // groups
    probes = 64 // here
    lane = lax.broadcasted_iota(jnp.int32, (tiles, ny), 1)
    parts = [vals_ref[pl.ds(g, tiles, stride=groups), :] for g in range(groups)]
    slabs = []
    for s in range(probes):
        slab = jnp.zeros((tiles, ny), F32)
        for g in range(groups):
            shift = (g - s) * here % ny
            moved = pltpu.roll(parts[g], shift, 1) if shift else parts[g]
            slab = jnp.where((lane >= g * here) & (lane < (g + 1) * here), moved, slab)
        slabs.append(slab)
    predicted = jnp.concatenate(slabs, axis=0)
    lanes = lax.broadcasted_iota(jnp.int32, predicted.shape, 1)
    mean = jnp.sum(predicted, axis=1, keepdims=True) / members
    spread = jnp.where(lanes < members, predicted - mean, 0.0)
    scaled = (spread * weight_ref[...]).T
    gram = dot(scaled, spread, ((1,), (0,)))
    rhs = dot(scaled, seen_ref[...] - predicted, ((1,), (0,)))
    half = 0.5 * jnp.max(jnp.sum(jnp.abs(gram), axis=1))
    alpha = 1.0 / (members - 1.0 + half)
    diagonal = lax.broadcasted_iota(jnp.int32, gram.shape, 0) == lax.broadcasted_iota(jnp.int32, gram.shape, 1)
    error = jnp.where(diagonal, alpha * half, 0.0) - alpha * gram

    def more(state):
        return (state[0] > 1e-9) & (state[1] < 40)

    def double(state):
        size, count, power_of, x = state
        both = dot(power_of, jnp.concatenate([power_of, x], axis=1), ((1,), (0,)))
        return size * size, count + 1, both[:, :ny], x + both[:, ny:]

    x = lax.while_loop(more, double, (half * alpha, 0, error, alpha * rhs))[3]
    me = me_ref[0]
    scr[...] = x
    order = [scr[pl.ds(pl.multiple_of((me ^ g) * here, here), here), :] for g in range(groups)]
    scr[...] = jnp.concatenate(order + [jnp.zeros((ny - members, ny), F32)], axis=0).T
    out_ref[...] = scr[pl.ds(pl.multiple_of(me * here, here), here), :].astype(BF16)[:, :members]


def solve(vals, seen, weight, me, members, here):
    return pl.pallas_call(
        functools.partial(solve_kernel, members, here),
        in_specs=[SMEM] + [VMEM] * 3,
        out_specs=VMEM,
        out_shape=jax.ShapeDtypeStruct((here, members), BF16),
        scratch_shapes=[pltpu.VMEM((128, 128), F32)],
        compiler_params=params(),
        name="solve",
    )(me, vals, seen, weight)


def update_kernel(weights_ref, prior_ref, *refs):
    blocks, out_ref = refs[:-1], refs[-1]
    members, _, nz, ny = prior_ref.shape
    flat = prior_ref.reshape(members * nz, ny)
    out = out_ref.reshape(members * nz, ny)
    weights = weights_ref[...]
    for z in range(0, nz, 2):
        pair = [jnp.concatenate([b[z + i] for b in blocks], axis=0) for i in range(2)]
        update = jnp.dot(weights, jnp.concatenate(pair, axis=1), preferred_element_type=F32)
        for i in range(2):
            where = pl.ds(z + i, members, stride=nz)
            out[where, :] = flat[where, :] + update[:, i * ny : (i + 1) * ny]


def updated(weights, prior, blocks):
    members, layers, nz, ny = prior.shape
    block = pl.BlockSpec((members, 1, nz, ny), lambda l: (0, l, 0, 0))
    part = pl.BlockSpec((nz, members, ny), lambda l: (l, 0, 0))
    return pl.pallas_call(
        update_kernel,
        grid=(layers,),
        in_specs=[pl.BlockSpec(weights.shape, lambda l: (0, 0)), block] + [part] * len(blocks),
        out_specs=block,
        out_shape=jax.ShapeDtypeStruct(prior.shape, F32),
        compiler_params=params(),
        name="update",
    )(weights, prior, *blocks)


def per_device(prior, base_flow, base_visc, probe_cells, obs_slot, obs_values, obs_var, obs_noise):
    here = prior.shape[0]
    tiles, groups = lax.axis_size("tile"), lax.axis_size("mem")
    members = here * groups
    me = lax.axis_index("mem").astype(jnp.int32).reshape(1)

    def along(x, step):
        return lax.ppermute(x, "tile", [(i, (i + step) % tiles) for i in range(tiles)])

    def across(x, bits):
        return lax.ppermute(x, "mem", [(i, i ^ bits) for i in range(groups)])

    halos, total = [], None
    for chunk in range(CHUNKS):
        right, left, total = encode(prior, base_flow, base_visc, chunk, total)
        halos.append((along(right, 1), along(left, -1)))
    totals = [total] + [across(total, bits) for bits in (1, 2, 3)]
    seen, weight = in_slots(obs_slot, obs_values, obs_var, obs_noise, probe_cells.shape[1])
    state = None
    for chunk in range(CHUNKS):
        state = sweeps(prior, base_flow, base_visc, probe_cells, halos[0], halos[chunk], chunk, state, tiles * groups)
    velocity, payload = state
    mine = anomalies(prior, totals, float(members))
    beside = across(mine, 1)
    over = across(mine, 2)
    blocks = [mine, beside, over, across(over, 1)]
    vals = lax.all_to_all(payload, ("tile", "mem"), 0, 0, tiled=True)
    weights = solve(vals, seen, weight, me, members, here)
    return velocity, updated(weights, prior, blocks)


def solution(mesh):
    placed = (
        P("mem", "tile", None, None),
        P("tile", None, None),
        P("tile", None, None),
        P("tile", None),
        P(),
        P(),
        P(),
        P(),
    )
    return jax.shard_map(
        per_device,
        mesh=mesh,
        in_specs=placed,
        out_specs=(P("mem", "tile", None, None), P("mem", "tile", None, None)),
        check_vma=False,
    )
```

time: 354 us -> 93 us (0.26)
  the two profiles are of different devices: /device:TPU:2 before, /device:TPU:1 now
where the time goes in v1:
time: 93 us; the launch traced here: 92.8 us
  waiting for transfers between devices  43.7 us (47%)
  starting transfers between devices  26.6 us (29%)
  Pallas kernels  17.6 us (19%)
  local copies, waits for them, and re-layouts  4.06 us (4%)
    ppermute x6, waiting for transfers between devices, across(): return lax.ppermute(x, 'mem', [(i, i ^ bits) for i in range(groups)])  29.3 us
    all_to_all x1, waiting for transfers between devices, per_device(): vals = lax.all_to_all(payload, ('tile', 'mem'), 0, 0, tiled=True)  11.4 us
    all_to_all x1, starting transfers between devices, per_device(): vals = lax.all_to_all(payload, ('tile', 'mem'), 0, 0, tiled=True)  10 us
    ppermute x4, starting transfers between devices, along(): lax.ppermute(x, 'tile', [(i, (i + step) % tiles) for i in range(tiles)])  9.67 us
    pallas_call x2, Pallas kernels, sweeps(): pl.pallas_call(functools.partial(sweep_kernel, chunk, base_slabs, devices...  9.13 us
    ppermute x6, starting transfers between devices, across(): return lax.ppermute(x, 'mem', [(i, i ^ bits) for i in range(groups)])  6.94 us
    pallas_call x1, Pallas kernels, updated(): pl.pallas_call(update_kernel, grid=(layers,), in_specs=[pl.BlockSpec(weig...  4.29 us
    unnamed x22, local copies, waits for them, and re-layouts  4.06 us
  transfers between devices with their start and end apart: 11, of which 7 were waited for; matrix products, arithmetic and copies ran while one was open for 0% of the time, Pallas kernels for 13%

profile of v1, /device:TPU:1, one launch (start us, length us, event | category | flops | bytes accessed | tf_op | source)
XLA Modules:
  0.0 92.8 jit_solution(17757414688814765271)
XLA Ops:
  0.6 1.4 %copy-done = f32[16,4,48,128]{3,2,1,0:T(8,128)S(1)} copy-done((f32[16,4,48,128]{3,2,1,0:T(8,128)S(1)}, f32[16,4,48,128]{3,2,1,0:T(8,128)}, u32[]{:S(2)}) %copy-start) | copy-done | bytes 1572888
  2.0 0.9 copy-done.2
  2.9 0.9 copy-done.4
  4.5 3.3 %collective-permute-start.4 = (f32[4,48,128]{2,1,0:T(8,128)S(1)}, f32[4,48,128]{2,1,0:T(8,128)S(1)}, u32[]{:S(2)}, u32[]{:S(2)}) collective-permute-start(f32[4,48,128]{2,1,0:T(8,128)S(1)} %get-tuple-element.25.a_ref), channel_id=1, source_target_pairs={{0,1},{1,0},{2,3},{3,2},{4,5},{5,4},{6,7},{7,6},{8,9},{9,8},{10,11... | collective-permute-start | bytes 294920 | tf_op jit(solution)/shard_map/ppermute | solution.py:383
  7.8 1.7 %collective-permute-start.6 = (f32[4,48,128]{2,1,0:T(8,128)S(1)}, f32[4,48,128]{2,1,0:T(8,128)S(1)}, u32[]{:S(2)}, u32[]{:S(2)}) collective-permute-start(f32[4,48,128]{2,1,0:T(8,128)S(1)} %get-tuple-element.25.a_ref), channel_id=1, source_target_pairs={{0,3},{1,2},{2,1},{3,0},{4,7},{5,6},{6,5},{7,4},{8,11},{9,10},{10,... | collective-permute-start | bytes 294920 | tf_op jit(solution)/shard_map/ppermute | solution.py:383
  9.5 2.6 %collective-permute-done.5.c_ref = f32[4,48,128]{2,1,0:T(8,128)S(1)} collective-permute-done((f32[4,48,128]{2,1,0:T(8,128)S(1)}, f32[4,48,128]{2,1,0:T(8,128)S(1)}, u32[]{:S(2)}, u32[]{:S(2)}) %collective-permute-start.5) | collective-permute-done | bytes 98336 | tf_op jit(solution)/shard_map/ppermute | solution.py:383
  12.2 2.3 %collective-permute-done.6.d_ref = f32[4,48,128]{2,1,0:T(8,128)S(1)} collective-permute-done((f32[4,48,128]{2,1,0:T(8,128)S(1)}, f32[4,48,128]{2,1,0:T(8,128)S(1)}, u32[]{:S(2)}, u32[]{:S(2)}) %collective-permute-start.6) | collective-permute-done | bytes 98336 | tf_op jit(solution)/shard_map/ppermute | solution.py:383
  14.4 0.7 anomalies.1.refs_0_
  15.2 1.1 %collective-permute-start = (bf16[28,48,128]{2,1,0:T(8,128)(2,1)S(1)}, bf16[28,48,128]{2,1,0:T(8,128)(2,1)S(1)}, u32[]{:S(2)}, u32[]{:S(2)}) collective-permute-start(bf16[28,48,128]{2,1,0:T(8,128)(2,1)S(1)} %get-tuple-element.14), channel_id=1, source_target_pairs={{0,4},{4,8},{8,12},{12,16},{16,20},{20,24},{24,28},{28,32},{32,36}... | collective-permute-start | bytes 1032200 | tf_op jit(solution)/shard_map/ppermute | solution.py:380
  16.3 0.8 collective-permute-start.7
  17.1 24.4 %collective-permute-done.8.refs_2_ = bf16[192,16,128]{2,1,0:T(8,128)(2,1)S(1)} collective-permute-done((bf16[192,16,128]{2,1,0:T(8,128)(2,1)S(1)}, bf16[192,16,128]{2,1,0:T(8,128)(2,1)S(1)}, u32[]{:S(2)}, u32[]{:S(2)}) %collective-permute-start.8) | collective-permute-done | bytes 786464 | tf_op jit(solution)/shard_map/ppermute | solution.py:383
  41.5 1.0 %collective-permute-start.9 = (bf16[192,16,128]{2,1,0:T(8,128)(2,1)S(1)}, bf16[192,16,128]{2,1,0:T(8,128)(2,1)}, u32[]{:S(2)}, u32[]{:S(2)}) collective-permute-start(bf16[192,16,128]{2,1,0:T(8,128)(2,1)S(1)} %collective-permute-done.8.refs_2_), channel_id=1, source_target_pairs={{0,1},{1,0},{2,3},{3,2},{4,5},{5,4},{6,7},{7,6},{8,9},{9,8},{10,11... | collective-permute-start | bytes 2359304 | tf_op jit(solution)/shard_map/ppermute | solution.py:383
  42.6 1.4 %collective-permute-start.1 = (bf16[28,48,128]{2,1,0:T(8,128)(2,1)S(1)}, bf16[28,48,128]{2,1,0:T(8,128)(2,1)S(1)}, u32[]{:S(2)}, u32[]{:S(2)}) collective-permute-start(bf16[28,48,128]{2,1,0:T(8,128)(2,1)S(1)} %get-tuple-element.15), channel_id=1, source_target_pairs={{0,252},{4,0},{8,4},{12,8},{16,12},{20,16},{24,20},{28,24},{32,28}... | collective-permute-start | bytes 1032200 | tf_op jit(solution)/shard_map/ppermute | solution.py:380
  44.0 7.1 %collective-permute-start.3 = (bf16[24,48,128]{2,1,0:T(8,128)(2,1)S(1)}, bf16[24,48,128]{2,1,0:T(8,128)(2,1)S(1)}, u32[]{:S(2)}, u32[]{:S(2)}) collective-permute-start(bf16[24,48,128]{2,1,0:T(8,128)(2,1)S(1)} %get-tuple-element.18), channel_id=1, source_target_pairs={{0,252},{4,0},{8,4},{12,8},{16,12},{20,16},{24,20},{28,24},{32,28}... | collective-permute-start | bytes 884744 | tf_op jit(solution)/shard_map/ppermute | solution.py:380
  51.1 1.1 %collective-permute-done.1.refs_5_.refs_7_ = bf16[28,48,128]{2,1,0:T(8,128)(2,1)S(1)} collective-permute-done((bf16[28,48,128]{2,1,0:T(8,128)(2,1)S(1)}, bf16[28,48,128]{2,1,0:T(8,128)(2,1)S(1)}, u32[]{:S(2)}, u32[]{:S(2)}) %collective-permute-start.1) | collective-permute-done | bytes 344096 | tf_op jit(solution)/shard_map/ppermute | solution.py:380
  52.3 4.5 %sweeps0.1 = (f32[16,4,48,128]{3,2,1,0:T(8,128)}, f32[64,128]{1,0:T(8,128)S(1)}) custom-call(s32[1,4]{1,0:T(1,128)S(1)} %copy-done.7, f32[16,4,48,128]{3,2,1,0:T(8,128)S(1)} %copy-done, f32[4,48,128]{2,1,0:T(8,128)S(1)} %copy-done.3, f32[4,48,128]{2,1,0:T(8,128)S(1)} %copy-done.5, bf16[28,48,128]{2,1,0:T(8,128)(2,1)S(1)} %collective-permute-done.refs_4_.refs_6_, ...), custom_call_target="tpu_custom_call" | custom-call | tf_op jit(solution)/shard_map/sweeps0/pallas_call | solution.py:206
  56.7 1.2 %collective-permute-done.2.refs_6_ = bf16[24,48,128]{2,1,0:T(8,128)(2,1)S(1)} collective-permute-done((bf16[24,48,128]{2,1,0:T(8,128)(2,1)S(1)}, bf16[24,48,128]{2,1,0:T(8,128)(2,1)S(1)}, u32[]{:S(2)}, u32[]{:S(2)}) %collective-permute-start.2) | collective-permute-done | bytes 294944 | tf_op jit(solution)/shard_map/ppermute | solution.py:380
  58.0 0.6 collective-permute-done.3.refs_7_
  58.6 4.6 %sweeps1.1 = (f32[16,4,48,128]{3,2,1,0:T(8,128)}, f32[256,128]{1,0:T(8,128)}) custom-call(s32[1,4]{1,0:T(1,128)S(1)} %copy-done.7, f32[16,4,48,128]{3,2,1,0:T(8,128)S(1)} %copy-done, f32[4,48,128]{2,1,0:T(8,128)S(1)} %copy-done.3, f32[4,48,128]{2,1,0:T(8,128)S(1)} %copy-done.5, ...), custom_call_target="tpu_custom_call", output_to_operand_aliasing={{0}: (9, {})} | custom-call | tf_op jit(solution)/shard_map/sweeps1/pallas_call | solution.py:206
  63.2 10.0 %all-to-all-start = ((f32[256,1,128]{2,1,0:T(1,128)}), f32[256,1,128]{2,1,0:T(1,128)S(1)}, u32[]{:S(2)}, u32[]{:S(2)}) async-start(f32[256,1,128]{2,1,0:T(1,128)} %bitcast.2), calls=%async_computation | async-start | bytes 262144 | tf_op jit(solution)/shard_map/all_to_all | solution.py:399
  73.3 0.8 copy-done.6
  74.6 11.4 %all-to-all-done = f32[256,1,128]{2,1,0:T(1,128)S(1)} async-done(((f32[256,1,128]{2,1,0:T(1,128)}), f32[256,1,128]{2,1,0:T(1,128)S(1)}, u32[]{:S(2)}, u32[]{:S(2)}) %all-to-all-start) | async-done | bytes 131104 | tf_op jit(solution)/shard_map/all_to_all | solution.py:399
  86.1 2.4 %solve.1.weights_ref = bf16[16,64]{1,0:T(8,128)(2,1)S(1)} custom-call(s32[1]{0:T(128)} %bitcast.me_ref, f32[256,128]{1,0:T(8,128)S(1)} %bitcast.8, f32[256,128]{1,0:T(8,128)S(1)} %get-tuple-element.23.seen_ref, f32[256,128]{1,0:T(8,128)S(1)} %get-tuple-element.24.weight_ref), custom_call_target="tpu_custom_call" | custom-call | tf_op jit(solution)/shard_map/solve/pallas_call | solution.py:333
  88.5 4.3 %update.1 = f32[16,4,48,128]{3,2,1,0:T(8,128)} custom-call(bf16[16,64]{1,0:T(8,128)(2,1)S(1)} %solve.1.weights_ref, f32[16,4,48,128]{3,2,1,0:T(8,128)S(1)} %copy-done.1, bf16[192,16,128]{2,1,0:T(8,128)(2,1)S(1)} %anomalies.1.refs_0_, bf16[192,16,128]{2,1,0:T(8,128)(2,1)} %collective-permute-done.7.refs_1_, ...), custom_call_target="tpu_custom_call" | custom-call | tf_op jit(solution)/shard_map/update/pallas_call | solution.py:362
  (28 shorter events, 1.3 us)
Async XLA Ops:
  0.6 1.4 %copy-start = (f32[16,4,48,128]{3,2,1,0:T(8,128)S(1)}, f32[16,4,48,128]{3,2,1,0:T(8,128)}, u32[]{:S(2)}) copy-start(f32[16,4,48,128]{3,2,1,0:T(8,128)} %prior_ref.5) | copy-start | bytes 4718596
  2.0 0.9 copy-start.2
  2.9 0.9 copy-start.4
  4.4 47.8 %copy-start.3 = (f32[4,48,128]{2,1,0:T(8,128)S(1)}, f32[4,48,128]{2,1,0:T(8,128)}, u32[]{:S(2)}) copy-start(f32[4,48,128]{2,1,0:T(8,128)} %refs_2_.3) | copy-start | bytes 294916
  4.4 47.8 %copy-start.5 = (f32[4,48,128]{2,1,0:T(8,128)S(1)}, f32[4,48,128]{2,1,0:T(8,128)}, u32[]{:S(2)}) copy-start(f32[4,48,128]{2,1,0:T(8,128)} %refs_3_.3) | copy-start | bytes 294916
  4.5 47.8 %copy-start.7 = (s32[1,4]{1,0:T(1,128)S(1)}, s32[1,4]{1,0:T(1,128)}, u32[]{:S(2)}) copy-start(s32[1,4]{1,0:T(1,128)} %refs_0_.3) | copy-start | bytes 52
  4.5 5.1 %collective-permute-start.4 = (f32[4,48,128]{2,1,0:T(8,128)S(1)}, f32[4,48,128]{2,1,0:T(8,128)S(1)}, u32[]{:S(2)}, u32[]{:S(2)}) collective-permute-start(f32[4,48,128]{2,1,0:T(8,128)S(1)} %get-tuple-element.25.a_ref), channel_id=1, source_target_pairs={{0,1},{1,0},{2,3},{3,2},{4,5},{5,4},{6,7},{7,6},{8,9},{9,8},{10,11... | collective-permute-start | bytes 294920 | tf_op jit(solution)/shard_map/ppermute | solution.py:383
  7.8 4.4 %collective-permute-start.5 = (f32[4,48,128]{2,1,0:T(8,128)S(1)}, f32[4,48,128]{2,1,0:T(8,128)S(1)}, u32[]{:S(2)}, u32[]{:S(2)}) collective-permute-start(f32[4,48,128]{2,1,0:T(8,128)S(1)} %get-tuple-element.25.a_ref), channel_id=1, source_target_pairs={{0,2},{1,3},{2,0},{3,1},{4,6},{5,7},{6,4},{7,5},{8,10},{9,11},{10,... | collective-permute-start | bytes 294920 | tf_op jit(solution)/shard_map/ppermute | solution.py:383
  7.8 6.6 %collective-permute-start.6 = (f32[4,48,128]{2,1,0:T(8,128)S(1)}, f32[4,48,128]{2,1,0:T(8,128)S(1)}, u32[]{:S(2)}, u32[]{:S(2)}) collective-permute-start(f32[4,48,128]{2,1,0:T(8,128)S(1)} %get-tuple-element.25.a_ref), channel_id=1, source_target_pairs={{0,3},{1,2},{2,1},{3,0},{4,7},{5,6},{6,5},{7,4},{8,11},{9,10},{10,... | collective-permute-start | bytes 294920 | tf_op jit(solution)/shard_map/ppermute | solution.py:383
  15.1 26.4 %collective-permute-start.8 = (bf16[192,16,128]{2,1,0:T(8,128)(2,1)S(1)}, bf16[192,16,128]{2,1,0:T(8,128)(2,1)S(1)}, u32[]{:S(2)}, u32[]{:S(2)}) collective-permute-start(bf16[192,16,128]{2,1,0:T(8,128)(2,1)S(1)} %anomalies.1.refs_0_), channel_id=1, source_target_pairs={{0,2},{1,3},{2,0},{3,1},{4,6},{5,7},{6,4},{7,5},{8,10},{9,11},{10,... | collective-permute-start | bytes 2359304 | tf_op jit(solution)/shard_map/ppermute | solution.py:383
  15.2 28.8 %collective-permute-start = (bf16[28,48,128]{2,1,0:T(8,128)(2,1)S(1)}, bf16[28,48,128]{2,1,0:T(8,128)(2,1)S(1)}, u32[]{:S(2)}, u32[]{:S(2)}) collective-permute-start(bf16[28,48,128]{2,1,0:T(8,128)(2,1)S(1)} %get-tuple-element.14), channel_id=1, source_target_pairs={{0,4},{4,8},{8,12},{12,16},{16,20},{20,24},{24,28},{28,32},{32,36}... | collective-permute-start | bytes 1032200 | tf_op jit(solution)/shard_map/ppermute | solution.py:380
  16.3 72.2 %collective-permute-start.7 = (bf16[192,16,128]{2,1,0:T(8,128)(2,1)S(1)}, bf16[192,16,128]{2,1,0:T(8,128)(2,1)}, u32[]{:S(2)}, u32[]{:S(2)}) collective-permute-start(bf16[192,16,128]{2,1,0:T(8,128)(2,1)S(1)} %anomalies.1.refs_0_), channel_id=1, source_target_pairs={{0,1},{1,0},{2,3},{3,2},{4,5},{5,4},{6,7},{7,6},{8,9},{9,8},{10,11... | collective-permute-start | bytes 2359304 | tf_op jit(solution)/shard_map/ppermute | solution.py:383
  41.5 47.0 %collective-permute-start.9 = (bf16[192,16,128]{2,1,0:T(8,128)(2,1)S(1)}, bf16[192,16,128]{2,1,0:T(8,128)(2,1)}, u32[]{:S(2)}, u32[]{:S(2)}) collective-permute-start(bf16[192,16,128]{2,1,0:T(8,128)(2,1)S(1)} %collective-permute-done.8.refs_2_), channel_id=1, source_target_pairs={{0,1},{1,0},{2,3},{3,2},{4,5},{5,4},{6,7},{7,6},{8,9},{9,8},{10,11... | collective-permute-start | bytes 2359304 | tf_op jit(solution)/shard_map/ppermute | solution.py:383
  42.6 9.7 %collective-permute-start.1 = (bf16[28,48,128]{2,1,0:T(8,128)(2,1)S(1)}, bf16[28,48,128]{2,1,0:T(8,128)(2,1)S(1)}, u32[]{:S(2)}, u32[]{:S(2)}) collective-permute-start(bf16[28,48,128]{2,1,0:T(8,128)(2,1)S(1)} %get-tuple-element.15), channel_id=1, source_target_pairs={{0,252},{4,0},{8,4},{12,8},{16,12},{20,16},{24,20},{28,24},{32,28}... | collective-permute-start | bytes 1032200 | tf_op jit(solution)/shard_map/ppermute | solution.py:380
  43.9 14.0 %collective-permute-start.2 = (bf16[24,48,128]{2,1,0:T(8,128)(2,1)S(1)}, bf16[24,48,128]{2,1,0:T(8,128)(2,1)S(1)}, u32[]{:S(2)}, u32[]{:S(2)}) collective-permute-start(bf16[24,48,128]{2,1,0:T(8,128)(2,1)S(1)} %get-tuple-element.17), channel_id=1, source_target_pairs={{0,4},{4,8},{8,12},{12,16},{16,20},{20,24},{24,28},{28,32},{32,36}... | collective-permute-start | bytes 884744 | tf_op jit(solution)/shard_map/ppermute | solution.py:380
  44.0 14.5 %collective-permute-start.3 = (bf16[24,48,128]{2,1,0:T(8,128)(2,1)S(1)}, bf16[24,48,128]{2,1,0:T(8,128)(2,1)S(1)}, u32[]{:S(2)}, u32[]{:S(2)}) collective-permute-start(bf16[24,48,128]{2,1,0:T(8,128)(2,1)S(1)} %get-tuple-element.18), channel_id=1, source_target_pairs={{0,252},{4,0},{8,4},{12,8},{16,12},{20,16},{24,20},{28,24},{32,28}... | collective-permute-start | bytes 884744 | tf_op jit(solution)/shard_map/ppermute | solution.py:380
  58.6 14.7 %copy-start.8 = (s32[256]{0:T(256)S(1)}, s32[256]{0:T(256)}, u32[]{:S(2)}) copy-start(s32[256]{0:T(256)} %param.12) | copy-start | bytes 3076
  58.6 14.7 %copy-start.9 = (f32[256]{0:T(256)S(1)}, f32[256]{0:T(256)}, u32[]{:S(2)}) copy-start(f32[256]{0:T(256)} %param.13) | copy-start | bytes 3076
  58.6 14.7 %copy-start.10 = (f32[256]{0:T(256)S(1)}, f32[256]{0:T(256)}, u32[]{:S(2)}) copy-start(f32[256]{0:T(256)} %param.14) | copy-start | bytes 3076
  58.6 30.0 %copy-start.1 = (f32[16,4,48,128]{3,2,1,0:T(8,128)S(1)}, f32[16,4,48,128]{3,2,1,0:T(8,128)}, u32[]{:S(2)}) copy-start(f32[16,4,48,128]{3,2,1,0:T(8,128)} %prior_ref.5) | copy-start | bytes 4718596
  63.2 22.8 %all-to-all-start = ((f32[256,1,128]{2,1,0:T(1,128)}), f32[256,1,128]{2,1,0:T(1,128)S(1)}, u32[]{:S(2)}, u32[]{:S(2)}) async-start(f32[256,1,128]{2,1,0:T(1,128)} %bitcast.2), calls=%async_computation | async-start | bytes 262144 | tf_op jit(solution)/shard_map/all_to_all | solution.py:399
  73.3 0.8 copy-start.6

commit v2 on v1

v2 whole, which is shorter than its diff:
```python
import functools
import math

import jax
import jax.numpy as jnp
from jax import lax
from jax.experimental import pallas as pl
from jax.experimental.pallas import tpu as pltpu
from jax.sharding import PartitionSpec as P

ITERS = 4
PARTS = ((8, 0), (4, 2), (4, 3))
CHUNKS = len(PARTS)
AT_ONCE = 4
TOTAL_AFTER, ANOMALY_AFTER = 0, 2
LOG_MID = 0.5 * (math.log(0.02) + math.log(0.05))
LOG_HALF = 0.5 * (math.log(0.05) - math.log(0.02)) + 1.0
NU_SCALE = 124.0 / LOG_HALF
FLOW_SCALE = 31.0
LN2 = math.log(2.0)
VMEM = pl.BlockSpec(memory_space=pltpu.VMEM)
SMEM = pl.BlockSpec(memory_space=pltpu.SMEM)
F32 = jnp.float32
BF16 = jnp.bfloat16


def params(mib=48):
    return pltpu.CompilerParams(vmem_limit_bytes=mib * 1024 * 1024)


def power(x):
    return jnp.exp(x * LN2)


def log2_of(x):
    return jnp.log(x) * (1.0 / LN2)


def encode_kernel(prior_hbm, flow_hbm, visc_hbm, *refs):
    outs, (prior, flow, visc, base, sems) = refs[: 2 * CHUNKS], refs[2 * CHUNKS :]
    layers = prior.shape[1]
    copies = [
        pltpu.make_async_copy(visc_hbm, visc, sems.at[0]),
        pltpu.make_async_copy(flow_hbm, flow, sems.at[1]),
    ]
    for c, (part, place) in enumerate(PARTS):
        span = pl.ds(place * part, part)
        copies.append(pltpu.make_async_copy(prior_hbm.at[span], prior.at[span], sems.at[2 + c]))
    for copy in copies:
        copy.start()
    copies[0].wait()
    base[...] = jnp.log(visc[...]) * NU_SCALE - LOG_MID * NU_SCALE
    copies[1].wait()
    for l in range(layers):
        code = power(flow[l] * FLOW_SCALE).astype(BF16)
        outs[0][l] = code
        outs[1][l] = code
    for c, (part, place) in enumerate(PARTS):
        copies[2 + c].wait()
        right_ref, left_ref = outs[2 * c], outs[2 * c + 1]
        first = layers if c == 0 else 0

        def member(m, carry):
            for l in range(layers):
                code = power(prior[place * part + m, l] * NU_SCALE + base[l]).astype(BF16)
                if l >= 1:
                    right_ref[first + m * 3 + l - 1] = code
                if l < 3:
                    left_ref[first + m * 3 + l] = code
            return carry

        lax.fori_loop(0, part, member, 0)


def encode(prior, flow, visc):
    members, layers, nz, ny = prior.shape
    shapes = []
    for c, (part, _) in enumerate(PARTS):
        slabs = 3 * part + (layers if c == 0 else 0)
        shapes += [jax.ShapeDtypeStruct((slabs, nz, ny), BF16)] * 2
    return pl.pallas_call(
        encode_kernel,
        in_specs=[pl.BlockSpec(memory_space=pltpu.HBM)] * 3,
        out_specs=[VMEM] * len(shapes),
        out_shape=shapes,
        scratch_shapes=[
            pltpu.VMEM(prior.shape, F32),
            pltpu.VMEM(flow.shape, F32),
            pltpu.VMEM(visc.shape, F32),
            pltpu.VMEM(visc.shape, F32),
            pltpu.SemaphoreType.DMA((2 + CHUNKS,)),
        ],
        compiler_params=params(),
        name="encode",
    )(*[pltpu.with_memory_space_constraint(x, pltpu.HBM) for x in (prior, flow, visc)])


def total_kernel(prior_ref, after, out_ref):
    out_ref[...] = prior_ref[0]
    for m in range(1, prior_ref.shape[0]):
        out_ref[...] += prior_ref[m]


def total_of(prior, after):
    return pl.pallas_call(
        total_kernel,
        in_specs=[VMEM, pl.BlockSpec(memory_space=pl.ANY)],
        out_specs=VMEM,
        out_shape=jax.ShapeDtypeStruct(prior.shape[1:], F32),
        compiler_params=params(),
        name="total",
    )(prior, after)


def hold_kernel(*refs):
    pass


def held(value, *after):
    anywhere = pl.BlockSpec(memory_space=pl.ANY)
    return pl.pallas_call(
        hold_kernel,
        in_specs=[anywhere] * (1 + len(after)),
        out_specs=anywhere,
        out_shape=jax.ShapeDtypeStruct(value.shape, value.dtype),
        input_output_aliases={0: 0},
        name="hold",
    )(value, *after)


def neighbours(buf, l, centre, nz, ny):
    lane = lax.broadcasted_iota(jnp.int32, centre.shape, 1)
    below = jnp.where(lane == 0, 0.0, pltpu.roll(centre, 1, 1))
    above = jnp.where(lane == ny - 1, 0.0, pltpu.roll(centre, ny - 1, 1))
    return (buf[l, 7 : 7 + nz] + buf[l, 9 : 9 + nz]) + (below + above)


def put(buf, l, value, nz):
    buf[l, 8 : 8 + nz] = value
    buf[l, 7:8] = value[nz - 1 : nz]
    buf[l, 8 + nz : 9 + nz] = value[0:1]


def sweep_kernel(chunk, devices, cells_ref, prior_ref, flow_ref, visc_ref, behind_ref, ahead_ref, *rest):
    part, layers, nz, ny = prior_ref.shape
    wide = layers + 2 * ITERS
    last = chunk == CHUNKS - 1
    if chunk == 0:
        out_ref, rows, lap0, adv0, buf0, buf1, nu = rest
        for l in range(ITERS):
            put(buf0, l, log2_of(behind_ref[l].astype(F32)) * (1.0 / FLOW_SCALE), nz)
            put(buf0, ITERS + layers + l, log2_of(ahead_ref[l].astype(F32)) * (1.0 / FLOW_SCALE), nz)
        for l in range(layers):
            put(buf0, ITERS + l, flow_ref[l], nz)
        for l in range(1, wide - 1):
            centre, back = buf0[l, 8 : 8 + nz], buf0[l - 1, 8 : 8 + nz]
            sides = back + buf0[l + 1, 8 : 8 + nz] + neighbours(buf0, l, centre, nz, ny)
            lap0[l - 1] = sides - 6.0 * centre
            adv0[l - 1] = centre - 0.15 * (centre - back) + 0.01
        rows[...] = jnp.zeros_like(rows)
    elif not last:
        lap0, adv0, rows_in, _, out_ref, rows, buf0, buf1, nu = rest
        rows[...] = rows_in[...]
    else:
        lap0, adv0, rows_in, _, out_ref, lines_ref, buf0, buf1, nu, rows = rest
        rows[...] = rows_in[...]
    base_slabs = layers if chunk == 0 else 0

    def member(m, carry):
        first = base_slabs + m * 3
        for l in range(3):
            behind = behind_ref[first + l].astype(F32)
            nu[l] = jnp.exp(jnp.log(behind) * (1.0 / (LN2 * NU_SCALE)) + LOG_MID)
            ahead = ahead_ref[first + l].astype(F32)
            nu[3 + layers + l] = jnp.exp(jnp.log(ahead) * (1.0 / (LN2 * NU_SCALE)) + LOG_MID)
        for l in range(layers):
            nu[3 + l] = visc_ref[l] * jnp.exp(prior_ref[m, l])
        for l in range(1, wide - 1):
            put(buf1, l, adv0[l - 1] + nu[l - 1] * lap0[l - 1], nz)
        src, dst = buf1, buf0
        for sweep in range(1, ITERS):
            low, high = sweep + 1, wide - sweep - 1
            back, centre = src[low - 1, 8 : 8 + nz], src[low, 8 : 8 + nz]
            for l in range(low, high):
                front = src[l + 1, 8 : 8 + nz]
                lap = back + front + neighbours(src, l, centre, nz, ny) - 6.0 * centre
                value = centre + nu[l - 1] * lap - 0.15 * (centre - back) + 0.01
                if sweep == ITERS - 1:
                    out_ref[m, l - ITERS] = value
                else:
                    put(dst, l, value, nz)
                back, centre = centre, front
            src, dst = dst, src
        for s in range(4):
            cell = cells_ref[0, s]
            layer, z = cell // (nz * ny), lax.rem(cell, nz * ny) // ny
            rows[pl.ds(s * 16 + PARTS[chunk][1] * part + m, 1), :] = out_ref[m, layer, pl.ds(z, 1), :]
        return carry

    lax.fori_loop(0, part, member, 0)
    if last:
        lane = lax.broadcasted_iota(jnp.int32, rows.shape, 1)
        row = lax.broadcasted_iota(jnp.int32, rows.shape, 0)
        y = jnp.zeros(rows.shape, jnp.int32)
        for s in range(4):
            y = jnp.where(row // 16 == s, lax.rem(cells_ref[0, s], ny), y)
        picked = jnp.sum(jnp.where(lane == y, rows[...], 0.0), axis=1, keepdims=True)
        line = jnp.sum(jnp.where(lane == row, picked, 0.0), axis=0, keepdims=True)
        lines_ref[...] = jnp.broadcast_to(line, (devices, ny))


def sweeps(prior, flow, visc, cells, halo, chunk, before, devices):
    members, layers, nz, ny = prior.shape
    part, place = PARTS[chunk]
    whole = lambda shape: pl.BlockSpec(shape, lambda i: (0,) * len(shape))
    block = pl.BlockSpec((part, layers, nz, ny), lambda i: (place, 0, 0, 0))
    wide = layers + 2 * ITERS
    base_shape = (wide - 2, nz, ny)
    args = [cells, prior, flow, visc, *halo]
    specs = [SMEM, block, whole(flow.shape), whole(visc.shape), whole(halo[0].shape), whole(halo[1].shape)]
    alias = {}
    scratch = [
        pltpu.VMEM((wide, nz + 16, ny), F32),
        pltpu.VMEM((wide, nz + 16, ny), F32),
        pltpu.VMEM(base_shape, F32),
    ]
    if chunk:
        velocity, rows, lap0, adv0 = before
        args += [lap0, adv0, rows, velocity]
        specs += [whole(base_shape)] * 2 + [whole((64, ny)), pl.BlockSpec(memory_space=pl.ANY)]
        alias = {len(args) - 1: 0}
    last = chunk == CHUNKS - 1
    more = [(devices, ny)] if last else [(64, ny)]
    if chunk == 0:
        more += [base_shape] * 2
    if last:
        scratch.append(pltpu.VMEM((64, ny), F32))
    out = pl.pallas_call(
        functools.partial(sweep_kernel, chunk, devices),
        grid=(1,),
        in_specs=specs,
        out_specs=[block] + [whole(shape) for shape in more],
        out_shape=[jax.ShapeDtypeStruct(shape, F32) for shape in [prior.shape] + more],
        input_output_aliases=alias,
        scratch_shapes=scratch,
        compiler_params=params(),
        name=f"sweeps{chunk}",
    )(*args)
    return tuple(out) + (tuple(before[2:]) if chunk else ())


def anomaly_kernel(members_all, prior_ref, a_ref, b_ref, c_ref, d_ref, after, out_ref):
    members, _, nz, ny = prior_ref.shape
    flat = prior_ref.reshape(members * nz, ny)
    mean = (a_ref[0] + b_ref[0] + c_ref[0] + d_ref[0]) / members_all
    for z in range(nz):
        rows = flat[pl.ds(z, members, stride=nz), :]
        out_ref[z] = (rows - mean[z : z + 1]).astype(BF16)


def anomalies(prior, totals, members_all, after):
    members, layers, nz, ny = prior.shape
    total = pl.BlockSpec((1, nz, ny), lambda l: (l, 0, 0))
    return pl.pallas_call(
        functools.partial(anomaly_kernel, members_all),
        grid=(layers,),
        in_specs=[pl.BlockSpec((members, 1, nz, ny), lambda l: (0, l, 0, 0))] + [total] * 4 + [pl.BlockSpec(memory_space=pl.ANY)],
        out_specs=pl.BlockSpec((nz, members, ny), lambda l: (l, 0, 0)),
        out_shape=jax.ShapeDtypeStruct((layers * nz, members, ny), BF16),
        compiler_params=params(),
        name="anomalies",
    )(prior, *totals, after)


def slots_kernel(probes, slot_ref, value_ref, var_ref, noise_ref, after, seen_ref, weight_ref, stack):
    members, count = noise_ref.shape
    stack[...] = jnp.zeros_like(stack)
    stack[0:members] = noise_ref[...]
    stack[members : members + 1] = value_ref[...]
    stack[members + 1 : members + 2] = var_ref[...]
    slot = slot_ref[...]
    place = lax.rem(slot, probes) * (count // probes) + slot // probes
    row = lax.broadcasted_iota(jnp.int32, (count, count), 0)
    chosen = jnp.where(row == place, 1.0, 0.0)
    ordered = lax.dot_general(
        chosen, stack[...], (((1,), (1,)), ((), ())), precision=lax.Precision.HIGHEST, preferred_element_type=F32
    )
    value = ordered[:, members : members + 1]
    var = ordered[:, members + 1 : members + 2]
    seen_ref[...] = value + jnp.sqrt(var) * ordered
    weight_ref[...] = jnp.broadcast_to(1.0 / var, weight_ref.shape)


def in_slots(slot, value, var, noise, probes, after):
    count = slot.shape[0]
    shape = jax.ShapeDtypeStruct((count, 128), F32)
    return pl.pallas_call(
        functools.partial(slots_kernel, probes),
        in_specs=[VMEM] * 4 + [pl.BlockSpec(memory_space=pl.ANY)],
        out_specs=[VMEM] * 2,
        out_shape=[shape, shape],
        scratch_shapes=[pltpu.VMEM((128, count), F32)],
        cost_estimate=pl.CostEstimate(flops=0, bytes_accessed=1 << 26, transcendentals=0),
        compiler_params=params(),
        name="slots",
    )(slot[None], value[None], var[None], noise, after)


def dot(a, b, dims):
    return lax.dot_general(a, b, (dims, ((), ())), precision=lax.Precision.HIGHEST, preferred_element_type=F32)


def solve_kernel(members, here, me_ref, vals_ref, seen_ref, weight_ref, out_ref, scr):
    devices, ny = vals_ref.shape
    groups = members // here
    tiles = devices // groups
    probes = 64 // here
    lane = lax.broadcasted_iota(jnp.int32, (tiles, ny), 1)
    parts = [vals_ref[pl.ds(g, tiles, stride=groups), :] for g in range(groups)]
    slabs = []
    for s in range(probes):
        slab = jnp.zeros((tiles, ny), F32)
        for g in range(groups):
            shift = (g - s) * here % ny
            moved = pltpu.roll(parts[g], shift, 1) if shift else parts[g]
            slab = jnp.where((lane >= g * here) & (lane < (g + 1) * here), moved, slab)
        slabs.append(slab)
    predicted = jnp.concatenate(slabs, axis=0)
    lanes = lax.broadcasted_iota(jnp.int32, predicted.shape, 1)
    mean = jnp.sum(predicted, axis=1, keepdims=True) / members
    spread = jnp.where(lanes < members, predicted - mean, 0.0)
    scaled = (spread * weight_ref[...]).T
    gram = dot(scaled, spread, ((1,), (0,)))
    rhs = dot(scaled, seen_ref[...] - predicted, ((1,), (0,)))
    half = 0.5 * jnp.max(jnp.sum(jnp.abs(gram), axis=1))
    alpha = 1.0 / (members - 1.0 + half)
    diagonal = lax.broadcasted_iota(jnp.int32, gram.shape, 0) == lax.broadcasted_iota(jnp.int32, gram.shape, 1)
    error = jnp.where(diagonal, alpha * half, 0.0) - alpha * gram

    def more(state):
        return (state[0] > 1e-9) & (state[1] < 40)

    def double(state):
        size, count, power_of, x = state
        both = dot(power_of, jnp.concatenate([power_of, x], axis=1), ((1,), (0,)))
        return size * size, count + 1, both[:, :ny], x + both[:, ny:]

    x = lax.while_loop(more, double, (half * alpha, 0, error, alpha * rhs))[3]
    me = me_ref[0]
    scr[...] = x
    order = [scr[pl.ds(pl.multiple_of((me ^ g) * here, here), here), :] for g in range(groups)]
    scr[...] = jnp.concatenate(order + [jnp.zeros((ny - members, ny), F32)], axis=0).T
    mine = scr[pl.ds(pl.multiple_of(me * here, here), here), :]
    copies = out_ref.shape[1] // members
    wide = jnp.concatenate([mine + pltpu.roll(mine, members, 1)] * (copies // 2), axis=1)
    wide = jnp.concatenate([wide] * copies, axis=0)
    row = lax.broadcasted_iota(jnp.int32, wide.shape, 0)
    column = lax.broadcasted_iota(jnp.int32, wide.shape, 1)
    out_ref[...] = jnp.where(row // here == column // members, wide, 0.0).astype(BF16)


def solve(vals, seen, weight, me, members, here):
    return pl.pallas_call(
        functools.partial(solve_kernel, members, here),
        in_specs=[SMEM] + [VMEM] * 3,
        out_specs=VMEM,
        out_shape=jax.ShapeDtypeStruct((AT_ONCE * here, AT_ONCE * members), BF16),
        scratch_shapes=[pltpu.VMEM((128, 128), F32)],
        compiler_params=params(),
        name="solve",
    )(me, vals, seen, weight)


def update_kernel(weights_ref, prior_ref, *refs):
    blocks, out_ref = refs[:-1], refs[-1]
    members, _, nz, ny = prior_ref.shape
    flat = prior_ref.reshape(members * nz, ny)
    out = out_ref.reshape(members * nz, ny)
    weights = weights_ref[...]
    for z in range(0, nz, 2 * AT_ONCE):
        sides = []
        for i in range(2):
            rows = range(z + i * AT_ONCE, z + (i + 1) * AT_ONCE)
            sides.append(jnp.concatenate([b[r] for r in rows for b in blocks], axis=0))
        update = jnp.dot(weights, jnp.concatenate(sides, axis=1), preferred_element_type=F32)
        for i in range(2):
            for r in range(AT_ONCE):
                where = pl.ds(z + i * AT_ONCE + r, members, stride=nz)
                part = update[r * members : (r + 1) * members, i * ny : (i + 1) * ny]
                out[where, :] = flat[where, :] + part


def updated(weights, prior, blocks):
    members, layers, nz, ny = prior.shape
    block = pl.BlockSpec((members, 1, nz, ny), lambda l: (0, l, 0, 0))
    part = pl.BlockSpec((nz, members, ny), lambda l: (l, 0, 0))
    return pl.pallas_call(
        update_kernel,
        grid=(layers,),
        in_specs=[pl.BlockSpec(weights.shape, lambda l: (0, 0)), block] + [part] * len(blocks),
        out_specs=block,
        out_shape=jax.ShapeDtypeStruct(prior.shape, F32),
        compiler_params=params(),
        name="update",
    )(weights, prior, *blocks)


def per_device(prior, base_flow, base_visc, probe_cells, obs_slot, obs_values, obs_var, obs_noise):
    here = prior.shape[0]
    tiles, groups = lax.axis_size("tile"), lax.axis_size("mem")
    members = here * groups
    me = lax.axis_index("mem").astype(jnp.int32).reshape(1)

    def along(x, step):
        return lax.ppermute(x, "tile", [(i, (i + step) % tiles) for i in range(tiles)])

    def across(x, bits):
        return lax.ppermute(x, "mem", [(i, i ^ bits) for i in range(groups)])

    sent = encode(prior, base_flow, base_visc)
    halos = [(along(sent[2 * c], 1), along(sent[2 * c + 1], -1)) for c in range(CHUNKS)]
    state, states = None, []
    for chunk in range(CHUNKS):
        state = sweeps(prior, base_flow, base_visc, probe_cells, halos[chunk], chunk, state, tiles * groups)
        states.append(state)
    velocity, payload = state[:2]
    total = total_of(prior, states[TOTAL_AFTER][1])
    totals = [total] + [across(total, bits) for bits in (1, 2, 3)]
    mine = anomalies(prior, totals, float(members), states[ANOMALY_AFTER][1])
    beside = across(mine, 1)
    over = across(mine, 2)
    vals = lax.all_to_all(payload, ("tile", "mem"), 0, 0, tiled=True)
    seen, weight = in_slots(obs_slot, obs_values, obs_var, obs_noise, probe_cells.shape[1], payload)
    over = held(over, vals, seen)
    blocks = [mine, beside, over, across(over, 1)]
    weights = solve(vals, seen, weight, me, members, here)
    return velocity, updated(weights, prior, blocks)


def solution(mesh):
    placed = (
        P("mem", "tile", None, None),
        P("tile", None, None),
        P("tile", None, None),
        P("tile", None),
        P(),
        P(),
        P(),
        P(),
    )
    return jax.shard_map(
        per_device,
        mesh=mesh,
        in_specs=placed,
        out_specs=(P("mem", "tile", None, None), P("mem", "tile", None, None)),
        check_vma=False,
    )
```

time: 93 us -> 74.4 us (0.80)
  waiting for transfers between devices: 43.7 us -> 11.8 us
  starting transfers between devices: 26.6 us -> 37.9 us
  Pallas kernels: 17.6 us -> 20 us
    ppermute x6, waiting for transfers between devices: 29.3 us -> 0.02 us  [across(): return lax.ppermute(x, 'mem', [(i, i ^ bits) for i in range(groups)])]
    ppermute x4 -> x6, starting transfers between devices: 9.67 us -> 25.4 us  [along(): lax.ppermute(x, 'tile', [(i, (i + step) % tiles) for i in range(tiles)])]
    all_to_all x1, starting transfers between devices: 10 us -> 5.61 us  [per_device(): vals = lax.all_to_all(payload, ('tile', 'mem'), 0, 0, tiled=True)]
    ppermute x4 -> x6, waiting for transfers between devices: 2.94 us -> 0.52 us  [along(): lax.ppermute(x, 'tile', [(i, (i + step) % tiles) for i in range(tiles)])]
    pallas_call x4 -> x6, Pallas kernels: 9.73 us -> 12.1 us  [the longest x3 10.2 us: sweeps(): pl.pallas_call(functools.partial(sweep_kernel, chunk, devices), grid=(1,)...]
    unnamed x22 -> x28, local copies, waits for them, and re-layouts: 4.06 us -> 3.65 us
  transfers between devices with their start and end apart: 11 -> 13, of which waited for: 7 -> 2; matrix products, arithmetic and copies ran while one was open for 0% -> 0% of each run, Pallas kernels for 13% -> 18%
where the time goes in v2:
time: 74.4 us; the launch traced here: 74.1 us
  starting transfers between devices  37.9 us (51%)
  Pallas kernels  20 us (27%)
  waiting for transfers between devices  11.8 us (16%)
  local copies, waits for them, and re-layouts  3.65 us (5%)
  between operations  0.83 us (1%)
    ppermute x6, starting transfers between devices, along(): lax.ppermute(x, 'tile', [(i, (i + step) % tiles) for i in range(tiles)])  25.4 us
    all_to_all x1, waiting for transfers between devices, per_device(): vals = lax.all_to_all(payload, ('tile', 'mem'), 0, 0, tiled=True)  11.3 us
    pallas_call x3, Pallas kernels, sweeps(): pl.pallas_call(functools.partial(sweep_kernel, chunk, devices), grid=(1,)...  10.2 us
    ppermute x6, starting transfers between devices, across(): return lax.ppermute(x, 'mem', [(i, i ^ bits) for i in range(groups)])  6.93 us
    all_to_all x1, starting transfers between devices, per_device(): vals = lax.all_to_all(payload, ('tile', 'mem'), 0, 0, tiled=True)  5.61 us
    pallas_call x1, Pallas kernels, updated(): pl.pallas_call(update_kernel, grid=(layers,), in_specs=[pl.BlockSpec(weig...  4.12 us
    unnamed x28, local copies, waits for them, and re-layouts  3.65 us
    pallas_call x1, Pallas kernels, solve(): pl.pallas_call(functools.partial(solve_kernel, members, here), in_specs=[...  2.51 us
  transfers between devices with their start and end apart: 13, of which 2 were waited for; matrix products, arithmetic and copies ran while one was open for 0% of the time, Pallas kernels for 18%

profile of v2, /device:TPU:1, one launch (start us, length us, event | category | flops | bytes accessed | tf_op | source)
XLA Modules:
  0.0 74.1 jit_solution(12716547101824825785)
XLA Ops:
  0.7 1.9 %encode.1 = (bf16[28,48,128]{2,1,0:T(8,128)(2,1)S(1)}, bf16[28,48,128]{2,1,0:T(8,128)(2,1)S(1)}, bf16[12,48,128]{2,1,0:T(8,128)(2,1)S(1)}, bf16[12,48,128]{2,1,0...) custom-call(f32[16,4,48,128]{3,2,1,0:T(8,128)} %prior_ref.11, ...), custom_call_target="tpu_custom_call" | custom-call | tf_op jit(solution)/shard_map/encode/pallas_call | solution.py:81
  2.5 2.5 %collective-permute-start.2 = (bf16[28,48,128]{2,1,0:T(8,128)(2,1)S(1)}, bf16[28,48,128]{2,1,0:T(8,128)(2,1)S(1)}, u32[]{:S(2)}, u32[]{:S(2)}) collective-permute-start(bf16[28,48,128]{2,1,0:T(8,128)(2,1)S(1)} %get-tuple-element.20), channel_id=1, source_target_pairs={{0,4},{4,8},{8,12},{12,16},{16,20},{20,24},{24,28},{28,32},{32,36}... | collective-permute-start | bytes 1032200 | tf_op jit(solution)/shard_map/ppermute | solution.py:415
  5.1 8.9 %collective-permute-start.3 = (bf16[28,48,128]{2,1,0:T(8,128)(2,1)S(1)}, bf16[28,48,128]{2,1,0:T(8,128)(2,1)S(1)}, u32[]{:S(2)}, u32[]{:S(2)}) collective-permute-start(bf16[28,48,128]{2,1,0:T(8,128)(2,1)S(1)} %get-tuple-element.21), channel_id=1, source_target_pairs={{0,252},{4,0},{8,4},{12,8},{16,12},{20,16},{24,20},{28,24},{32,28}... | collective-permute-start | bytes 1032200 | tf_op jit(solution)/shard_map/ppermute | solution.py:415
  14.0 7.2 %collective-permute-start.5 = (bf16[12,48,128]{2,1,0:T(8,128)(2,1)S(1)}, bf16[12,48,128]{2,1,0:T(8,128)(2,1)S(1)}, u32[]{:S(2)}, u32[]{:S(2)}) collective-permute-start(bf16[12,48,128]{2,1,0:T(8,128)(2,1)S(1)} %get-tuple-element.25), channel_id=1, source_target_pairs={{0,252},{4,0},{8,4},{12,8},{16,12},{20,16},{24,20},{28,24},{32,28}... | collective-permute-start | bytes 442376 | tf_op jit(solution)/shard_map/ppermute | solution.py:415
  21.2 0.5 collective-permute-done.2.behind_ref
  21.7 6.7 %collective-permute-start.1 = (bf16[12,48,128]{2,1,0:T(8,128)(2,1)S(1)}, bf16[12,48,128]{2,1,0:T(8,128)(2,1)S(1)}, u32[]{:S(2)}, u32[]{:S(2)}) collective-permute-start(bf16[12,48,128]{2,1,0:T(8,128)(2,1)S(1)} %get-tuple-element.19), channel_id=1, source_target_pairs={{0,252},{4,0},{8,4},{12,8},{16,12},{20,16},{24,20},{28,24},{32,28}... | collective-permute-start | bytes 442376 | tf_op jit(solution)/shard_map/ppermute | solution.py:415
  28.4 4.6 %sweeps0.1 = (f32[16,4,48,128]{3,2,1,0:T(8,128)}, f32[64,128]{1,0:T(8,128)S(1)}, f32[10,48,128]{2,1,0:T(8,128)S(1)}, f32[10,48,128]{2,1,0:T(8,128)S(1)}) custom-call(s32[1,4]{1,0:T(1,128)S(1)} %copy-done.10, f32[16,4,48,128]{3,2,1,0:T(8,128)S(1)} %copy-done, f32[4,48,128]{2,1,0:T(8,128)S(1)} %copy-done.3, f32[4,48,128]{2,1,0:T(8,128)S(1)} %copy-done.4, ...), custom_call_target="tpu_custom_call" | custom-call | tf_op jit(solution)/shard_map/sweeps0/pallas_call | solution.py:238
  33.1 2.4 %collective-permute-start.8 = (f32[4,48,128]{2,1,0:T(8,128)S(1)}, f32[4,48,128]{2,1,0:T(8,128)S(1)}, u32[]{:S(2)}, u32[]{:S(2)}) collective-permute-start(f32[4,48,128]{2,1,0:T(8,128)S(1)} %total.1.a_ref), channel_id=1, source_target_pairs={{0,3},{1,2},{2,1},{3,0},{4,7},{5,6},{6,5},{7,4},{8,11},{9,10},{10,... | collective-permute-start | bytes 294920 | tf_op jit(solution)/shard_map/ppermute | solution.py:418
  35.5 1.2 %collective-permute-start.7 = (f32[4,48,128]{2,1,0:T(8,128)S(1)}, f32[4,48,128]{2,1,0:T(8,128)S(1)}, u32[]{:S(2)}, u32[]{:S(2)}) collective-permute-start(f32[4,48,128]{2,1,0:T(8,128)S(1)} %total.1.a_ref), channel_id=1, source_target_pairs={{0,2},{1,3},{2,0},{3,1},{4,6},{5,7},{6,4},{7,5},{8,10},{9,11},{10,... | collective-permute-start | bytes 294920 | tf_op jit(solution)/shard_map/ppermute | solution.py:418
  36.7 2.8 %sweeps1.1 = (f32[16,4,48,128]{3,2,1,0:T(8,128)}, f32[64,128]{1,0:T(8,128)S(1)}) custom-call(s32[1,4]{1,0:T(1,128)S(1)} %copy-done.10, f32[16,4,48,128]{3,2,1,0:T(8,128)S(1)} %copy-done, f32[4,48,128]{2,1,0:T(8,128)S(1)} %copy-done.3, f32[4,48,128]{2,1,0:T(8,128)S(1)} %copy-done.4, ...), custom_call_target="tpu_custom_call", output_to_operand_aliasing={{0}: (9, {})} | custom-call | tf_op jit(solution)/shard_map/sweeps1/pallas_call | solution.py:238
  39.4 2.8 %sweeps2.1 = (f32[16,4,48,128]{3,2,1,0:T(8,128)}, f32[256,128]{1,0:T(8,128)}) custom-call(s32[1,4]{1,0:T(1,128)S(1)} %copy-done.10, f32[16,4,48,128]{3,2,1,0:T(8,128)S(1)} %copy-done, f32[4,48,128]{2,1,0:T(8,128)S(1)} %copy-done.3, f32[4,48,128]{2,1,0:T(8,128)S(1)} %copy-done.4, ...), custom_call_target="tpu_custom_call", output_to_operand_aliasing={{0}: (9, {})} | custom-call | tf_op jit(solution)/shard_map/sweeps2/pallas_call | solution.py:238
  42.3 0.7 anomalies.1.refs_0_
  43.0 0.6 collective-permute-start.10
  43.6 5.6 %all-to-all-start = ((f32[256,1,128]{2,1,0:T(1,128)}), f32[256,1,128]{2,1,0:T(1,128)S(1)}, u32[]{:S(2)}, u32[]{:S(2)}) async-start(f32[256,1,128]{2,1,0:T(1,128)} %bitcast.2), calls=%async_computation | async-start | bytes 262144 | tf_op jit(solution)/shard_map/all_to_all | solution.py:432
  49.3 0.5 slots.1
  49.8 0.6 copy-done.7
  50.4 2.3 %collective-permute-start.9 = (bf16[192,16,128]{2,1,0:T(8,128)(2,1)S(1)}, bf16[192,16,128]{2,1,0:T(8,128)(2,1)}, u32[]{:S(2)}, u32[]{:S(2)}) collective-permute-start(bf16[192,16,128]{2,1,0:T(8,128)(2,1)S(1)} %anomalies.1.refs_0_), channel_id=1, source_target_pairs={{0,1},{1,0},{2,3},{3,2},{4,5},{5,4},{6,7},{7,6},{8,9},{9,8},{10,11... | collective-permute-start | bytes 2359304 | tf_op jit(solution)/shard_map/ppermute | solution.py:418
  52.7 11.3 %all-to-all-done = f32[256,1,128]{2,1,0:T(1,128)S(1)} async-done(((f32[256,1,128]{2,1,0:T(1,128)}), f32[256,1,128]{2,1,0:T(1,128)S(1)}, u32[]{:S(2)}, u32[]{:S(2)}) %all-to-all-start) | async-done | bytes 131104 | tf_op jit(solution)/shard_map/all_to_all | solution.py:432
  64.0 0.7 copy-done.5
  64.9 0.5 collective-permute-start.11
  65.4 0.9 %copy-done.6 = f32[256,1,128]{2,1,0:T(1,128)S(1)} copy-done((f32[256,1,128]{2,1,0:T(1,128)S(1)}, f32[256,1,128]{2,1,0:T(1,128)}, u32[]{:S(2)}) %copy-start.6) | copy-done | bytes 131096
  66.3 2.5 %solve.1.weights_ref = bf16[64,256]{1,0:T(8,128)(2,1)S(1)} custom-call(s32[1]{0:T(128)} %bitcast.me_ref, f32[256,128]{1,0:T(8,128)S(1)} %bitcast.9, f32[256,128]{1,0:T(8,128)S(1)} %copy-done.8, f32[256,128]{1,0:T(8,128)S(1)} %get-tuple-element.33.weight_ref), custom_call_target="tpu_custom_call" | custom-call | tf_op jit(solution)/shard_map/solve/pallas_call | solution.py:363
  68.9 1.1 %copy-done.2 = bf16[192,16,128]{2,1,0:T(8,128)(2,1)S(1)} copy-done((bf16[192,16,128]{2,1,0:T(8,128)(2,1)S(1)}, bf16[192,16,128]{2,1,0:T(8,128)(2,1)}, u32[]{:S(2)}) %copy-start.2) | copy-done | bytes 786456
  70.0 4.1 %update.1 = f32[16,4,48,128]{3,2,1,0:T(8,128)} custom-call(bf16[64,256]{1,0:T(8,128)(2,1)S(1)} %solve.1.weights_ref, f32[16,4,48,128]{3,2,1,0:T(8,128)S(1)} %copy-done, bf16[192,16,128]{2,1,0:T(8,128)(2,1)S(1)} %anomalies.1.refs_0_, bf16[192,16,128]{2,1,0:T(8,128)(2,1)} %collective-permute-done.9.refs_1_, bf16[192,16,128]{2,1,0:T(8,128)(2,1)S(1)} %copy-done.2, ...), custom_call_target="tpu_custom_call" | custom-call | tf_op jit(solution)/shard_map/update/pallas_call | solution.py:397
  (40 shorter events, 0.4 us)
Async XLA Ops:
  0.6 27.8 %copy-start = (f32[16,4,48,128]{3,2,1,0:T(8,128)S(1)}, f32[16,4,48,128]{3,2,1,0:T(8,128)}, u32[]{:S(2)}) copy-start(f32[16,4,48,128]{3,2,1,0:T(8,128)} %prior_ref.11) | copy-start | bytes 4718596
  0.6 27.8 %copy-start.4 = (f32[4,48,128]{2,1,0:T(8,128)S(1)}, f32[4,48,128]{2,1,0:T(8,128)}, u32[]{:S(2)}) copy-start(f32[4,48,128]{2,1,0:T(8,128)} %visc_ref.5) | copy-start | bytes 294916
  0.7 27.8 %copy-start.3 = (f32[4,48,128]{2,1,0:T(8,128)S(1)}, f32[4,48,128]{2,1,0:T(8,128)}, u32[]{:S(2)}) copy-start(f32[4,48,128]{2,1,0:T(8,128)} %flow_ref.5) | copy-start | bytes 294916
  0.7 27.8 %copy-start.10 = (s32[1,4]{1,0:T(1,128)S(1)}, s32[1,4]{1,0:T(1,128)}, u32[]{:S(2)}) copy-start(s32[1,4]{1,0:T(1,128)} %cells_ref.5) | copy-start | bytes 52
  2.5 19.2 %collective-permute-start.2 = (bf16[28,48,128]{2,1,0:T(8,128)(2,1)S(1)}, bf16[28,48,128]{2,1,0:T(8,128)(2,1)S(1)}, u32[]{:S(2)}, u32[]{:S(2)}) collective-permute-start(bf16[28,48,128]{2,1,0:T(8,128)(2,1)S(1)} %get-tuple-element.20), channel_id=1, source_target_pairs={{0,4},{4,8},{8,12},{12,16},{16,20},{20,24},{24,28},{28,32},{32,36}... | collective-permute-start | bytes 1032200 | tf_op jit(solution)/shard_map/ppermute | solution.py:415
  5.1 23.3 %collective-permute-start.3 = (bf16[28,48,128]{2,1,0:T(8,128)(2,1)S(1)}, bf16[28,48,128]{2,1,0:T(8,128)(2,1)S(1)}, u32[]{:S(2)}, u32[]{:S(2)}) collective-permute-start(bf16[28,48,128]{2,1,0:T(8,128)(2,1)S(1)} %get-tuple-element.21), channel_id=1, source_target_pairs={{0,252},{4,0},{8,4},{12,8},{16,12},{20,16},{24,20},{28,24},{32,28}... | collective-permute-start | bytes 1032200 | tf_op jit(solution)/shard_map/ppermute | solution.py:415
  14.0 21.5 %collective-permute-start.4 = (bf16[12,48,128]{2,1,0:T(8,128)(2,1)S(1)}, bf16[12,48,128]{2,1,0:T(8,128)(2,1)S(1)}, u32[]{:S(2)}, u32[]{:S(2)}) collective-permute-start(bf16[12,48,128]{2,1,0:T(8,128)(2,1)S(1)} %get-tuple-element.24), channel_id=1, source_target_pairs={{0,4},{4,8},{8,12},{12,16},{16,20},{20,24},{24,28},{28,32},{32,36}... | collective-permute-start | bytes 442376 | tf_op jit(solution)/shard_map/ppermute | solution.py:415
  14.0 22.6 %collective-permute-start.5 = (bf16[12,48,128]{2,1,0:T(8,128)(2,1)S(1)}, bf16[12,48,128]{2,1,0:T(8,128)(2,1)S(1)}, u32[]{:S(2)}, u32[]{:S(2)}) collective-permute-start(bf16[12,48,128]{2,1,0:T(8,128)(2,1)S(1)} %get-tuple-element.25), channel_id=1, source_target_pairs={{0,252},{4,0},{8,4},{12,8},{16,12},{20,16},{24,20},{28,24},{32,28}... | collective-permute-start | bytes 442376 | tf_op jit(solution)/shard_map/ppermute | solution.py:415
  21.2 18.2 %collective-permute-start = (bf16[12,48,128]{2,1,0:T(8,128)(2,1)S(1)}, bf16[12,48,128]{2,1,0:T(8,128)(2,1)S(1)}, u32[]{:S(2)}, u32[]{:S(2)}) collective-permute-start(bf16[12,48,128]{2,1,0:T(8,128)(2,1)S(1)} %get-tuple-element.18), channel_id=1, source_target_pairs={{0,4},{4,8},{8,12},{12,16},{16,20},{20,24},{24,28},{28,32},{32,36}... | collective-permute-start | bytes 442376 | tf_op jit(solution)/shard_map/ppermute | solution.py:415
  21.7 17.7 %collective-permute-start.1 = (bf16[12,48,128]{2,1,0:T(8,128)(2,1)S(1)}, bf16[12,48,128]{2,1,0:T(8,128)(2,1)S(1)}, u32[]{:S(2)}, u32[]{:S(2)}) collective-permute-start(bf16[12,48,128]{2,1,0:T(8,128)(2,1)S(1)} %get-tuple-element.19), channel_id=1, source_target_pairs={{0,252},{4,0},{8,4},{12,8},{16,12},{20,16},{24,20},{28,24},{32,28}... | collective-permute-start | bytes 442376 | tf_op jit(solution)/shard_map/ppermute | solution.py:415
  33.1 9.1 %collective-permute-start.8 = (f32[4,48,128]{2,1,0:T(8,128)S(1)}, f32[4,48,128]{2,1,0:T(8,128)S(1)}, u32[]{:S(2)}, u32[]{:S(2)}) collective-permute-start(f32[4,48,128]{2,1,0:T(8,128)S(1)} %total.1.a_ref), channel_id=1, source_target_pairs={{0,3},{1,2},{2,1},{3,0},{4,7},{5,6},{6,5},{7,4},{8,11},{9,10},{10,... | collective-permute-start | bytes 294920 | tf_op jit(solution)/shard_map/ppermute | solution.py:418
  35.5 6.8 %collective-permute-start.7 = (f32[4,48,128]{2,1,0:T(8,128)S(1)}, f32[4,48,128]{2,1,0:T(8,128)S(1)}, u32[]{:S(2)}, u32[]{:S(2)}) collective-permute-start(f32[4,48,128]{2,1,0:T(8,128)S(1)} %total.1.a_ref), channel_id=1, source_target_pairs={{0,2},{1,3},{2,0},{3,1},{4,6},{5,7},{6,4},{7,5},{8,10},{9,11},{10,... | collective-permute-start | bytes 294920 | tf_op jit(solution)/shard_map/ppermute | solution.py:418
  36.6 5.6 %collective-permute-start.6 = (f32[4,48,128]{2,1,0:T(8,128)S(1)}, f32[4,48,128]{2,1,0:T(8,128)S(1)}, u32[]{:S(2)}, u32[]{:S(2)}) collective-permute-start(f32[4,48,128]{2,1,0:T(8,128)S(1)} %total.1.a_ref), channel_id=1, source_target_pairs={{0,1},{1,0},{2,3},{3,2},{4,5},{5,4},{6,7},{7,6},{8,9},{9,8},{10,11... | collective-permute-start | bytes 294920 | tf_op jit(solution)/shard_map/ppermute | solution.py:418
  42.3 7.0 %copy-start.9 = (f32[64,256]{1,0:T(8,128)S(1)}, f32[64,256]{1,0:T(8,128)}, u32[]{:S(2)}) copy-start(f32[64,256]{1,0:T(8,128)} %noise_ref.1) | copy-start | bytes 196612
  42.3 7.0 %copy-start.11 = (s32[256]{0:T(256)S(1)}, s32[256]{0:T(256)}, u32[]{:S(2)}) copy-start(s32[256]{0:T(256)} %param.12) | copy-start | bytes 3076
  42.3 7.0 %copy-start.12 = (f32[256]{0:T(256)S(1)}, f32[256]{0:T(256)}, u32[]{:S(2)}) copy-start(f32[256]{0:T(256)} %param.13) | copy-start | bytes 3076
  42.3 7.0 %copy-start.13 = (f32[256]{0:T(256)S(1)}, f32[256]{0:T(256)}, u32[]{:S(2)}) copy-start(f32[256]{0:T(256)} %param.14) | copy-start | bytes 3076
  43.0 21.0 %collective-permute-start.10 = (bf16[192,16,128]{2,1,0:T(8,128)(2,1)S(1)}, bf16[192,16,128]{2,1,0:T(8,128)(2,1)S(1)}, u32[]{:S(2)}, u32[]{:S(2)}) collective-permute-start(bf16[192,16,128]{2,1,0:T(8,128)(2,1)S(1)} %anomalies.1.refs_0_), channel_id=1, source_target_pairs={{0,2},{1,3},{2,0},{3,1},{4,6},{5,7},{6,4},{7,5},{8,10},{9,11},{10,... | collective-permute-start | bytes 2359304 | tf_op jit(solution)/shard_map/ppermute | solution.py:418
  43.6 20.4 %all-to-all-start = ((f32[256,1,128]{2,1,0:T(1,128)}), f32[256,1,128]{2,1,0:T(1,128)S(1)}, u32[]{:S(2)}, u32[]{:S(2)}) async-start(f32[256,1,128]{2,1,0:T(1,128)} %bitcast.2), calls=%async_computation | async-start | bytes 262144 | tf_op jit(solution)/shard_map/all_to_all | solution.py:432
  50.4 18.4 %collective-permute-start.9 = (bf16[192,16,128]{2,1,0:T(8,128)(2,1)S(1)}, bf16[192,16,128]{2,1,0:T(8,128)(2,1)}, u32[]{:S(2)}, u32[]{:S(2)}) collective-permute-start(bf16[192,16,128]{2,1,0:T(8,128)(2,1)S(1)} %anomalies.1.refs_0_), channel_id=1, source_target_pairs={{0,1},{1,0},{2,3},{3,2},{4,5},{5,4},{6,7},{7,6},{8,9},{9,8},{10,11... | collective-permute-start | bytes 2359304 | tf_op jit(solution)/shard_map/ppermute | solution.py:418
  52.7 12.7 %copy-start.8 = (f32[256,128]{1,0:T(8,128)S(1)}, f32[256,128]{1,0:T(8,128)}, u32[]{:S(2)}) copy-start(f32[256,128]{1,0:T(8,128)} %copy-done.7) | copy-start | bytes 393220
  64.0 0.9 %copy-start.1 = (bf16[192,16,128]{2,1,0:T(8,128)(2,1)}, bf16[192,16,128]{2,1,0:T(8,128)(2,1)S(1)}, u32[]{:S(2)}) copy-start(bf16[192,16,128]{2,1,0:T(8,128)(2,1)S(1)} %collective-permute-done.10.refs_0_) | copy-start | bytes 2359300
  64.9 4.0 %collective-permute-start.11 = (bf16[192,16,128]{2,1,0:T(8,128)(2,1)}, bf16[192,16,128]{2,1,0:T(8,128)(2,1)S(1)}, u32[]{:S(2)}, u32[]{:S(2)}) collective-permute-start(bf16[192,16,128]{2,1,0:T(8,128)(2,1)} %hold.1.refs_2_), channel_id=1, source_target_pairs={{0,1},{1,0},{2,3},{3,2},{4,5},{5,4},{6,7},{7,6},{8,9},{9,8},{10,11... | collective-permute-start | bytes 2359304 | tf_op jit(solution)/shard_map/ppermute | solution.py:418
  68.9 1.1 %copy-start.2 = (bf16[192,16,128]{2,1,0:T(8,128)(2,1)S(1)}, bf16[192,16,128]{2,1,0:T(8,128)(2,1)}, u32[]{:S(2)}) copy-start(bf16[192,16,128]{2,1,0:T(8,128)(2,1)} %hold.1.refs_2_) | copy-start | bytes 2359300
  (3 other events, 2.2 us)

commit v3 on v2

--- a/solution.py
+++ b/solution.py
@@ -9,10 +9,10 @@
 from jax.sharding import PartitionSpec as P
 
 ITERS = 4
-PARTS = ((8, 0), (4, 2), (4, 3))
+PARTS = ((8, 0), (8, 1))
 CHUNKS = len(PARTS)
 AT_ONCE = 4
-TOTAL_AFTER, ANOMALY_AFTER = 0, 2
+TOTAL_AFTER, ANOMALY_AFTER = 0, 1
 LOG_MID = 0.5 * (math.log(0.02) + math.log(0.05))
 LOG_HALF = 0.5 * (math.log(0.05) - math.log(0.02)) + 1.0
 NU_SCALE = 124.0 / LOG_HALF
@@ -24,7 +24,7 @@
 BF16 = jnp.bfloat16
 
 
-def params(mib=48):
+def params(mib=24):
     return pltpu.CompilerParams(vmem_limit_bytes=mib * 1024 * 1024)
 
 
@@ -117,13 +117,13 @@
 
 
 def held(value, *after):
-    anywhere = pl.BlockSpec(memory_space=pl.ANY)
     return pl.pallas_call(
         hold_kernel,
-        in_specs=[anywhere] * (1 + len(after)),
-        out_specs=anywhere,
+        in_specs=[VMEM] * (1 + len(after)),
+        out_specs=VMEM,
         out_shape=jax.ShapeDtypeStruct(value.shape, value.dtype),
         input_output_aliases={0: 0},
+        compiler_params=params(),
         name="hold",
     )(value, *after)
 

time: 74.4 us -> 66.3 us (0.89)
  local copies, waits for them, and re-layouts: 3.65 us -> 0.86 us
  starting transfers between devices: 37.9 us -> 35.6 us
  waiting for transfers between devices: 11.8 us -> 9.85 us
  Pallas kernels: 20 us -> 19 us
    ppermute x6 -> x4, starting transfers between devices: 25.4 us -> 18.7 us  [along(): lax.ppermute(x, 'tile', [(i, (i + step) % tiles) for i in range(tiles)])]
    all_to_all x1, starting transfers between devices: 5.61 us -> 10 us  [per_device(): vals = lax.all_to_all(payload, ('tile', 'mem'), 0, 0, tiled=True)]
    unnamed x28 -> x16, local copies, waits for them, and re-layouts: 3.65 us -> 0.86 us
    all_to_all x1, waiting for transfers between devices: 11.3 us -> 9.18 us  [per_device(): vals = lax.all_to_all(payload, ('tile', 'mem'), 0, 0, tiled=True)]
    pallas_call x3 -> x2, Pallas kernels: 10.2 us -> 9.06 us  [sweeps(): pl.pallas_call(functools.partial(sweep_kernel, chunk, devices), grid=(1,)...]
  transfers between devices with their start and end apart: 13 -> 11, of which waited for: 2 -> 3; matrix products, arithmetic and copies ran while one was open for 0% -> 0% of each run, Pallas kernels for 18% -> 18%
where the time goes in v3:
time: 66.3 us; the launch traced here: 66.1 us
  starting transfers between devices  35.6 us (54%)
  Pallas kernels  19 us (29%)
  waiting for transfers between devices  9.85 us (15%)
  local copies, waits for them, and re-layouts  0.86 us (1%)
  between operations  0.79 us (1%)
    ppermute x4, starting transfers between devices, along(): lax.ppermute(x, 'tile', [(i, (i + step) % tiles) for i in range(tiles)])  18.7 us
    all_to_all x1, starting transfers between devices, per_device(): vals = lax.all_to_all(payload, ('tile', 'mem'), 0, 0, tiled=True)  10 us
    all_to_all x1, waiting for transfers between devices, per_device(): vals = lax.all_to_all(payload, ('tile', 'mem'), 0, 0, tiled=True)  9.18 us
    pallas_call x2, Pallas kernels, sweeps(): pl.pallas_call(functools.partial(sweep_kernel, chunk, devices), grid=(1,)...  9.06 us
    ppermute x6, starting transfers between devices, across(): return lax.ppermute(x, 'mem', [(i, i ^ bits) for i in range(groups)])  6.89 us
    pallas_call x1, Pallas kernels, updated(): pl.pallas_call(update_kernel, grid=(layers,), in_specs=[pl.BlockSpec(weig...  4.36 us
    pallas_call x1, Pallas kernels, solve(): pl.pallas_call(functools.partial(solve_kernel, members, here), in_specs=[...  2.51 us
    pallas_call x1, Pallas kernels, encode(): pl.pallas_call(encode_kernel, in_specs=[pl.BlockSpec(memory_space=pltpu.H...  1.85 us
  transfers between devices with their start and end apart: 11, of which 3 were waited for; matrix products, arithmetic and copies ran while one was open for 0% of the time, Pallas kernels for 18%

profile of v3, /device:TPU:1, one launch (start us, length us, event | category | flops | bytes accessed | tf_op | source)
XLA Modules:
  0.0 66.1 jit_solution(2078608152642806678)
XLA Ops:
  0.7 1.9 %encode.1 = (bf16[28,48,128]{2,1,0:T(8,128)(2,1)S(1)}, bf16[28,48,128]{2,1,0:T(8,128)(2,1)S(1)}, bf16[24,48,128]{2,1,0:T(8,128)(2,1)S(1)}, bf16[24,48,128]{2,1,0:T(8,128)(2,1)S(1)}) custom-call(f32[16,4,48,128]{3,2,1,0:T(8,128)} %prior_ref.9, f32[4,48,128]{2,1,0:T(8,128)} %flow_ref.3, f32[4,48,128]{2,1,0:T(8,128)} %visc_ref.3), custom_call_target="tpu_custom_call" | custom-call | tf_op jit(solution)/shard_map/encode/pallas_call | solution.py:81
  2.5 2.5 %collective-permute-start.2 = (bf16[28,48,128]{2,1,0:T(8,128)(2,1)S(1)}, bf16[28,48,128]{2,1,0:T(8,128)(2,1)S(1)}, u32[]{:S(2)}, u32[]{:S(2)}) collective-permute-start(bf16[28,48,128]{2,1,0:T(8,128)(2,1)S(1)} %get-tuple-element.16), channel_id=1, source_target_pairs={{0,4},{4,8},{8,12},{12,16},{16,20},{20,24},{24,28},{28,32},{32,36}... | collective-permute-start | bytes 1032200 | tf_op jit(solution)/shard_map/ppermute | solution.py:415
  5.1 8.9 %collective-permute-start.3 = (bf16[28,48,128]{2,1,0:T(8,128)(2,1)S(1)}, bf16[28,48,128]{2,1,0:T(8,128)(2,1)S(1)}, u32[]{:S(2)}, u32[]{:S(2)}) collective-permute-start(bf16[28,48,128]{2,1,0:T(8,128)(2,1)S(1)} %get-tuple-element.17), channel_id=1, source_target_pairs={{0,252},{4,0},{8,4},{12,8},{16,12},{20,16},{24,20},{28,24},{32,28}... | collective-permute-start | bytes 1032200 | tf_op jit(solution)/shard_map/ppermute | solution.py:415
  14.0 0.0 collective-permute-start
  14.0 7.2 %collective-permute-start.1 = (bf16[24,48,128]{2,1,0:T(8,128)(2,1)S(1)}, bf16[24,48,128]{2,1,0:T(8,128)(2,1)S(1)}, u32[]{:S(2)}, u32[]{:S(2)}) collective-permute-start(bf16[24,48,128]{2,1,0:T(8,128)(2,1)S(1)} %get-tuple-element.15), channel_id=1, source_target_pairs={{0,252},{4,0},{8,4},{12,8},{16,12},{20,16},{24,20},{28,24},{32,28}... | collective-permute-start | bytes 884744 | tf_op jit(solution)/shard_map/ppermute | solution.py:415
  21.2 0.5 collective-permute-done.2.behind_ref
  21.7 4.6 %sweeps0.1 = (f32[16,4,48,128]{3,2,1,0:T(8,128)}, f32[64,128]{1,0:T(8,128)S(1)}, f32[10,48,128]{2,1,0:T(8,128)S(1)}, f32[10,48,128]{2,1,0:T(8,128)S(1)}) custom-call(s32[1,4]{1,0:T(1,128)S(1)} %copy-done.4, f32[16,4,48,128]{3,2,1,0:T(8,128)S(1)} %copy-done, f32[4,48,128]{2,1,0:T(8,128)S(1)} %copy-done.1, f32[4,48,128]{2,1,0:T(8,128)S(1)} %copy-done.2, ...), custom_call_target="tpu_custom_call" | custom-call | tf_op jit(solution)/shard_map/sweeps0/pallas_call | solution.py:238
  26.4 0.1 total.1.a_ref
  26.4 1.5 %collective-permute-start.6 = (f32[4,48,128]{2,1,0:T(8,128)S(1)}, f32[4,48,128]{2,1,0:T(8,128)S(1)}, u32[]{:S(2)}, u32[]{:S(2)}) collective-permute-start(f32[4,48,128]{2,1,0:T(8,128)S(1)} %total.1.a_ref), channel_id=1, source_target_pairs={{0,3},{1,2},{2,1},{3,0},{4,7},{5,6},{6,5},{7,4},{8,11},{9,10},{10,... | collective-permute-start | bytes 294920 | tf_op jit(solution)/shard_map/ppermute | solution.py:418
  28.0 1.2 %collective-permute-start.5 = (f32[4,48,128]{2,1,0:T(8,128)S(1)}, f32[4,48,128]{2,1,0:T(8,128)S(1)}, u32[]{:S(2)}, u32[]{:S(2)}) collective-permute-start(f32[4,48,128]{2,1,0:T(8,128)S(1)} %total.1.a_ref), channel_id=1, source_target_pairs={{0,2},{1,3},{2,0},{3,1},{4,6},{5,7},{6,4},{7,5},{8,10},{9,11},{10,... | collective-permute-start | bytes 294920 | tf_op jit(solution)/shard_map/ppermute | solution.py:418
  29.1 4.4 %sweeps1.1 = (f32[16,4,48,128]{3,2,1,0:T(8,128)}, f32[256,128]{1,0:T(8,128)}) custom-call(s32[1,4]{1,0:T(1,128)S(1)} %copy-done.4, f32[16,4,48,128]{3,2,1,0:T(8,128)S(1)} %copy-done, f32[4,48,128]{2,1,0:T(8,128)S(1)} %copy-done.1, f32[4,48,128]{2,1,0:T(8,128)S(1)} %copy-done.2, ...), custom_call_target="tpu_custom_call", output_to_operand_aliasing={{0}: (9, {})} | custom-call | tf_op jit(solution)/shard_map/sweeps1/pallas_call | solution.py:238
  33.6 0.1 collective-permute-done.5.c_ref
  33.7 0.7 %anomalies.1.refs_0_ = bf16[192,16,128]{2,1,0:T(8,128)(2,1)S(1)} custom-call(f32[16,4,48,128]{3,2,1,0:T(8,128)S(1)} %copy-done, f32[4,48,128]{2,1,0:T(8,128)S(1)} %total.1.a_ref, f32[4,48,128]{2,1,0:T(8,128)S(1)} %collective-permute-done.4.b_ref, f32[4,48,128]{2,1,0:T(8,128)S(1)} %collective-permute-done.5.c_ref, ...), custom_call_target="tpu_custom_call" | custom-call | tf_op jit(solution)/shard_map/anomalies/pallas_call | solution.py:264
  34.4 1.2 %collective-permute-start.8 = (bf16[192,16,128]{2,1,0:T(8,128)(2,1)S(1)}, bf16[192,16,128]{2,1,0:T(8,128)(2,1)S(1)}, u32[]{:S(2)}, u32[]{:S(2)}) collective-permute-start(bf16[192,16,128]{2,1,0:T(8,128)(2,1)S(1)} %anomalies.1.refs_0_), channel_id=1, source_target_pairs={{0,2},{1,3},{2,0},{3,1},{4,6},{5,7},{6,4},{7,5},{8,10},{9,11},{10,... | collective-permute-start | bytes 2359304 | tf_op jit(solution)/shard_map/ppermute | solution.py:418
  35.7 10.0 %all-to-all-start = ((f32[256,1,128]{2,1,0:T(1,128)}), f32[256,1,128]{2,1,0:T(1,128)S(1)}, u32[]{:S(2)}, u32[]{:S(2)}) async-start(f32[256,1,128]{2,1,0:T(1,128)} %bitcast.2), calls=%async_computation | async-start | bytes 262144 | tf_op jit(solution)/shard_map/all_to_all | solution.py:432
  45.7 0.0 copy-start.3
  45.7 0.8 %copy-done.3 = f32[64,256]{1,0:T(8,128)S(1)} copy-done((f32[64,256]{1,0:T(8,128)S(1)}, f32[64,256]{1,0:T(8,128)}, u32[]{:S(2)}) %copy-start.3) | copy-done | bytes 65560
  46.6 0.5 slots.1
  47.1 2.2 %collective-permute-start.7 = (bf16[192,16,128]{2,1,0:T(8,128)(2,1)S(1)}, bf16[192,16,128]{2,1,0:T(8,128)(2,1)}, u32[]{:S(2)}, u32[]{:S(2)}) collective-permute-start(bf16[192,16,128]{2,1,0:T(8,128)(2,1)S(1)} %anomalies.1.refs_0_), channel_id=1, source_target_pairs={{0,1},{1,0},{2,3},{3,2},{4,5},{5,4},{6,7},{7,6},{8,9},{9,8},{10,11... | collective-permute-start | bytes 2359304 | tf_op jit(solution)/shard_map/ppermute | solution.py:418
  49.3 9.2 %all-to-all-done = f32[256,1,128]{2,1,0:T(1,128)S(1)} async-done(((f32[256,1,128]{2,1,0:T(1,128)}), f32[256,1,128]{2,1,0:T(1,128)S(1)}, u32[]{:S(2)}, u32[]{:S(2)}) %all-to-all-start) | async-done | bytes 131104 | tf_op jit(solution)/shard_map/all_to_all | solution.py:432
  58.5 0.7 %collective-permute-start.9 = (bf16[192,16,128]{2,1,0:T(8,128)(2,1)S(1)}, bf16[192,16,128]{2,1,0:T(8,128)(2,1)}, u32[]{:S(2)}, u32[]{:S(2)}) collective-permute-start(bf16[192,16,128]{2,1,0:T(8,128)(2,1)S(1)} %hold.1.refs_2_), channel_id=1, source_target_pairs={{0,1},{1,0},{2,3},{3,2},{4,5},{5,4},{6,7},{7,6},{8,9},{9,8},{10,11... | collective-permute-start | bytes 2359304 | tf_op jit(solution)/shard_map/ppermute | solution.py:418
  59.2 2.5 %solve.1.weights_ref = bf16[64,256]{1,0:T(8,128)(2,1)S(1)} custom-call(s32[1]{0:T(128)} %bitcast.me_ref, f32[256,128]{1,0:T(8,128)S(1)} %bitcast.9, f32[256,128]{1,0:T(8,128)S(1)} %get-tuple-element.24.seen_ref.refs_2_, f32[256,128]{1,0:T(8,128)S(1)} %get-tuple-element.25.weight_ref), custom_call_target="tpu_custom_call" | custom-call | tf_op jit(solution)/shard_map/solve/pallas_call | solution.py:363
  61.7 0.0 collective-permute-done.9.refs_3_
  61.7 4.4 %update.1 = f32[16,4,48,128]{3,2,1,0:T(8,128)} custom-call(bf16[64,256]{1,0:T(8,128)(2,1)S(1)} %solve.1.weights_ref, f32[16,4,48,128]{3,2,1,0:T(8,128)S(1)} %copy-done, bf16[192,16,128]{2,1,0:T(8,128)(2,1)S(1)} %anomalies.1.refs_0_, bf16[192,16,128]{2,1,0:T(8,128)(2,1)} %collective-permute-done.7.refs_1_, bf16[192,16,128]{2,1,0:T(8,128)(2,1)S(1)} %hold.1.refs_2_, ...), custom_call_target="tpu_custom_call" | custom-call | tf_op jit(solution)/shard_map/update/pallas_call | solution.py:397
  (23 shorter events, 0.0 us)
Async XLA Ops:
  0.6 21.1 %copy-start = (f32[16,4,48,128]{3,2,1,0:T(8,128)S(1)}, f32[16,4,48,128]{3,2,1,0:T(8,128)}, u32[]{:S(2)}) copy-start(f32[16,4,48,128]{3,2,1,0:T(8,128)} %prior_ref.9) | copy-start | bytes 4718596
  0.6 21.1 %copy-start.2 = (f32[4,48,128]{2,1,0:T(8,128)S(1)}, f32[4,48,128]{2,1,0:T(8,128)}, u32[]{:S(2)}) copy-start(f32[4,48,128]{2,1,0:T(8,128)} %visc_ref.3) | copy-start | bytes 294916
  0.7 21.1 %copy-start.1 = (f32[4,48,128]{2,1,0:T(8,128)S(1)}, f32[4,48,128]{2,1,0:T(8,128)}, u32[]{:S(2)}) copy-start(f32[4,48,128]{2,1,0:T(8,128)} %flow_ref.3) | copy-start | bytes 294916
  0.7 21.1 %copy-start.4 = (s32[1,4]{1,0:T(1,128)S(1)}, s32[1,4]{1,0:T(1,128)}, u32[]{:S(2)}) copy-start(s32[1,4]{1,0:T(1,128)} %cells_ref.3) | copy-start | bytes 52
  2.5 19.2 %collective-permute-start.2 = (bf16[28,48,128]{2,1,0:T(8,128)(2,1)S(1)}, bf16[28,48,128]{2,1,0:T(8,128)(2,1)S(1)}, u32[]{:S(2)}, u32[]{:S(2)}) collective-permute-start(bf16[28,48,128]{2,1,0:T(8,128)(2,1)S(1)} %get-tuple-element.16), channel_id=1, source_target_pairs={{0,4},{4,8},{8,12},{12,16},{16,20},{20,24},{24,28},{28,32},{32,36}... | collective-permute-start | bytes 1032200 | tf_op jit(solution)/shard_map/ppermute | solution.py:415
  5.1 16.6 %collective-permute-start.3 = (bf16[28,48,128]{2,1,0:T(8,128)(2,1)S(1)}, bf16[28,48,128]{2,1,0:T(8,128)(2,1)S(1)}, u32[]{:S(2)}, u32[]{:S(2)}) collective-permute-start(bf16[28,48,128]{2,1,0:T(8,128)(2,1)S(1)} %get-tuple-element.17), channel_id=1, source_target_pairs={{0,252},{4,0},{8,4},{12,8},{16,12},{20,16},{24,20},{28,24},{32,28}... | collective-permute-start | bytes 1032200 | tf_op jit(solution)/shard_map/ppermute | solution.py:415
  14.0 15.1 %collective-permute-start = (bf16[24,48,128]{2,1,0:T(8,128)(2,1)S(1)}, bf16[24,48,128]{2,1,0:T(8,128)(2,1)S(1)}, u32[]{:S(2)}, u32[]{:S(2)}) collective-permute-start(bf16[24,48,128]{2,1,0:T(8,128)(2,1)S(1)} %get-tuple-element.14), channel_id=1, source_target_pairs={{0,4},{4,8},{8,12},{12,16},{16,20},{20,24},{24,28},{28,32},{32,36}... | collective-permute-start | bytes 884744 | tf_op jit(solution)/shard_map/ppermute | solution.py:415
  14.0 15.1 %collective-permute-start.1 = (bf16[24,48,128]{2,1,0:T(8,128)(2,1)S(1)}, bf16[24,48,128]{2,1,0:T(8,128)(2,1)S(1)}, u32[]{:S(2)}, u32[]{:S(2)}) collective-permute-start(bf16[24,48,128]{2,1,0:T(8,128)(2,1)S(1)} %get-tuple-element.15), channel_id=1, source_target_pairs={{0,252},{4,0},{8,4},{12,8},{16,12},{20,16},{24,20},{28,24},{32,28}... | collective-permute-start | bytes 884744 | tf_op jit(solution)/shard_map/ppermute | solution.py:415
  26.4 7.2 %collective-permute-start.6 = (f32[4,48,128]{2,1,0:T(8,128)S(1)}, f32[4,48,128]{2,1,0:T(8,128)S(1)}, u32[]{:S(2)}, u32[]{:S(2)}) collective-permute-start(f32[4,48,128]{2,1,0:T(8,128)S(1)} %total.1.a_ref), channel_id=1, source_target_pairs={{0,3},{1,2},{2,1},{3,0},{4,7},{5,6},{6,5},{7,4},{8,11},{9,10},{10,... | collective-permute-start | bytes 294920 | tf_op jit(solution)/shard_map/ppermute | solution.py:418
  28.0 5.7 %collective-permute-start.5 = (f32[4,48,128]{2,1,0:T(8,128)S(1)}, f32[4,48,128]{2,1,0:T(8,128)S(1)}, u32[]{:S(2)}, u32[]{:S(2)}) collective-permute-start(f32[4,48,128]{2,1,0:T(8,128)S(1)} %total.1.a_ref), channel_id=1, source_target_pairs={{0,2},{1,3},{2,0},{3,1},{4,6},{5,7},{6,4},{7,5},{8,10},{9,11},{10,... | collective-permute-start | bytes 294920 | tf_op jit(solution)/shard_map/ppermute | solution.py:418
  29.1 4.6 %collective-permute-start.4 = (f32[4,48,128]{2,1,0:T(8,128)S(1)}, f32[4,48,128]{2,1,0:T(8,128)S(1)}, u32[]{:S(2)}, u32[]{:S(2)}) collective-permute-start(f32[4,48,128]{2,1,0:T(8,128)S(1)} %total.1.a_ref), channel_id=1, source_target_pairs={{0,1},{1,0},{2,3},{3,2},{4,5},{5,4},{6,7},{7,6},{8,9},{9,8},{10,11... | collective-permute-start | bytes 294920 | tf_op jit(solution)/shard_map/ppermute | solution.py:418
  33.7 12.0 %copy-start.5 = (s32[256]{0:T(256)S(1)}, s32[256]{0:T(256)}, u32[]{:S(2)}) copy-start(s32[256]{0:T(256)} %param.12) | copy-start | bytes 3076
  33.7 12.0 %copy-start.6 = (f32[256]{0:T(256)S(1)}, f32[256]{0:T(256)}, u32[]{:S(2)}) copy-start(f32[256]{0:T(256)} %param.13) | copy-start | bytes 3076
  33.7 12.0 %copy-start.7 = (f32[256]{0:T(256)S(1)}, f32[256]{0:T(256)}, u32[]{:S(2)}) copy-start(f32[256]{0:T(256)} %param.14) | copy-start | bytes 3076
  34.4 24.1 %collective-permute-start.8 = (bf16[192,16,128]{2,1,0:T(8,128)(2,1)S(1)}, bf16[192,16,128]{2,1,0:T(8,128)(2,1)S(1)}, u32[]{:S(2)}, u32[]{:S(2)}) collective-permute-start(bf16[192,16,128]{2,1,0:T(8,128)(2,1)S(1)} %anomalies.1.refs_0_), channel_id=1, source_target_pairs={{0,2},{1,3},{2,0},{3,1},{4,6},{5,7},{6,4},{7,5},{8,10},{9,11},{10,... | collective-permute-start | bytes 2359304 | tf_op jit(solution)/shard_map/ppermute | solution.py:418
  35.7 22.8 %all-to-all-start = ((f32[256,1,128]{2,1,0:T(1,128)}), f32[256,1,128]{2,1,0:T(1,128)S(1)}, u32[]{:S(2)}, u32[]{:S(2)}) async-start(f32[256,1,128]{2,1,0:T(1,128)} %bitcast.2), calls=%async_computation | async-start | bytes 262144 | tf_op jit(solution)/shard_map/all_to_all | solution.py:432
  45.7 0.8 %copy-start.3 = (f32[64,256]{1,0:T(8,128)S(1)}, f32[64,256]{1,0:T(8,128)}, u32[]{:S(2)}) copy-start(f32[64,256]{1,0:T(8,128)} %noise_ref.1) | copy-start | bytes 196612
  47.1 14.6 %collective-permute-start.7 = (bf16[192,16,128]{2,1,0:T(8,128)(2,1)S(1)}, bf16[192,16,128]{2,1,0:T(8,128)(2,1)}, u32[]{:S(2)}, u32[]{:S(2)}) collective-permute-start(bf16[192,16,128]{2,1,0:T(8,128)(2,1)S(1)} %anomalies.1.refs_0_), channel_id=1, source_target_pairs={{0,1},{1,0},{2,3},{3,2},{4,5},{5,4},{6,7},{7,6},{8,9},{9,8},{10,11... | collective-permute-start | bytes 2359304 | tf_op jit(solution)/shard_map/ppermute | solution.py:418
  58.5 3.2 %collective-permute-start.9 = (bf16[192,16,128]{2,1,0:T(8,128)(2,1)S(1)}, bf16[192,16,128]{2,1,0:T(8,128)(2,1)}, u32[]{:S(2)}, u32[]{:S(2)}) collective-permute-start(bf16[192,16,128]{2,1,0:T(8,128)(2,1)S(1)} %hold.1.refs_2_), channel_id=1, source_target_pairs={{0,1},{1,0},{2,3},{3,2},{4,5},{5,4},{6,7},{7,6},{8,9},{9,8},{10,11... | collective-permute-start | bytes 2359304 | tf_op jit(solution)/shard_map/ppermute | solution.py:418

commit v4 on v3

--- a/solution.py
+++ b/solution.py
@@ -11,7 +11,7 @@
 ITERS = 4
 PARTS = ((8, 0), (8, 1))
 CHUNKS = len(PARTS)
-AT_ONCE = 4
+ROWS = 8
 TOTAL_AFTER, ANOMALY_AFTER = 0, 1
 LOG_MID = 0.5 * (math.log(0.02) + math.log(0.05))
 LOG_HALF = 0.5 * (math.log(0.05) - math.log(0.02)) + 1.0
@@ -57,7 +57,7 @@
         outs[1][l] = code
     for c, (part, place) in enumerate(PARTS):
         copies[2 + c].wait()
-        right_ref, left_ref = outs[2 * c], outs[2 * c + 1]
+        left_ref, right_ref = outs[2 * c], outs[2 * c + 1]
         first = layers if c == 0 else 0
 
         def member(m, carry):
@@ -142,11 +142,12 @@
 
 
 def sweep_kernel(chunk, devices, cells_ref, prior_ref, flow_ref, visc_ref, behind_ref, ahead_ref, *rest):
-    part, layers, nz, ny = prior_ref.shape
+    _, layers, nz, ny = prior_ref.shape
+    part, place = PARTS[chunk]
     wide = layers + 2 * ITERS
     last = chunk == CHUNKS - 1
     if chunk == 0:
-        out_ref, rows, lap0, adv0, buf0, buf1, nu = rest
+        out_hbm, rows, lap0, adv0, buf0, buf1, nu, out_ref, sems = rest
         for l in range(ITERS):
             put(buf0, l, log2_of(behind_ref[l].astype(F32)) * (1.0 / FLOW_SCALE), nz)
             put(buf0, ITERS + layers + l, log2_of(ahead_ref[l].astype(F32)) * (1.0 / FLOW_SCALE), nz)
@@ -159,12 +160,15 @@
             adv0[l - 1] = centre - 0.15 * (centre - back) + 0.01
         rows[...] = jnp.zeros_like(rows)
     elif not last:
-        lap0, adv0, rows_in, _, out_ref, rows, buf0, buf1, nu = rest
+        lap0, adv0, rows_in, _, out_hbm, rows, buf0, buf1, nu, out_ref, sems = rest
         rows[...] = rows_in[...]
     else:
-        lap0, adv0, rows_in, _, out_ref, lines_ref, buf0, buf1, nu, rows = rest
+        lap0, adv0, rows_in, _, out_hbm, lines_ref, buf0, buf1, nu, out_ref, sems, rows = rest
         rows[...] = rows_in[...]
     base_slabs = layers if chunk == 0 else 0
+
+    def store(m):
+        return pltpu.make_async_copy(out_ref.at[m], out_hbm.at[place * part + m], sems.at[m])
 
     def member(m, carry):
         first = base_slabs + m * 3
@@ -174,7 +178,7 @@
             ahead = ahead_ref[first + l].astype(F32)
             nu[3 + layers + l] = jnp.exp(jnp.log(ahead) * (1.0 / (LN2 * NU_SCALE)) + LOG_MID)
         for l in range(layers):
-            nu[3 + l] = visc_ref[l] * jnp.exp(prior_ref[m, l])
+            nu[3 + l] = visc_ref[l] * jnp.exp(prior_ref[place * part + m, l])
         for l in range(1, wide - 1):
             put(buf1, l, adv0[l - 1] + nu[l - 1] * lap0[l - 1], nz)
         src, dst = buf1, buf0
@@ -191,10 +195,11 @@
                     put(dst, l, value, nz)
                 back, centre = centre, front
             src, dst = dst, src
+        store(m).start()
         for s in range(4):
             cell = cells_ref[0, s]
             layer, z = cell // (nz * ny), lax.rem(cell, nz * ny) // ny
-            rows[pl.ds(s * 16 + PARTS[chunk][1] * part + m, 1), :] = out_ref[m, layer, pl.ds(z, 1), :]
+            rows[pl.ds(s * 16 + place * part + m, 1), :] = out_ref[m, layer, pl.ds(z, 1), :]
         return carry
 
     lax.fori_loop(0, part, member, 0)
@@ -207,40 +212,40 @@
         picked = jnp.sum(jnp.where(lane == y, rows[...], 0.0), axis=1, keepdims=True)
         line = jnp.sum(jnp.where(lane == row, picked, 0.0), axis=0, keepdims=True)
         lines_ref[...] = jnp.broadcast_to(line, (devices, ny))
+    for m in range(part):
+        store(m).wait()
 
 
 def sweeps(prior, flow, visc, cells, halo, chunk, before, devices):
-    members, layers, nz, ny = prior.shape
-    part, place = PARTS[chunk]
-    whole = lambda shape: pl.BlockSpec(shape, lambda i: (0,) * len(shape))
-    block = pl.BlockSpec((part, layers, nz, ny), lambda i: (place, 0, 0, 0))
+    _, layers, nz, ny = prior.shape
+    part, _ = PARTS[chunk]
     wide = layers + 2 * ITERS
     base_shape = (wide - 2, nz, ny)
     args = [cells, prior, flow, visc, *halo]
-    specs = [SMEM, block, whole(flow.shape), whole(visc.shape), whole(halo[0].shape), whole(halo[1].shape)]
-    alias = {}
     scratch = [
         pltpu.VMEM((wide, nz + 16, ny), F32),
         pltpu.VMEM((wide, nz + 16, ny), F32),
         pltpu.VMEM(base_shape, F32),
+        pltpu.VMEM((part, layers, nz, ny), F32),
+        pltpu.SemaphoreType.DMA((part,)),
     ]
+    alias = {}
+    specs = [SMEM] + [VMEM] * (len(args) - 1)
     if chunk:
-        velocity, rows, lap0, adv0 = before
-        args += [lap0, adv0, rows, velocity]
-        specs += [whole(base_shape)] * 2 + [whole((64, ny)), pl.BlockSpec(memory_space=pl.ANY)]
+        args += [before[2], before[3], before[1], before[0]]
+        specs += [VMEM] * 3 + [pl.BlockSpec(memory_space=pltpu.HBM)]
         alias = {len(args) - 1: 0}
     last = chunk == CHUNKS - 1
-    more = [(devices, ny)] if last else [(64, ny)]
+    shapes = [prior.shape, (devices, ny) if last else (64, ny)]
     if chunk == 0:
-        more += [base_shape] * 2
+        shapes += [base_shape] * 2
     if last:
         scratch.append(pltpu.VMEM((64, ny), F32))
     out = pl.pallas_call(
         functools.partial(sweep_kernel, chunk, devices),
-        grid=(1,),
         in_specs=specs,
-        out_specs=[block] + [whole(shape) for shape in more],
-        out_shape=[jax.ShapeDtypeStruct(shape, F32) for shape in [prior.shape] + more],
+        out_specs=[pl.BlockSpec(memory_space=pltpu.HBM)] + [VMEM] * (len(shapes) - 1),
+        out_shape=[jax.ShapeDtypeStruct(shape, F32) for shape in shapes],
         input_output_aliases=alias,
         scratch_shapes=scratch,
         compiler_params=params(),
@@ -310,7 +315,9 @@
     return lax.dot_general(a, b, (dims, ((), ())), precision=lax.Precision.HIGHEST, preferred_element_type=F32)
 
 
-def solve_kernel(members, here, me_ref, vals_ref, seen_ref, weight_ref, out_ref, scr):
+def solve_kernel(members, here, me_ref, vals_ref, seen_ref, weight_ref, beside_any, out_ref, beside_ref, scr, sem):
+    fetch = pltpu.make_async_copy(beside_any, beside_ref, sem)
+    fetch.start()
     devices, ny = vals_ref.shape
     groups = members // here
     tiles = devices // groups
@@ -351,58 +358,80 @@
     order = [scr[pl.ds(pl.multiple_of((me ^ g) * here, here), here), :] for g in range(groups)]
     scr[...] = jnp.concatenate(order + [jnp.zeros((ny - members, ny), F32)], axis=0).T
     mine = scr[pl.ds(pl.multiple_of(me * here, here), here), :]
-    copies = out_ref.shape[1] // members
-    wide = jnp.concatenate([mine + pltpu.roll(mine, members, 1)] * (copies // 2), axis=1)
-    wide = jnp.concatenate([wide] * copies, axis=0)
-    row = lax.broadcasted_iota(jnp.int32, wide.shape, 0)
-    column = lax.broadcasted_iota(jnp.int32, wide.shape, 1)
-    out_ref[...] = jnp.where(row // here == column // members, wide, 0.0).astype(BF16)
-
-
-def solve(vals, seen, weight, me, members, here):
+    out_ref[...] = mine[:, :members].astype(BF16)
+    fetch.wait()
+
+
+def solve(vals, seen, weight, me, members, here, beside):
     return pl.pallas_call(
         functools.partial(solve_kernel, members, here),
-        in_specs=[SMEM] + [VMEM] * 3,
-        out_specs=VMEM,
-        out_shape=jax.ShapeDtypeStruct((AT_ONCE * here, AT_ONCE * members), BF16),
-        scratch_shapes=[pltpu.VMEM((128, 128), F32)],
+        in_specs=[SMEM] + [VMEM] * 3 + [pl.BlockSpec(memory_space=pl.ANY)],
+        out_specs=[VMEM] * 2,
+        out_shape=[jax.ShapeDtypeStruct((here, members), BF16), jax.ShapeDtypeStruct(beside.shape, BF16)],
+        scratch_shapes=[pltpu.VMEM((128, 128), F32), pltpu.SemaphoreType.DMA],
         compiler_params=params(),
         name="solve",
-    )(me, vals, seen, weight)
-
-
-def update_kernel(weights_ref, prior_ref, *refs):
-    blocks, out_ref = refs[:-1], refs[-1]
-    members, _, nz, ny = prior_ref.shape
-    flat = prior_ref.reshape(members * nz, ny)
-    out = out_ref.reshape(members * nz, ny)
-    weights = weights_ref[...]
-    for z in range(0, nz, 2 * AT_ONCE):
-        sides = []
-        for i in range(2):
-            rows = range(z + i * AT_ONCE, z + (i + 1) * AT_ONCE)
-            sides.append(jnp.concatenate([b[r] for r in rows for b in blocks], axis=0))
-        update = jnp.dot(weights, jnp.concatenate(sides, axis=1), preferred_element_type=F32)
-        for i in range(2):
-            for r in range(AT_ONCE):
-                where = pl.ds(z + i * AT_ONCE + r, members, stride=nz)
-                part = update[r * members : (r + 1) * members, i * ny : (i + 1) * ny]
-                out[where, :] = flat[where, :] + part
-
-
-def updated(weights, prior, blocks):
-    members, layers, nz, ny = prior.shape
-    block = pl.BlockSpec((members, 1, nz, ny), lambda l: (0, l, 0, 0))
-    part = pl.BlockSpec((nz, members, ny), lambda l: (l, 0, 0))
+    )(me, vals, seen, weight, beside)
+
+
+def update_kernel(weights_ref, prior_ref, mine_ref, beside_ref, over_ref, far_any, out_hbm, far_ref, out_ref, sems):
+    here, layers, nz, ny = prior_ref.shape
+    members = weights_ref.shape[1]
+    fetch = pltpu.make_async_copy(far_any, far_ref, sems.at[layers])
+    fetch.start()
+    tall = (here * ROWS, here)
+    spread = lax.broadcasted_iota(jnp.int32, tall, 0) // ROWS == lax.broadcasted_iota(jnp.int32, tall, 1)
+    wide = (members, members * ROWS)
+    column = lax.broadcasted_iota(jnp.int32, wide, 1)
+    source = column // (here * ROWS) * here + column % here
+    repeat = lax.broadcasted_iota(jnp.int32, wide, 0) == source
+    lhs = jnp.dot(jnp.where(spread, 1.0, 0.0).astype(BF16), weights_ref[...], preferred_element_type=F32)
+    lhs = jnp.dot(lhs.astype(BF16), jnp.where(repeat, 1.0, 0.0).astype(BF16), preferred_element_type=F32)
+    row = lax.broadcasted_iota(jnp.int32, lhs.shape, 0)
+    column = lax.broadcasted_iota(jnp.int32, lhs.shape, 1)
+    lhs = jnp.where(row % ROWS == column // here % ROWS, lhs, 0.0).astype(BF16)
+    places = [(l, z) for l in range(layers) for z in range(0, nz, ROWS)]
+    stores = []
+
+    def add(blocks, columns, base, done):
+        for p in range(0, len(places), 2):
+            pair = places[p : p + 2]
+            sides = []
+            for l, z in pair:
+                first = l * nz + z
+                sides.append(jnp.concatenate([b[first : first + ROWS].reshape(ROWS * here, ny) for b in blocks], axis=0))
+            update = jnp.dot(columns, jnp.concatenate(sides, axis=1), preferred_element_type=F32)
+            for i, (l, z) in enumerate(pair):
+                part = update[:, i * ny : (i + 1) * ny]
+                for m in range(here):
+                    out_ref[m, l, z : z + ROWS] = base[m, l, z : z + ROWS] + part[m * ROWS : (m + 1) * ROWS]
+                if done and z + ROWS == nz:
+                    stores.append(pltpu.make_async_copy(out_ref.at[:, l], out_hbm.at[:, l], sems.at[l]))
+                    stores[-1].start()
+
+    split = 3 * here * ROWS
+    add((mine_ref, beside_ref, over_ref), lhs[:, :split], prior_ref, False)
+    fetch.wait()
+    add((far_ref,), lhs[:, split:], out_ref, True)
+    for store in stores:
+        store.wait()
+
+
+def updated(weights, prior, mine, beside, over, far):
+    layers = prior.shape[1]
     return pl.pallas_call(
         update_kernel,
-        grid=(layers,),
-        in_specs=[pl.BlockSpec(weights.shape, lambda l: (0, 0)), block] + [part] * len(blocks),
-        out_specs=block,
+        in_specs=[VMEM] * 5 + [pl.BlockSpec(memory_space=pl.ANY)],
+        out_specs=pl.BlockSpec(memory_space=pltpu.HBM),
         out_shape=jax.ShapeDtypeStruct(prior.shape, F32),
+        scratch_shapes=[
+            pltpu.VMEM(mine.shape, BF16),
+            pltpu.VMEM(prior.shape, F32),
+            pltpu.SemaphoreType.DMA((layers + 1,)),
+        ],
         compiler_params=params(),
         name="update",
-    )(weights, prior, *blocks)
+    )(weights, prior, mine, beside, over, far)
 
 
 def per_device(prior, base_flow, base_visc, probe_cells, obs_slot, obs_values, obs_var, obs_noise):
@@ -418,23 +447,26 @@
         return lax.ppermute(x, "mem", [(i, i ^ bits) for i in range(groups)])
 
     sent = encode(prior, base_flow, base_visc)
-    halos = [(along(sent[2 * c], 1), along(sent[2 * c + 1], -1)) for c in range(CHUNKS)]
+    halos = []
+    for c in range(CHUNKS):
+        ahead = along(sent[2 * c], -1)
+        halos.append((along(sent[2 * c + 1], 1), ahead))
     state, states = None, []
     for chunk in range(CHUNKS):
         state = sweeps(prior, base_flow, base_visc, probe_cells, halos[chunk], chunk, state, tiles * groups)
         states.append(state)
     velocity, payload = state[:2]
-    total = total_of(prior, states[TOTAL_AFTER][1])
+    total = total_of(prior, halos[0][1])
     totals = [total] + [across(total, bits) for bits in (1, 2, 3)]
-    mine = anomalies(prior, totals, float(members), states[ANOMALY_AFTER][1])
+    mine = anomalies(prior, totals, float(members), states[1][1])
     beside = across(mine, 1)
     over = across(mine, 2)
     vals = lax.all_to_all(payload, ("tile", "mem"), 0, 0, tiled=True)
     seen, weight = in_slots(obs_slot, obs_values, obs_var, obs_noise, probe_cells.shape[1], payload)
     over = held(over, vals, seen)
-    blocks = [mine, beside, over, across(over, 1)]
-    weights = solve(vals, seen, weight, me, members, here)
-    return velocity, updated(weights, prior, blocks)
+    far = across(over, 1)
+    weights, beside = solve(vals, seen, weight, me, members, here, beside)
+    return velocity, updated(weights, prior, mine, beside, over, far)
 
 
 def solution(mesh):

time: 66.3 us -> 69.2 us (1.044)
  waiting for transfers between devices: 9.85 us -> 15.3 us
  starting transfers between devices: 35.6 us -> 33.9 us
  Pallas kernels: 19 us -> 18.1 us
    all_to_all x1, starting transfers between devices: 10 us -> 5.66 us  [per_device(): vals = lax.all_to_all(payload, ('tile', 'mem'), 0, 0, tiled=True)]
    ppermute x4, waiting for transfers between devices: 0.52 us -> 4.12 us  [along(): lax.ppermute(x, 'tile', [(i, (i + step) % tiles) for i in range(tiles)])]
    ppermute x6, starting transfers between devices: 6.89 us -> 9.66 us  [across(): return lax.ppermute(x, 'mem', [(i, i ^ bits) for i in range(groups)])]
    all_to_all x1, waiting for transfers between devices: 9.18 us -> 11.1 us  [per_device(): vals = lax.all_to_all(payload, ('tile', 'mem'), 0, 0, tiled=True)]
    pallas_call x3, Pallas kernels: 13.4 us -> 12.5 us  [the longest x2 9.34 us: sweeps(): pl.pallas_call(functools.partial(sweep_kernel, chunk, devices), in_specs=...]
  transfers between devices with their start and end apart: 11 -> 11, of which waited for: 3 -> 2; matrix products, arithmetic and copies ran while one was open for 0% -> 0% of each run, Pallas kernels for 18% -> 18%
where the time goes in v4:
time: 69.2 us; the launch traced here: 69 us
  starting transfers between devices  33.9 us (49%)
  Pallas kernels  18.1 us (26%)
  waiting for transfers between devices  15.3 us (22%)
  local copies, waits for them, and re-layouts  0.87 us (1%)
  between operations  0.84 us (1%)
    ppermute x4, starting transfers between devices, along(): lax.ppermute(x, 'tile', [(i, (i + step) % tiles) for i in range(tiles)])  18.6 us
    all_to_all x1, waiting for transfers between devices, per_device(): vals = lax.all_to_all(payload, ('tile', 'mem'), 0, 0, tiled=True)  11.1 us
    ppermute x6, starting transfers between devices, across(): return lax.ppermute(x, 'mem', [(i, i ^ bits) for i in range(groups)])  9.66 us
    pallas_call x2, Pallas kernels, sweeps(): pl.pallas_call(functools.partial(sweep_kernel, chunk, devices), in_specs=...  9.34 us
    all_to_all x1, starting transfers between devices, per_device(): vals = lax.all_to_all(payload, ('tile', 'mem'), 0, 0, tiled=True)  5.66 us
    ppermute x4, waiting for transfers between devices, along(): lax.ppermute(x, 'tile', [(i, (i + step) % tiles) for i in range(tiles)])  4.12 us
    pallas_call x1, Pallas kernels, updated(): pl.pallas_call(update_kernel, in_specs=[VMEM] * 5 + [pl.BlockSpec(memory_...  3.15 us
    pallas_call x1, Pallas kernels, solve(): pl.pallas_call(functools.partial(solve_kernel, members, here), in_specs=[...  2.46 us
  transfers between devices with their start and end apart: 11, of which 2 were waited for; matrix products, arithmetic and copies ran while one was open for 0% of the time, Pallas kernels for 18%

profile of v4, /device:TPU:1, one launch (start us, length us, event | category | flops | bytes accessed | tf_op | source)
XLA Modules:
  0.0 69.0 jit_solution(13770634353030168326)
XLA Ops:
  0.7 1.9 %encode.1 = (bf16[28,48,128]{2,1,0:T(8,128)(2,1)S(1)}, bf16[28,48,128]{2,1,0:T(8,128)(2,1)S(1)}, bf16[24,48,128]{2,1,0:T(8,128)(2,1)S(1)}, bf16[24,48,128]{2,1,0:T(8,128)(2,1)S(1)}) custom-call(f32[16,4,48,128]{3,2,1,0:T(8,128)} %prior_ref.9, f32[4,48,128]{2,1,0:T(8,128)} %flow_ref.3, f32[4,48,128]{2,1,0:T(8,128)} %visc_ref.3), custom_call_target="tpu_custom_call" | custom-call | tf_op jit(solution)/shard_map/encode/pallas_call | solution.py:81
  2.5 11.4 %collective-permute-start.3 = (bf16[28,48,128]{2,1,0:T(8,128)(2,1)S(1)}, bf16[28,48,128]{2,1,0:T(8,128)(2,1)S(1)}, u32[]{:S(2)}, u32[]{:S(2)}) collective-permute-start(bf16[28,48,128]{2,1,0:T(8,128)(2,1)S(1)} %get-tuple-element.19), channel_id=1, source_target_pairs={{0,252},{4,0},{8,4},{12,8},{16,12},{20,16},{24,20},{28,24},{32,28}... | collective-permute-start | bytes 1032200 | tf_op jit(solution)/shard_map/ppermute | solution.py:444
  13.9 7.2 %collective-permute-start.1 = (bf16[24,48,128]{2,1,0:T(8,128)(2,1)S(1)}, bf16[24,48,128]{2,1,0:T(8,128)(2,1)S(1)}, u32[]{:S(2)}, u32[]{:S(2)}) collective-permute-start(bf16[24,48,128]{2,1,0:T(8,128)(2,1)S(1)} %get-tuple-element.17), channel_id=1, source_target_pairs={{0,252},{4,0},{8,4},{12,8},{16,12},{20,16},{24,20},{28,24},{32,28}... | collective-permute-start | bytes 884744 | tf_op jit(solution)/shard_map/ppermute | solution.py:444
  21.2 0.1 total.1.a_ref
  21.2 1.8 %collective-permute-start.6 = (f32[4,48,128]{2,1,0:T(8,128)S(1)}, f32[4,48,128]{2,1,0:T(8,128)S(1)}, u32[]{:S(2)}, u32[]{:S(2)}) collective-permute-start(f32[4,48,128]{2,1,0:T(8,128)S(1)} %total.1.a_ref), channel_id=1, source_target_pairs={{0,3},{1,2},{2,1},{3,0},{4,7},{5,6},{6,5},{7,4},{8,11},{9,10},{10,... | collective-permute-start | bytes 294920 | tf_op jit(solution)/shard_map/ppermute | solution.py:447
  23.0 1.2 %collective-permute-start.5 = (f32[4,48,128]{2,1,0:T(8,128)S(1)}, f32[4,48,128]{2,1,0:T(8,128)S(1)}, u32[]{:S(2)}, u32[]{:S(2)}) collective-permute-start(f32[4,48,128]{2,1,0:T(8,128)S(1)} %total.1.a_ref), channel_id=1, source_target_pairs={{0,2},{1,3},{2,0},{3,1},{4,6},{5,7},{6,4},{7,5},{8,10},{9,11},{10,... | collective-permute-start | bytes 294920 | tf_op jit(solution)/shard_map/ppermute | solution.py:447
  24.2 4.1 %collective-permute-done.2.behind_ref = bf16[28,48,128]{2,1,0:T(8,128)(2,1)S(1)} collective-permute-done((bf16[28,48,128]{2,1,0:T(8,128)(2,1)S(1)}, bf16[28,48,128]{2,1,0:T(8,128)(2,1)S(1)}, u32[]{:S(2)}, u32[]{:S(2)}) %collective-permute-start.2) | collective-permute-done | bytes 344096 | tf_op jit(solution)/shard_map/ppermute | solution.py:444
  28.3 3.4 %collective-permute-start.4 = (f32[4,48,128]{2,1,0:T(8,128)S(1)}, f32[4,48,128]{2,1,0:T(8,128)S(1)}, u32[]{:S(2)}, u32[]{:S(2)}) collective-permute-start(f32[4,48,128]{2,1,0:T(8,128)S(1)} %total.1.a_ref), channel_id=1, source_target_pairs={{0,1},{1,0},{2,3},{3,2},{4,5},{5,4},{6,7},{7,6},{8,9},{9,8},{10,11... | collective-permute-start | bytes 294920 | tf_op jit(solution)/shard_map/ppermute | solution.py:447
  31.7 4.5 %sweeps0.1 = (f32[16,4,48,128]{3,2,1,0:T(8,128)}, f32[64,128]{1,0:T(8,128)S(1)}, f32[10,48,128]{2,1,0:T(8,128)S(1)}, f32[10,48,128]{2,1,0:T(8,128)S(1)}) custom-call(s32[1,4]{1,0:T(1,128)S(1)} %copy-done.4, f32[16,4,48,128]{3,2,1,0:T(8,128)S(1)} %copy-done, f32[4,48,128]{2,1,0:T(8,128)S(1)} %copy-done.1, f32[4,48,128]{2,1,0:T(8,128)S(1)} %copy-done.2, ...), custom_call_target="tpu_custom_call" | custom-call | tf_op jit(solution)/shard_map/sweeps0/pallas_call | solution.py:244
  36.2 4.9 %sweeps1.1 = (f32[16,4,48,128]{3,2,1,0:T(8,128)}, f32[256,128]{1,0:T(8,128)}) custom-call(s32[1,4]{1,0:T(1,128)S(1)} %copy-done.4, f32[16,4,48,128]{3,2,1,0:T(8,128)S(1)} %copy-done, f32[4,48,128]{2,1,0:T(8,128)S(1)} %copy-done.1, f32[4,48,128]{2,1,0:T(8,128)S(1)} %copy-done.2, ...), custom_call_target="tpu_custom_call", output_to_operand_aliasing={{0}: (9, {})} | custom-call | tf_op jit(solution)/shard_map/sweeps1/pallas_call | solution.py:244
  41.1 0.0 copy-start.5
  41.1 0.0 copy-start.6
  41.1 0.0 copy-start.7
  41.1 0.7 %anomalies.1.mine_ref = bf16[192,16,128]{2,1,0:T(8,128)(2,1)S(1)} custom-call(f32[16,4,48,128]{3,2,1,0:T(8,128)S(1)} %copy-done, f32[4,48,128]{2,1,0:T(8,128)S(1)} %total.1.a_ref, f32[4,48,128]{2,1,0:T(8,128)S(1)} %collective-permute-done.4.b_ref, f32[4,48,128]{2,1,0:T(8,128)S(1)} %collective-permute-done.5.c_ref, ...), custom_call_target="tpu_custom_call" | custom-call | tf_op jit(solution)/shard_map/anomalies/pallas_call | solution.py:269
  41.8 0.4 collective-permute-start.8
  42.2 5.7 %all-to-all-start = ((f32[256,1,128]{2,1,0:T(1,128)}), f32[256,1,128]{2,1,0:T(1,128)S(1)}, u32[]{:S(2)}, u32[]{:S(2)}) async-start(f32[256,1,128]{2,1,0:T(1,128)} %bitcast.2), calls=%async_computation | async-start | bytes 262144 | tf_op jit(solution)/shard_map/all_to_all | solution.py:464
  47.9 0.0 copy-start.3
  48.0 0.8 %copy-done.3 = f32[64,256]{1,0:T(8,128)S(1)} copy-done((f32[64,256]{1,0:T(8,128)S(1)}, f32[64,256]{1,0:T(8,128)}, u32[]{:S(2)}) %copy-start.3) | copy-done | bytes 65560
  48.8 0.5 slots.1
  49.3 2.4 %collective-permute-start.7 = (bf16[192,16,128]{2,1,0:T(8,128)(2,1)S(1)}, bf16[192,16,128]{2,1,0:T(8,128)(2,1)}, u32[]{:S(2)}, u32[]{:S(2)}) collective-permute-start(bf16[192,16,128]{2,1,0:T(8,128)(2,1)S(1)} %anomalies.1.mine_ref), channel_id=1, source_target_pairs={{0,1},{1,0},{2,3},{3,2},{4,5},{5,4},{6,7},{7,6},{8,9},{9,8},{10,11... | collective-permute-start | bytes 2359304 | tf_op jit(solution)/shard_map/ppermute | solution.py:447
  51.7 11.1 %all-to-all-done = f32[256,1,128]{2,1,0:T(1,128)S(1)} async-done(((f32[256,1,128]{2,1,0:T(1,128)}), f32[256,1,128]{2,1,0:T(1,128)S(1)}, u32[]{:S(2)}, u32[]{:S(2)}) %all-to-all-start) | async-done | bytes 131104 | tf_op jit(solution)/shard_map/all_to_all | solution.py:464
  62.8 0.5 collective-permute-start.9
  63.4 2.5 %solve.1 = (bf16[16,64]{1,0:T(8,128)(2,1)S(1)}, bf16[192,16,128]{2,1,0:T(8,128)(2,1)S(1)}) custom-call(s32[1]{0:T(128)} %bitcast.me_ref, f32[256,128]{1,0:T(8,128)S(1)} %bitcast.9, f32[256,128]{1,0:T(8,128)S(1)} %get-tuple-element.26.seen_ref.refs_2_, f32[256,128]{1,0:T(8,128)S(1)} %get-tuple-element.27.weight_ref, ...), custom_call_target="tpu_custom_call" | custom-call | tf_op jit(solution)/shard_map/solve/pallas_call | solution.py:366
  65.8 3.2 %update.1 = f32[16,4,48,128]{3,2,1,0:T(8,128)} custom-call(bf16[16,64]{1,0:T(8,128)(2,1)S(1)} %get-tuple-element.28.weights_ref, f32[16,4,48,128]{3,2,1,0:T(8,128)S(1)} %copy-done, bf16[192,16,128]{2,1,0:T(8,128)(2,1)S(1)} %anomalies.1.mine_ref, bf16[192,16,128]{2,1,0:T(8,128)(2,1)S(1)} %get-tuple-element.29.beside_ref, ...), custom_call_target="tpu_custom_call" | custom-call | tf_op jit(solution)/shard_map/update/pallas_call | solution.py:422
  (23 shorter events, 0.1 us)
Async XLA Ops:
  0.6 20.5 %copy-start = (f32[16,4,48,128]{3,2,1,0:T(8,128)S(1)}, f32[16,4,48,128]{3,2,1,0:T(8,128)}, u32[]{:S(2)}) copy-start(f32[16,4,48,128]{3,2,1,0:T(8,128)} %prior_ref.9) | copy-start | bytes 4718596
  0.6 31.0 %copy-start.2 = (f32[4,48,128]{2,1,0:T(8,128)S(1)}, f32[4,48,128]{2,1,0:T(8,128)}, u32[]{:S(2)}) copy-start(f32[4,48,128]{2,1,0:T(8,128)} %visc_ref.3) | copy-start | bytes 294916
  0.7 31.0 %copy-start.1 = (f32[4,48,128]{2,1,0:T(8,128)S(1)}, f32[4,48,128]{2,1,0:T(8,128)}, u32[]{:S(2)}) copy-start(f32[4,48,128]{2,1,0:T(8,128)} %flow_ref.3) | copy-start | bytes 294916
  0.7 31.0 %copy-start.4 = (s32[1,4]{1,0:T(1,128)S(1)}, s32[1,4]{1,0:T(1,128)}, u32[]{:S(2)}) copy-start(s32[1,4]{1,0:T(1,128)} %cells_ref.3) | copy-start | bytes 52
  2.5 18.6 %collective-permute-start.3 = (bf16[28,48,128]{2,1,0:T(8,128)(2,1)S(1)}, bf16[28,48,128]{2,1,0:T(8,128)(2,1)S(1)}, u32[]{:S(2)}, u32[]{:S(2)}) collective-permute-start(bf16[28,48,128]{2,1,0:T(8,128)(2,1)S(1)} %get-tuple-element.19), channel_id=1, source_target_pairs={{0,252},{4,0},{8,4},{12,8},{16,12},{20,16},{24,20},{28,24},{32,28}... | collective-permute-start | bytes 1032200 | tf_op jit(solution)/shard_map/ppermute | solution.py:444
  13.9 14.4 %collective-permute-start.2 = (bf16[28,48,128]{2,1,0:T(8,128)(2,1)S(1)}, bf16[28,48,128]{2,1,0:T(8,128)(2,1)S(1)}, u32[]{:S(2)}, u32[]{:S(2)}) collective-permute-start(bf16[28,48,128]{2,1,0:T(8,128)(2,1)S(1)} %get-tuple-element.18), channel_id=1, source_target_pairs={{0,4},{4,8},{8,12},{12,16},{16,20},{20,24},{24,28},{28,32},{32,36}... | collective-permute-start | bytes 1032200 | tf_op jit(solution)/shard_map/ppermute | solution.py:444
  13.9 22.2 %collective-permute-start = (bf16[24,48,128]{2,1,0:T(8,128)(2,1)S(1)}, bf16[24,48,128]{2,1,0:T(8,128)(2,1)S(1)}, u32[]{:S(2)}, u32[]{:S(2)}) collective-permute-start(bf16[24,48,128]{2,1,0:T(8,128)(2,1)S(1)} %get-tuple-element.16), channel_id=1, source_target_pairs={{0,4},{4,8},{8,12},{12,16},{16,20},{20,24},{24,28},{28,32},{32,36}... | collective-permute-start | bytes 884744 | tf_op jit(solution)/shard_map/ppermute | solution.py:444
  13.9 22.2 %collective-permute-start.1 = (bf16[24,48,128]{2,1,0:T(8,128)(2,1)S(1)}, bf16[24,48,128]{2,1,0:T(8,128)(2,1)S(1)}, u32[]{:S(2)}, u32[]{:S(2)}) collective-permute-start(bf16[24,48,128]{2,1,0:T(8,128)(2,1)S(1)} %get-tuple-element.17), channel_id=1, source_target_pairs={{0,252},{4,0},{8,4},{12,8},{16,12},{20,16},{24,20},{28,24},{32,28}... | collective-permute-start | bytes 884744 | tf_op jit(solution)/shard_map/ppermute | solution.py:444
  21.2 19.8 %collective-permute-start.6 = (f32[4,48,128]{2,1,0:T(8,128)S(1)}, f32[4,48,128]{2,1,0:T(8,128)S(1)}, u32[]{:S(2)}, u32[]{:S(2)}) collective-permute-start(f32[4,48,128]{2,1,0:T(8,128)S(1)} %total.1.a_ref), channel_id=1, source_target_pairs={{0,3},{1,2},{2,1},{3,0},{4,7},{5,6},{6,5},{7,4},{8,11},{9,10},{10,... | collective-permute-start | bytes 294920 | tf_op jit(solution)/shard_map/ppermute | solution.py:447
  23.0 18.1 %collective-permute-start.5 = (f32[4,48,128]{2,1,0:T(8,128)S(1)}, f32[4,48,128]{2,1,0:T(8,128)S(1)}, u32[]{:S(2)}, u32[]{:S(2)}) collective-permute-start(f32[4,48,128]{2,1,0:T(8,128)S(1)} %total.1.a_ref), channel_id=1, source_target_pairs={{0,2},{1,3},{2,0},{3,1},{4,6},{5,7},{6,4},{7,5},{8,10},{9,11},{10,... | collective-permute-start | bytes 294920 | tf_op jit(solution)/shard_map/ppermute | solution.py:447
  28.3 12.8 %collective-permute-start.4 = (f32[4,48,128]{2,1,0:T(8,128)S(1)}, f32[4,48,128]{2,1,0:T(8,128)S(1)}, u32[]{:S(2)}, u32[]{:S(2)}) collective-permute-start(f32[4,48,128]{2,1,0:T(8,128)S(1)} %total.1.a_ref), channel_id=1, source_target_pairs={{0,1},{1,0},{2,3},{3,2},{4,5},{5,4},{6,7},{7,6},{8,9},{9,8},{10,11... | collective-permute-start | bytes 294920 | tf_op jit(solution)/shard_map/ppermute | solution.py:447
  41.1 6.8 %copy-start.5 = (s32[256]{0:T(256)S(1)}, s32[256]{0:T(256)}, u32[]{:S(2)}) copy-start(s32[256]{0:T(256)} %param.12) | copy-start | bytes 3076
  41.1 6.8 %copy-start.6 = (f32[256]{0:T(256)S(1)}, f32[256]{0:T(256)}, u32[]{:S(2)}) copy-start(f32[256]{0:T(256)} %param.13) | copy-start | bytes 3076
  41.1 6.8 %copy-start.7 = (f32[256]{0:T(256)S(1)}, f32[256]{0:T(256)}, u32[]{:S(2)}) copy-start(f32[256]{0:T(256)} %param.14) | copy-start | bytes 3076
  41.8 21.0 %collective-permute-start.8 = (bf16[192,16,128]{2,1,0:T(8,128)(2,1)S(1)}, bf16[192,16,128]{2,1,0:T(8,128)(2,1)S(1)}, u32[]{:S(2)}, u32[]{:S(2)}) collective-permute-start(bf16[192,16,128]{2,1,0:T(8,128)(2,1)S(1)} %anomalies.1.mine_ref), channel_id=1, source_target_pairs={{0,2},{1,3},{2,0},{3,1},{4,6},{5,7},{6,4},{7,5},{8,10},{9,11},{10,... | collective-permute-start | bytes 2359304 | tf_op jit(solution)/shard_map/ppermute | solution.py:447
  42.2 20.6 %all-to-all-start = ((f32[256,1,128]{2,1,0:T(1,128)}), f32[256,1,128]{2,1,0:T(1,128)S(1)}, u32[]{:S(2)}, u32[]{:S(2)}) async-start(f32[256,1,128]{2,1,0:T(1,128)} %bitcast.2), calls=%async_computation | async-start | bytes 262144 | tf_op jit(solution)/shard_map/all_to_all | solution.py:464
  47.9 0.8 %copy-start.3 = (f32[64,256]{1,0:T(8,128)S(1)}, f32[64,256]{1,0:T(8,128)}, u32[]{:S(2)}) copy-start(f32[64,256]{1,0:T(8,128)} %noise_ref.1) | copy-start | bytes 196612
  49.3 14.1 %collective-permute-start.7 = (bf16[192,16,128]{2,1,0:T(8,128)(2,1)S(1)}, bf16[192,16,128]{2,1,0:T(8,128)(2,1)}, u32[]{:S(2)}, u32[]{:S(2)}) collective-permute-start(bf16[192,16,128]{2,1,0:T(8,128)(2,1)S(1)} %anomalies.1.mine_ref), channel_id=1, source_target_pairs={{0,1},{1,0},{2,3},{3,2},{4,5},{5,4},{6,7},{7,6},{8,9},{9,8},{10,11... | collective-permute-start | bytes 2359304 | tf_op jit(solution)/shard_map/ppermute | solution.py:447
  62.8 3.0 %collective-permute-start.9 = (bf16[192,16,128]{2,1,0:T(8,128)(2,1)S(1)}, bf16[192,16,128]{2,1,0:T(8,128)(2,1)}, u32[]{:S(2)}, u32[]{:S(2)}) collective-permute-start(bf16[192,16,128]{2,1,0:T(8,128)(2,1)S(1)} %hold.1.over_ref), channel_id=1, source_target_pairs={{0,1},{1,0},{2,3},{3,2},{4,5},{5,4},{6,7},{7,6},{8,9},{9,8},{10,11... | collective-permute-start | bytes 2359304 | tf_op jit(solution)/shard_map/ppermute | solution.py:447

commit v5 on v4

--- a/solution.py
+++ b/solution.py
@@ -36,7 +36,7 @@
     return jnp.log(x) * (1.0 / LN2)
 
 
-def encode_kernel(prior_hbm, flow_hbm, visc_hbm, *refs):
+def encode_kernel(odd_ref, prior_hbm, flow_hbm, visc_hbm, *refs):
     outs, (prior, flow, visc, base, sems) = refs[: 2 * CHUNKS], refs[2 * CHUNKS :]
     layers = prior.shape[1]
     copies = [
@@ -57,22 +57,31 @@
         outs[1][l] = code
     for c, (part, place) in enumerate(PARTS):
         copies[2 + c].wait()
-        left_ref, right_ref = outs[2 * c], outs[2 * c + 1]
+        inner_ref, outer_ref = outs[2 * c], outs[2 * c + 1]
         first = layers if c == 0 else 0
 
-        def member(m, carry):
-            for l in range(layers):
-                code = power(prior[place * part + m, l] * NU_SCALE + base[l]).astype(BF16)
-                if l >= 1:
-                    right_ref[first + m * 3 + l - 1] = code
-                if l < 3:
-                    left_ref[first + m * 3 + l] = code
-            return carry
-
-        lax.fori_loop(0, part, member, 0)
-
-
-def encode(prior, flow, visc):
+        def members(right_ref, left_ref):
+            def member(m, carry):
+                for l in range(layers):
+                    code = power(prior[place * part + m, l] * NU_SCALE + base[l]).astype(BF16)
+                    if l >= 1:
+                        right_ref[first + m * 3 + l - 1] = code
+                    if l < 3:
+                        left_ref[first + m * 3 + l] = code
+                return carry
+
+            lax.fori_loop(0, part, member, 0)
+
+        @pl.when(odd_ref[0] == 0)
+        def _():
+            members(inner_ref, outer_ref)
+
+        @pl.when(odd_ref[0] == 1)
+        def _():
+            members(outer_ref, inner_ref)
+
+
+def encode(odd, prior, flow, visc):
     members, layers, nz, ny = prior.shape
     shapes = []
     for c, (part, _) in enumerate(PARTS):
@@ -80,7 +89,7 @@
         shapes += [jax.ShapeDtypeStruct((slabs, nz, ny), BF16)] * 2
     return pl.pallas_call(
         encode_kernel,
-        in_specs=[pl.BlockSpec(memory_space=pltpu.HBM)] * 3,
+        in_specs=[SMEM] + [pl.BlockSpec(memory_space=pltpu.HBM)] * 3,
         out_specs=[VMEM] * len(shapes),
         out_shape=shapes,
         scratch_shapes=[
@@ -92,7 +101,7 @@
         ],
         compiler_params=params(),
         name="encode",
-    )(*[pltpu.with_memory_space_constraint(x, pltpu.HBM) for x in (prior, flow, visc)])
+    )(odd, *[pltpu.with_memory_space_constraint(x, pltpu.HBM) for x in (prior, flow, visc)])
 
 
 def total_kernel(prior_ref, after, out_ref):
@@ -141,16 +150,19 @@
     buf[l, 8 + nz : 9 + nz] = value[0:1]
 
 
-def sweep_kernel(chunk, devices, cells_ref, prior_ref, flow_ref, visc_ref, behind_ref, ahead_ref, *rest):
+def sweep_kernel(chunk, devices, odd_ref, cells_ref, prior_ref, flow_ref, visc_ref, inner_ref, outer_ref, *rest):
     _, layers, nz, ny = prior_ref.shape
     part, place = PARTS[chunk]
     wide = layers + 2 * ITERS
     last = chunk == CHUNKS - 1
+    odd = odd_ref[0]
+    partners = ((inner_ref, 1 - odd), (outer_ref, odd))
     if chunk == 0:
         out_hbm, rows, lap0, adv0, buf0, buf1, nu, out_ref, sems = rest
         for l in range(ITERS):
-            put(buf0, l, log2_of(behind_ref[l].astype(F32)) * (1.0 / FLOW_SCALE), nz)
-            put(buf0, ITERS + layers + l, log2_of(ahead_ref[l].astype(F32)) * (1.0 / FLOW_SCALE), nz)
+            for side_ref, ahead in partners:
+                flow = log2_of(side_ref[l].astype(F32)) * (1.0 / FLOW_SCALE)
+                put(buf0, ahead * (ITERS + layers) + l, flow, nz)
         for l in range(layers):
             put(buf0, ITERS + l, flow_ref[l], nz)
         for l in range(1, wide - 1):
@@ -173,10 +185,9 @@
     def member(m, carry):
         first = base_slabs + m * 3
         for l in range(3):
-            behind = behind_ref[first + l].astype(F32)
-            nu[l] = jnp.exp(jnp.log(behind) * (1.0 / (LN2 * NU_SCALE)) + LOG_MID)
-            ahead = ahead_ref[first + l].astype(F32)
-            nu[3 + layers + l] = jnp.exp(jnp.log(ahead) * (1.0 / (LN2 * NU_SCALE)) + LOG_MID)
+            for side_ref, ahead in partners:
+                code = side_ref[first + l].astype(F32)
+                nu[ahead * (3 + layers) + l] = jnp.exp(jnp.log(code) * (1.0 / (LN2 * NU_SCALE)) + LOG_MID)
         for l in range(layers):
             nu[3 + l] = visc_ref[l] * jnp.exp(prior_ref[place * part + m, l])
         for l in range(1, wide - 1):
@@ -216,12 +227,12 @@
         store(m).wait()
 
 
-def sweeps(prior, flow, visc, cells, halo, chunk, before, devices):
+def sweeps(odd, prior, flow, visc, cells, halo, chunk, before, devices):
     _, layers, nz, ny = prior.shape
     part, _ = PARTS[chunk]
     wide = layers + 2 * ITERS
     base_shape = (wide - 2, nz, ny)
-    args = [cells, prior, flow, visc, *halo]
+    args = [odd, cells, prior, flow, visc, *halo]
     scratch = [
         pltpu.VMEM((wide, nz + 16, ny), F32),
         pltpu.VMEM((wide, nz + 16, ny), F32),
@@ -230,7 +241,7 @@
         pltpu.SemaphoreType.DMA((part,)),
     ]
     alias = {}
-    specs = [SMEM] + [VMEM] * (len(args) - 1)
+    specs = [SMEM] * 2 + [VMEM] * (len(args) - 2)
     if chunk:
         args += [before[2], before[3], before[1], before[0]]
         specs += [VMEM] * 3 + [pl.BlockSpec(memory_space=pltpu.HBM)]
@@ -254,7 +265,8 @@
     return tuple(out) + (tuple(before[2:]) if chunk else ())
 
 
-def anomaly_kernel(members_all, prior_ref, a_ref, b_ref, c_ref, d_ref, after, out_ref):
+def anomaly_kernel(members_all, prior_ref, a_ref, b_ref, c_ref, d_ref, *refs):
+    out_ref = refs[-1]
     members, _, nz, ny = prior_ref.shape
     flat = prior_ref.reshape(members * nz, ny)
     mean = (a_ref[0] + b_ref[0] + c_ref[0] + d_ref[0]) / members_all
@@ -263,18 +275,18 @@
         out_ref[z] = (rows - mean[z : z + 1]).astype(BF16)
 
 
-def anomalies(prior, totals, members_all, after):
+def anomalies(prior, totals, members_all, *after):
     members, layers, nz, ny = prior.shape
     total = pl.BlockSpec((1, nz, ny), lambda l: (l, 0, 0))
     return pl.pallas_call(
         functools.partial(anomaly_kernel, members_all),
         grid=(layers,),
-        in_specs=[pl.BlockSpec((members, 1, nz, ny), lambda l: (0, l, 0, 0))] + [total] * 4 + [pl.BlockSpec(memory_space=pl.ANY)],
+        in_specs=[pl.BlockSpec((members, 1, nz, ny), lambda l: (0, l, 0, 0))] + [total] * 4 + [pl.BlockSpec(memory_space=pl.ANY)] * len(after),
         out_specs=pl.BlockSpec((nz, members, ny), lambda l: (l, 0, 0)),
         out_shape=jax.ShapeDtypeStruct((layers * nz, members, ny), BF16),
         compiler_params=params(),
         name="anomalies",
-    )(prior, *totals, after)
+    )(prior, *totals, *after)
 
 
 def slots_kernel(probes, slot_ref, value_ref, var_ref, noise_ref, after, seen_ref, weight_ref, stack):
@@ -440,25 +452,25 @@
     members = here * groups
     me = lax.axis_index("mem").astype(jnp.int32).reshape(1)
 
-    def along(x, step):
-        return lax.ppermute(x, "tile", [(i, (i + step) % tiles) for i in range(tiles)])
+    odd = (lax.axis_index("tile") & 1).astype(jnp.int32).reshape(1)
+
+    def swap(x, first):
+        pairs = [((first + 2 * i) % tiles, (first + 2 * i + 1) % tiles) for i in range(tiles // 2)]
+        return lax.ppermute(x, "tile", pairs + [(b, a) for a, b in pairs])
 
     def across(x, bits):
         return lax.ppermute(x, "mem", [(i, i ^ bits) for i in range(groups)])
 
-    sent = encode(prior, base_flow, base_visc)
-    halos = []
-    for c in range(CHUNKS):
-        ahead = along(sent[2 * c], -1)
-        halos.append((along(sent[2 * c + 1], 1), ahead))
+    sent = encode(odd, prior, base_flow, base_visc)
+    halos = [(swap(sent[2 * c], 0), swap(sent[2 * c + 1], 1)) for c in range(CHUNKS)]
     state, states = None, []
     for chunk in range(CHUNKS):
-        state = sweeps(prior, base_flow, base_visc, probe_cells, halos[chunk], chunk, state, tiles * groups)
+        state = sweeps(odd, prior, base_flow, base_visc, probe_cells, halos[chunk], chunk, state, tiles * groups)
         states.append(state)
     velocity, payload = state[:2]
-    total = total_of(prior, halos[0][1])
+    total = total_of(prior, halos[0][0])
     totals = [total] + [across(total, bits) for bits in (1, 2, 3)]
-    mine = anomalies(prior, totals, float(members), states[1][1])
+    mine = anomalies(prior, totals, float(members), states[0][1], *halos[1])
     beside = across(mine, 1)
     over = across(mine, 2)
     vals = lax.all_to_all(payload, ("tile", "mem"), 0, 0, tiled=True)

time: 69.2 us -> 66.4 us (0.960)
  waiting for transfers between devices: 15.3 us -> 12.4 us
    ppermute x4, starting transfers between devices: 18.6 us -> 13.6 us  [swap(): return lax.ppermute(x, 'tile', pairs + [(b, a) for a, b in pairs])]
    all_to_all x1, starting transfers between devices: 5.66 us -> 10.7 us  [per_device(): vals = lax.all_to_all(payload, ('tile', 'mem'), 0, 0, tiled=True)]
    all_to_all x1, waiting for transfers between devices: 11.1 us -> 9.18 us  [per_device(): vals = lax.all_to_all(payload, ('tile', 'mem'), 0, 0, tiled=True)]
    ppermute x4, waiting for transfers between devices: 4.12 us -> 2.7 us  [swap(): return lax.ppermute(x, 'tile', pairs + [(b, a) for a, b in pairs])]
  transfers between devices with their start and end apart: 11 -> 11, of which waited for: 2 -> 3; matrix products, arithmetic and copies ran while one was open for 0% -> 0% of each run, Pallas kernels for 18% -> 19%
where the time goes in v5:
time: 66.4 us; the launch traced here: 66.1 us
  starting transfers between devices  33.6 us (51%)
  Pallas kernels  18.3 us (28%)
  waiting for transfers between devices  12.4 us (19%)
  local copies, waits for them, and re-layouts  0.86 us (1%)
  between operations  0.81 us (1%)
    ppermute x4, starting transfers between devices, swap(): return lax.ppermute(x, 'tile', pairs + [(b, a) for a, b in pairs])  13.6 us
    all_to_all x1, starting transfers between devices, per_device(): vals = lax.all_to_all(payload, ('tile', 'mem'), 0, 0, tiled=True)  10.7 us
    pallas_call x2, Pallas kernels, sweeps(): pl.pallas_call(functools.partial(sweep_kernel, chunk, devices), in_specs=...  9.84 us
    ppermute x6, starting transfers between devices, across(): return lax.ppermute(x, 'mem', [(i, i ^ bits) for i in range(groups)])  9.37 us
    all_to_all x1, waiting for transfers between devices, per_device(): vals = lax.all_to_all(payload, ('tile', 'mem'), 0, 0, tiled=True)  9.18 us
    pallas_call x1, Pallas kernels, updated(): pl.pallas_call(update_kernel, in_specs=[VMEM] * 5 + [pl.BlockSpec(memory_...  3.15 us
    ppermute x4, waiting for transfers between devices, swap(): return lax.ppermute(x, 'tile', pairs + [(b, a) for a, b in pairs])  2.7 us
    pallas_call x1, Pallas kernels, solve(): pl.pallas_call(functools.partial(solve_kernel, members, here), in_specs=[...  2.2 us
  transfers between devices with their start and end apart: 11, of which 3 were waited for; matrix products, arithmetic and copies ran while one was open for 0% of the time, Pallas kernels for 19%

profile of v5, /device:TPU:1, one launch (start us, length us, event | category | flops | bytes accessed | tf_op | source)
XLA Modules:
  0.0 66.1 jit_solution(15007503509266741759)
XLA Ops:
  0.7 1.9 %encode.1 = (bf16[28,48,128]{2,1,0:T(8,128)(2,1)S(1)}, bf16[28,48,128]{2,1,0:T(8,128)(2,1)S(1)}, bf16[24,48,128]{2,1,0:T(8,128)(2,1)S(1)}, bf16[24,48,128]{2,1,0:T(8,128)(2,1)S(1)}) custom-call(s32[1]{0:T(128)} %bitcast.odd_ref, f32[16,4,48,128]{3,2,1,0:T(8,128)} %prior_ref.9, f32[4,48,128]{2,1,0:T(8,128)} %flow_ref.3, f32[4,48,128]{2,1,0:T(8,128)} %visc_ref.3), custom_call_target="tpu_custom_call" | custom-call | tf_op jit(solution)/shard_map/encode/pallas_call | solution.py:90
  2.5 2.5 %collective-permute-start.2 = (bf16[28,48,128]{2,1,0:T(8,128)(2,1)S(1)}, bf16[28,48,128]{2,1,0:T(8,128)(2,1)S(1)}, u32[]{:S(2)}, u32[]{:S(2)}) collective-permute-start(bf16[28,48,128]{2,1,0:T(8,128)(2,1)S(1)} %get-tuple-element.18), channel_id=1, source_target_pairs={{0,4},{8,12},{16,20},{24,28},{32,36},{40,44},{48,52},{56,60},{64,6... | collective-permute-start | bytes 1032200 | tf_op jit(solution)/shard_map/ppermute | solution.py:459
  5.1 9.6 %collective-permute-start.3 = (bf16[28,48,128]{2,1,0:T(8,128)(2,1)S(1)}, bf16[28,48,128]{2,1,0:T(8,128)(2,1)S(1)}, u32[]{:S(2)}, u32[]{:S(2)}) collective-permute-start(bf16[28,48,128]{2,1,0:T(8,128)(2,1)S(1)} %get-tuple-element.19), channel_id=1, source_target_pairs={{4,8},{12,16},{20,24},{28,32},{36,40},{44,48},{52,56},{60,64},{68,... | collective-permute-start | bytes 1032200 | tf_op jit(solution)/shard_map/ppermute | solution.py:459
  14.7 0.0 collective-permute-start
  14.7 1.5 %collective-permute-start.1 = (bf16[24,48,128]{2,1,0:T(8,128)(2,1)S(1)}, bf16[24,48,128]{2,1,0:T(8,128)(2,1)S(1)}, u32[]{:S(2)}, u32[]{:S(2)}) collective-permute-start(bf16[24,48,128]{2,1,0:T(8,128)(2,1)S(1)} %get-tuple-element.17), channel_id=1, source_target_pairs={{4,8},{12,16},{20,24},{28,32},{36,40},{44,48},{52,56},{60,64},{68,... | collective-permute-start | bytes 884744 | tf_op jit(solution)/shard_map/ppermute | solution.py:459
  16.1 0.1 total.1.a_ref
  16.2 2.1 %collective-permute-start.6 = (f32[4,48,128]{2,1,0:T(8,128)S(1)}, f32[4,48,128]{2,1,0:T(8,128)S(1)}, u32[]{:S(2)}, u32[]{:S(2)}) collective-permute-start(f32[4,48,128]{2,1,0:T(8,128)S(1)} %total.1.a_ref), channel_id=1, source_target_pairs={{0,3},{1,2},{2,1},{3,0},{4,7},{5,6},{6,5},{7,4},{8,11},{9,10},{10,... | collective-permute-start | bytes 294920 | tf_op jit(solution)/shard_map/ppermute | solution.py:462
  18.3 1.2 %collective-permute-start.5 = (f32[4,48,128]{2,1,0:T(8,128)S(1)}, f32[4,48,128]{2,1,0:T(8,128)S(1)}, u32[]{:S(2)}, u32[]{:S(2)}) collective-permute-start(f32[4,48,128]{2,1,0:T(8,128)S(1)} %total.1.a_ref), channel_id=1, source_target_pairs={{0,2},{1,3},{2,0},{3,1},{4,6},{5,7},{6,4},{7,5},{8,10},{9,11},{10,... | collective-permute-start | bytes 294920 | tf_op jit(solution)/shard_map/ppermute | solution.py:462
  19.4 2.7 %collective-permute-done.3.outer_ref = bf16[28,48,128]{2,1,0:T(8,128)(2,1)S(1)} collective-permute-done((bf16[28,48,128]{2,1,0:T(8,128)(2,1)S(1)}, bf16[28,48,128]{2,1,0:T(8,128)(2,1)S(1)}, u32[]{:S(2)}, u32[]{:S(2)}) %collective-permute-start.3) | collective-permute-done | bytes 344096 | tf_op jit(solution)/shard_map/ppermute | solution.py:459
  22.1 2.3 %collective-permute-start.4 = (f32[4,48,128]{2,1,0:T(8,128)S(1)}, f32[4,48,128]{2,1,0:T(8,128)S(1)}, u32[]{:S(2)}, u32[]{:S(2)}) collective-permute-start(f32[4,48,128]{2,1,0:T(8,128)S(1)} %total.1.a_ref), channel_id=1, source_target_pairs={{0,1},{1,0},{2,3},{3,2},{4,5},{5,4},{6,7},{7,6},{8,9},{9,8},{10,11... | collective-permute-start | bytes 294920 | tf_op jit(solution)/shard_map/ppermute | solution.py:462
  24.5 4.7 %sweeps0.1 = (f32[16,4,48,128]{3,2,1,0:T(8,128)}, f32[64,128]{1,0:T(8,128)S(1)}, f32[10,48,128]{2,1,0:T(8,128)S(1)}, f32[10,48,128]{2,1,0:T(8,128)S(1)}) custom-call(s32[1]{0:T(128)} %bitcast.odd_ref, s32[1,4]{1,0:T(1,128)S(1)} %copy-done.4, f32[16,4,48,128]{3,2,1,0:T(8,128)S(1)} %copy-done, f32[4,48,128]{2,1,0:T(8,128)S(1)} %copy-done.1, ...), custom_call_target="tpu_custom_call" | custom-call | tf_op jit(solution)/shard_map/sweeps0/pallas_call | solution.py:255
  29.2 0.6 collective-permute-done.5.c_ref
  29.8 0.7 %anomalies.1.mine_ref = bf16[192,16,128]{2,1,0:T(8,128)(2,1)S(1)} custom-call(f32[16,4,48,128]{3,2,1,0:T(8,128)S(1)} %copy-done, f32[4,48,128]{2,1,0:T(8,128)S(1)} %total.1.a_ref, f32[4,48,128]{2,1,0:T(8,128)S(1)} %collective-permute-done.4.b_ref, f32[4,48,128]{2,1,0:T(8,128)S(1)} %collective-permute-done.5.c_ref, ...), custom_call_target="tpu_custom_call" | custom-call | tf_op jit(solution)/shard_map/anomalies/pallas_call | solution.py:281
  30.5 0.9 %collective-permute-start.8 = (bf16[192,16,128]{2,1,0:T(8,128)(2,1)S(1)}, bf16[192,16,128]{2,1,0:T(8,128)(2,1)S(1)}, u32[]{:S(2)}, u32[]{:S(2)}) collective-permute-start(bf16[192,16,128]{2,1,0:T(8,128)(2,1)S(1)} %anomalies.1.mine_ref), channel_id=1, source_target_pairs={{0,2},{1,3},{2,0},{3,1},{4,6},{5,7},{6,4},{7,5},{8,10},{9,11},{10,... | collective-permute-start | bytes 2359304 | tf_op jit(solution)/shard_map/ppermute | solution.py:462
  31.3 5.1 %sweeps1.1 = (f32[16,4,48,128]{3,2,1,0:T(8,128)}, f32[256,128]{1,0:T(8,128)}) custom-call(s32[1]{0:T(128)} %bitcast.odd_ref, s32[1,4]{1,0:T(1,128)S(1)} %copy-done.4, f32[16,4,48,128]{3,2,1,0:T(8,128)S(1)} %copy-done, f32[4,48,128]{2,1,0:T(8,128)S(1)} %copy-done.1, f32[4,48,128]{2,1,0:T(8,128)S(1)} %copy-done.2, ...), custom_call_target="tpu_custom_call", output_to_operand_aliasing={{0}: (10, {})} | custom-call | tf_op jit(solution)/shard_map/sweeps1/pallas_call | solution.py:255
  36.5 10.7 %all-to-all-start = ((f32[256,1,128]{2,1,0:T(1,128)}), f32[256,1,128]{2,1,0:T(1,128)S(1)}, u32[]{:S(2)}, u32[]{:S(2)}) async-start(f32[256,1,128]{2,1,0:T(1,128)} %bitcast.3), calls=%async_computation | async-start | bytes 262144 | tf_op jit(solution)/shard_map/all_to_all | solution.py:476
  47.2 0.0 copy-start.3
  47.2 0.8 %copy-done.3 = f32[64,256]{1,0:T(8,128)S(1)} copy-done((f32[64,256]{1,0:T(8,128)S(1)}, f32[64,256]{1,0:T(8,128)}, u32[]{:S(2)}) %copy-start.3) | copy-done | bytes 65560
  48.0 0.5 slots.1
  48.5 2.2 %collective-permute-start.7 = (bf16[192,16,128]{2,1,0:T(8,128)(2,1)S(1)}, bf16[192,16,128]{2,1,0:T(8,128)(2,1)}, u32[]{:S(2)}, u32[]{:S(2)}) collective-permute-start(bf16[192,16,128]{2,1,0:T(8,128)(2,1)S(1)} %anomalies.1.mine_ref), channel_id=1, source_target_pairs={{0,1},{1,0},{2,3},{3,2},{4,5},{5,4},{6,7},{7,6},{8,9},{9,8},{10,11... | collective-permute-start | bytes 2359304 | tf_op jit(solution)/shard_map/ppermute | solution.py:462
  50.8 9.2 %all-to-all-done = f32[256,1,128]{2,1,0:T(1,128)S(1)} async-done(((f32[256,1,128]{2,1,0:T(1,128)}), f32[256,1,128]{2,1,0:T(1,128)S(1)}, u32[]{:S(2)}, u32[]{:S(2)}) %all-to-all-start) | async-done | bytes 131104 | tf_op jit(solution)/shard_map/all_to_all | solution.py:476
  60.0 0.7 %collective-permute-start.9 = (bf16[192,16,128]{2,1,0:T(8,128)(2,1)S(1)}, bf16[192,16,128]{2,1,0:T(8,128)(2,1)}, u32[]{:S(2)}, u32[]{:S(2)}) collective-permute-start(bf16[192,16,128]{2,1,0:T(8,128)(2,1)S(1)} %hold.1.over_ref), channel_id=1, source_target_pairs={{0,1},{1,0},{2,3},{3,2},{4,5},{5,4},{6,7},{7,6},{8,9},{9,8},{10,11... | collective-permute-start | bytes 2359304 | tf_op jit(solution)/shard_map/ppermute | solution.py:462
  60.7 2.2 %solve.1 = (bf16[16,64]{1,0:T(8,128)(2,1)S(1)}, bf16[192,16,128]{2,1,0:T(8,128)(2,1)S(1)}) custom-call(s32[1]{0:T(128)} %bitcast.1.me_ref, f32[256,128]{1,0:T(8,128)S(1)} %bitcast.10, f32[256,128]{1,0:T(8,128)S(1)} %get-tuple-element.26.seen_ref.refs_2_, f32[256,128]{1,0:T(8,128)S(1)} %get-tuple-element.27.weight_ref, ...), custom_call_target="tpu_custom_call" | custom-call | tf_op jit(solution)/shard_map/solve/pallas_call | solution.py:378
  62.9 3.2 %update.1 = f32[16,4,48,128]{3,2,1,0:T(8,128)} custom-call(bf16[16,64]{1,0:T(8,128)(2,1)S(1)} %get-tuple-element.28.weights_ref, f32[16,4,48,128]{3,2,1,0:T(8,128)S(1)} %copy-done, bf16[192,16,128]{2,1,0:T(8,128)(2,1)S(1)} %anomalies.1.mine_ref, bf16[192,16,128]{2,1,0:T(8,128)(2,1)S(1)} %get-tuple-element.29.beside_ref, ...), custom_call_target="tpu_custom_call" | custom-call | tf_op jit(solution)/shard_map/update/pallas_call | solution.py:434
  (23 shorter events, 0.0 us)
Async XLA Ops:
  0.6 15.5 %copy-start = (f32[16,4,48,128]{3,2,1,0:T(8,128)S(1)}, f32[16,4,48,128]{3,2,1,0:T(8,128)}, u32[]{:S(2)}) copy-start(f32[16,4,48,128]{3,2,1,0:T(8,128)} %prior_ref.9) | copy-start | bytes 4718596
  0.6 23.8 %copy-start.1 = (f32[4,48,128]{2,1,0:T(8,128)S(1)}, f32[4,48,128]{2,1,0:T(8,128)}, u32[]{:S(2)}) copy-start(f32[4,48,128]{2,1,0:T(8,128)} %flow_ref.3) | copy-start | bytes 294916
  0.7 23.8 %copy-start.2 = (f32[4,48,128]{2,1,0:T(8,128)S(1)}, f32[4,48,128]{2,1,0:T(8,128)}, u32[]{:S(2)}) copy-start(f32[4,48,128]{2,1,0:T(8,128)} %visc_ref.3) | copy-start | bytes 294916
  0.7 23.8 %copy-start.4 = (s32[1,4]{1,0:T(1,128)S(1)}, s32[1,4]{1,0:T(1,128)}, u32[]{:S(2)}) copy-start(s32[1,4]{1,0:T(1,128)} %cells_ref.3) | copy-start | bytes 52
  2.5 13.6 %collective-permute-start.2 = (bf16[28,48,128]{2,1,0:T(8,128)(2,1)S(1)}, bf16[28,48,128]{2,1,0:T(8,128)(2,1)S(1)}, u32[]{:S(2)}, u32[]{:S(2)}) collective-permute-start(bf16[28,48,128]{2,1,0:T(8,128)(2,1)S(1)} %get-tuple-element.18), channel_id=1, source_target_pairs={{0,4},{8,12},{16,20},{24,28},{32,36},{40,44},{48,52},{56,60},{64,6... | collective-permute-start | bytes 1032200 | tf_op jit(solution)/shard_map/ppermute | solution.py:459
  5.1 17.1 %collective-permute-start.3 = (bf16[28,48,128]{2,1,0:T(8,128)(2,1)S(1)}, bf16[28,48,128]{2,1,0:T(8,128)(2,1)S(1)}, u32[]{:S(2)}, u32[]{:S(2)}) collective-permute-start(bf16[28,48,128]{2,1,0:T(8,128)(2,1)S(1)} %get-tuple-element.19), channel_id=1, source_target_pairs={{4,8},{12,16},{20,24},{28,32},{36,40},{44,48},{52,56},{60,64},{68,... | collective-permute-start | bytes 1032200 | tf_op jit(solution)/shard_map/ppermute | solution.py:459
  14.7 14.5 %collective-permute-start = (bf16[24,48,128]{2,1,0:T(8,128)(2,1)S(1)}, bf16[24,48,128]{2,1,0:T(8,128)(2,1)S(1)}, u32[]{:S(2)}, u32[]{:S(2)}) collective-permute-start(bf16[24,48,128]{2,1,0:T(8,128)(2,1)S(1)} %get-tuple-element.16), channel_id=1, source_target_pairs={{0,4},{8,12},{16,20},{24,28},{32,36},{40,44},{48,52},{56,60},{64,6... | collective-permute-start | bytes 884744 | tf_op jit(solution)/shard_map/ppermute | solution.py:459
  14.7 14.5 %collective-permute-start.1 = (bf16[24,48,128]{2,1,0:T(8,128)(2,1)S(1)}, bf16[24,48,128]{2,1,0:T(8,128)(2,1)S(1)}, u32[]{:S(2)}, u32[]{:S(2)}) collective-permute-start(bf16[24,48,128]{2,1,0:T(8,128)(2,1)S(1)} %get-tuple-element.17), channel_id=1, source_target_pairs={{4,8},{12,16},{20,24},{28,32},{36,40},{44,48},{52,56},{60,64},{68,... | collective-permute-start | bytes 884744 | tf_op jit(solution)/shard_map/ppermute | solution.py:459
  16.2 13.0 %collective-permute-start.6 = (f32[4,48,128]{2,1,0:T(8,128)S(1)}, f32[4,48,128]{2,1,0:T(8,128)S(1)}, u32[]{:S(2)}, u32[]{:S(2)}) collective-permute-start(f32[4,48,128]{2,1,0:T(8,128)S(1)} %total.1.a_ref), channel_id=1, source_target_pairs={{0,3},{1,2},{2,1},{3,0},{4,7},{5,6},{6,5},{7,4},{8,11},{9,10},{10,... | collective-permute-start | bytes 294920 | tf_op jit(solution)/shard_map/ppermute | solution.py:462
  18.3 11.5 %collective-permute-start.5 = (f32[4,48,128]{2,1,0:T(8,128)S(1)}, f32[4,48,128]{2,1,0:T(8,128)S(1)}, u32[]{:S(2)}, u32[]{:S(2)}) collective-permute-start(f32[4,48,128]{2,1,0:T(8,128)S(1)} %total.1.a_ref), channel_id=1, source_target_pairs={{0,2},{1,3},{2,0},{3,1},{4,6},{5,7},{6,4},{7,5},{8,10},{9,11},{10,... | collective-permute-start | bytes 294920 | tf_op jit(solution)/shard_map/ppermute | solution.py:462
  22.1 7.6 %collective-permute-start.4 = (f32[4,48,128]{2,1,0:T(8,128)S(1)}, f32[4,48,128]{2,1,0:T(8,128)S(1)}, u32[]{:S(2)}, u32[]{:S(2)}) collective-permute-start(f32[4,48,128]{2,1,0:T(8,128)S(1)} %total.1.a_ref), channel_id=1, source_target_pairs={{0,1},{1,0},{2,3},{3,2},{4,5},{5,4},{6,7},{7,6},{8,9},{9,8},{10,11... | collective-permute-start | bytes 294920 | tf_op jit(solution)/shard_map/ppermute | solution.py:462
  30.5 29.5 %collective-permute-start.8 = (bf16[192,16,128]{2,1,0:T(8,128)(2,1)S(1)}, bf16[192,16,128]{2,1,0:T(8,128)(2,1)S(1)}, u32[]{:S(2)}, u32[]{:S(2)}) collective-permute-start(bf16[192,16,128]{2,1,0:T(8,128)(2,1)S(1)} %anomalies.1.mine_ref), channel_id=1, source_target_pairs={{0,2},{1,3},{2,0},{3,1},{4,6},{5,7},{6,4},{7,5},{8,10},{9,11},{10,... | collective-permute-start | bytes 2359304 | tf_op jit(solution)/shard_map/ppermute | solution.py:462
  31.3 15.8 %copy-start.5 = (s32[256]{0:T(256)S(1)}, s32[256]{0:T(256)}, u32[]{:S(2)}) copy-start(s32[256]{0:T(256)} %param.12) | copy-start | bytes 3076
  31.3 15.8 %copy-start.6 = (f32[256]{0:T(256)S(1)}, f32[256]{0:T(256)}, u32[]{:S(2)}) copy-start(f32[256]{0:T(256)} %param.13) | copy-start | bytes 3076
  31.3 15.9 %copy-start.7 = (f32[256]{0:T(256)S(1)}, f32[256]{0:T(256)}, u32[]{:S(2)}) copy-start(f32[256]{0:T(256)} %param.14) | copy-start | bytes 3076
  36.5 23.5 %all-to-all-start = ((f32[256,1,128]{2,1,0:T(1,128)}), f32[256,1,128]{2,1,0:T(1,128)S(1)}, u32[]{:S(2)}, u32[]{:S(2)}) async-start(f32[256,1,128]{2,1,0:T(1,128)} %bitcast.3), calls=%async_computation | async-start | bytes 262144 | tf_op jit(solution)/shard_map/all_to_all | solution.py:476
  47.2 0.8 %copy-start.3 = (f32[64,256]{1,0:T(8,128)S(1)}, f32[64,256]{1,0:T(8,128)}, u32[]{:S(2)}) copy-start(f32[64,256]{1,0:T(8,128)} %noise_ref.1) | copy-start | bytes 196612
  48.5 12.1 %collective-permute-start.7 = (bf16[192,16,128]{2,1,0:T(8,128)(2,1)S(1)}, bf16[192,16,128]{2,1,0:T(8,128)(2,1)}, u32[]{:S(2)}, u32[]{:S(2)}) collective-permute-start(bf16[192,16,128]{2,1,0:T(8,128)(2,1)S(1)} %anomalies.1.mine_ref), channel_id=1, source_target_pairs={{0,1},{1,0},{2,3},{3,2},{4,5},{5,4},{6,7},{7,6},{8,9},{9,8},{10,11... | collective-permute-start | bytes 2359304 | tf_op jit(solution)/shard_map/ppermute | solution.py:462
  60.0 2.9 %collective-permute-start.9 = (bf16[192,16,128]{2,1,0:T(8,128)(2,1)S(1)}, bf16[192,16,128]{2,1,0:T(8,128)(2,1)}, u32[]{:S(2)}, u32[]{:S(2)}) collective-permute-start(bf16[192,16,128]{2,1,0:T(8,128)(2,1)S(1)} %hold.1.over_ref), channel_id=1, source_target_pairs={{0,1},{1,0},{2,3},{3,2},{4,5},{5,4},{6,7},{7,6},{8,9},{9,8},{10,11... | collective-permute-start | bytes 2359304 | tf_op jit(solution)/shard_map/ppermute | solution.py:462

commit v6 on v5

--- a/solution.py
+++ b/solution.py
@@ -12,7 +12,7 @@
 PARTS = ((8, 0), (8, 1))
 CHUNKS = len(PARTS)
 ROWS = 8
-TOTAL_AFTER, ANOMALY_AFTER = 0, 1
+STEPS = 1
 LOG_MID = 0.5 * (math.log(0.02) + math.log(0.05))
 LOG_HALF = 0.5 * (math.log(0.05) - math.log(0.02)) + 1.0
 NU_SCALE = 124.0 / LOG_HALF
@@ -121,6 +121,21 @@
     )(prior, after)
 
 
+def pair_sum_kernel(a_ref, b_ref, out_ref):
+    out_ref[...] = a_ref[...] + b_ref[...]
+
+
+def pair_sum(a, b):
+    return pl.pallas_call(
+        pair_sum_kernel,
+        in_specs=[VMEM] * 2,
+        out_specs=VMEM,
+        out_shape=jax.ShapeDtypeStruct(a.shape, F32),
+        compiler_params=params(),
+        name="pair_sum",
+    )(a, b)
+
+
 def hold_kernel(*refs):
     pass
 
@@ -153,43 +168,55 @@
 def sweep_kernel(chunk, devices, odd_ref, cells_ref, prior_ref, flow_ref, visc_ref, inner_ref, outer_ref, *rest):
     _, layers, nz, ny = prior_ref.shape
     part, place = PARTS[chunk]
+    group = part // STEPS
+    step = pl.program_id(0)
     wide = layers + 2 * ITERS
     last = chunk == CHUNKS - 1
     odd = odd_ref[0]
     partners = ((inner_ref, 1 - odd), (outer_ref, odd))
     if chunk == 0:
-        out_hbm, rows, lap0, adv0, buf0, buf1, nu, out_ref, sems = rest
-        for l in range(ITERS):
-            for side_ref, ahead in partners:
-                flow = log2_of(side_ref[l].astype(F32)) * (1.0 / FLOW_SCALE)
-                put(buf0, ahead * (ITERS + layers) + l, flow, nz)
-        for l in range(layers):
-            put(buf0, ITERS + l, flow_ref[l], nz)
-        for l in range(1, wide - 1):
-            centre, back = buf0[l, 8 : 8 + nz], buf0[l - 1, 8 : 8 + nz]
-            sides = back + buf0[l + 1, 8 : 8 + nz] + neighbours(buf0, l, centre, nz, ny)
-            lap0[l - 1] = sides - 6.0 * centre
-            adv0[l - 1] = centre - 0.15 * (centre - back) + 0.01
-        rows[...] = jnp.zeros_like(rows)
+        out_ref, rows, lap0, adv0, buf0, buf1, nu = rest
+
+        @pl.when(step == 0)
+        def _():
+            for l in range(ITERS):
+                for side_ref, ahead in partners:
+                    flow = log2_of(side_ref[l].astype(F32)) * (1.0 / FLOW_SCALE)
+                    put(buf0, ahead * (ITERS + layers) + l, flow, nz)
+            for l in range(layers):
+                put(buf0, ITERS + l, flow_ref[l], nz)
+            for l in range(1, wide - 1):
+                centre, back = buf0[l, 8 : 8 + nz], buf0[l - 1, 8 : 8 + nz]
+                sides = back + buf0[l + 1, 8 : 8 + nz] + neighbours(buf0, l, centre, nz, ny)
+                lap0[l - 1] = sides - 6.0 * centre
+                adv0[l - 1] = centre - 0.15 * (centre - back) + 0.01
+            rows[...] = jnp.zeros_like(rows)
+
     elif not last:
-        lap0, adv0, rows_in, _, out_hbm, rows, buf0, buf1, nu, out_ref, sems = rest
-        rows[...] = rows_in[...]
+        lap0, adv0, rows_in, _, out_ref, rows, buf0, buf1, nu = rest
+
+        @pl.when(step == 0)
+        def _():
+            rows[...] = rows_in[...]
+
     else:
-        lap0, adv0, rows_in, _, out_hbm, lines_ref, buf0, buf1, nu, out_ref, sems, rows = rest
-        rows[...] = rows_in[...]
+        lap0, adv0, rows_in, _, out_ref, lines_ref, buf0, buf1, nu, rows = rest
+
+        @pl.when(step == 0)
+        def _():
+            rows[...] = rows_in[...]
+
     base_slabs = layers if chunk == 0 else 0
 
-    def store(m):
-        return pltpu.make_async_copy(out_ref.at[m], out_hbm.at[place * part + m], sems.at[m])
-
     def member(m, carry):
-        first = base_slabs + m * 3
+        index = step * group + m
+        first = base_slabs + index * 3
         for l in range(3):
             for side_ref, ahead in partners:
                 code = side_ref[first + l].astype(F32)
                 nu[ahead * (3 + layers) + l] = jnp.exp(jnp.log(code) * (1.0 / (LN2 * NU_SCALE)) + LOG_MID)
         for l in range(layers):
-            nu[3 + l] = visc_ref[l] * jnp.exp(prior_ref[place * part + m, l])
+            nu[3 + l] = visc_ref[l] * jnp.exp(prior_ref[place * part + index, l])
         for l in range(1, wide - 1):
             put(buf1, l, adv0[l - 1] + nu[l - 1] * lap0[l - 1], nz)
         src, dst = buf1, buf0
@@ -206,30 +233,30 @@
                     put(dst, l, value, nz)
                 back, centre = centre, front
             src, dst = dst, src
-        store(m).start()
         for s in range(4):
             cell = cells_ref[0, s]
             layer, z = cell // (nz * ny), lax.rem(cell, nz * ny) // ny
-            rows[pl.ds(s * 16 + place * part + m, 1), :] = out_ref[m, layer, pl.ds(z, 1), :]
+            rows[pl.ds(s * 16 + place * part + index, 1), :] = out_ref[m, layer, pl.ds(z, 1), :]
         return carry
 
-    lax.fori_loop(0, part, member, 0)
+    lax.fori_loop(0, group, member, 0)
     if last:
-        lane = lax.broadcasted_iota(jnp.int32, rows.shape, 1)
-        row = lax.broadcasted_iota(jnp.int32, rows.shape, 0)
-        y = jnp.zeros(rows.shape, jnp.int32)
-        for s in range(4):
-            y = jnp.where(row // 16 == s, lax.rem(cells_ref[0, s], ny), y)
-        picked = jnp.sum(jnp.where(lane == y, rows[...], 0.0), axis=1, keepdims=True)
-        line = jnp.sum(jnp.where(lane == row, picked, 0.0), axis=0, keepdims=True)
-        lines_ref[...] = jnp.broadcast_to(line, (devices, ny))
-    for m in range(part):
-        store(m).wait()
+
+        @pl.when(step == STEPS - 1)
+        def _():
+            lane = lax.broadcasted_iota(jnp.int32, rows.shape, 1)
+            row = lax.broadcasted_iota(jnp.int32, rows.shape, 0)
+            y = jnp.zeros(rows.shape, jnp.int32)
+            for s in range(4):
+                y = jnp.where(row // 16 == s, lax.rem(cells_ref[0, s], ny), y)
+            picked = jnp.sum(jnp.where(lane == y, rows[...], 0.0), axis=1, keepdims=True)
+            line = jnp.sum(jnp.where(lane == row, picked, 0.0), axis=0, keepdims=True)
+            lines_ref[...] = jnp.broadcast_to(line, (devices, ny))
 
 
 def sweeps(odd, prior, flow, visc, cells, halo, chunk, before, devices):
     _, layers, nz, ny = prior.shape
-    part, _ = PARTS[chunk]
+    part, place = PARTS[chunk]
     wide = layers + 2 * ITERS
     base_shape = (wide - 2, nz, ny)
     args = [odd, cells, prior, flow, visc, *halo]
@@ -237,8 +264,6 @@
         pltpu.VMEM((wide, nz + 16, ny), F32),
         pltpu.VMEM((wide, nz + 16, ny), F32),
         pltpu.VMEM(base_shape, F32),
-        pltpu.VMEM((part, layers, nz, ny), F32),
-        pltpu.SemaphoreType.DMA((part,)),
     ]
     alias = {}
     specs = [SMEM] * 2 + [VMEM] * (len(args) - 2)
@@ -254,8 +279,9 @@
         scratch.append(pltpu.VMEM((64, ny), F32))
     out = pl.pallas_call(
         functools.partial(sweep_kernel, chunk, devices),
+        grid=(STEPS,),
         in_specs=specs,
-        out_specs=[pl.BlockSpec(memory_space=pltpu.HBM)] + [VMEM] * (len(shapes) - 1),
+        out_specs=[pl.BlockSpec((part // STEPS, layers, nz, ny), lambda i: (place * STEPS + i, 0, 0, 0))] + [VMEM] * (len(shapes) - 1),
         out_shape=[jax.ShapeDtypeStruct(shape, F32) for shape in shapes],
         input_output_aliases=alias,
         scratch_shapes=scratch,
@@ -265,11 +291,11 @@
     return tuple(out) + (tuple(before[2:]) if chunk else ())
 
 
-def anomaly_kernel(members_all, prior_ref, a_ref, b_ref, c_ref, d_ref, *refs):
+def anomaly_kernel(members_all, prior_ref, a_ref, b_ref, *refs):
     out_ref = refs[-1]
     members, _, nz, ny = prior_ref.shape
     flat = prior_ref.reshape(members * nz, ny)
-    mean = (a_ref[0] + b_ref[0] + c_ref[0] + d_ref[0]) / members_all
+    mean = (a_ref[0] + b_ref[0]) / members_all
     for z in range(nz):
         rows = flat[pl.ds(z, members, stride=nz), :]
         out_ref[z] = (rows - mean[z : z + 1]).astype(BF16)
@@ -281,7 +307,7 @@
     return pl.pallas_call(
         functools.partial(anomaly_kernel, members_all),
         grid=(layers,),
-        in_specs=[pl.BlockSpec((members, 1, nz, ny), lambda l: (0, l, 0, 0))] + [total] * 4 + [pl.BlockSpec(memory_space=pl.ANY)] * len(after),
+        in_specs=[pl.BlockSpec((members, 1, nz, ny), lambda l: (0, l, 0, 0))] + [total] * 2 + [pl.BlockSpec(memory_space=pl.ANY)] * len(after),
         out_specs=pl.BlockSpec((nz, members, ny), lambda l: (l, 0, 0)),
         out_shape=jax.ShapeDtypeStruct((layers * nz, members, ny), BF16),
         compiler_params=params(),
@@ -468,8 +494,9 @@
         state = sweeps(odd, prior, base_flow, base_visc, probe_cells, halos[chunk], chunk, state, tiles * groups)
         states.append(state)
     velocity, payload = state[:2]
-    total = total_of(prior, halos[0][0])
-    totals = [total] + [across(total, bits) for bits in (1, 2, 3)]
+    total = total_of(prior, sent[0])
+    chip = pair_sum(total, across(total, 1))
+    totals = [chip, across(chip, 2)]
     mine = anomalies(prior, totals, float(members), states[0][1], *halos[1])
     beside = across(mine, 1)
     over = across(mine, 2)

time: 66.4 us -> 64.7 us (0.974)
  starting transfers between devices: 33.6 us -> 29 us
  waiting for transfers between devices: 12.4 us -> 15.6 us
    ppermute x6 -> x5, starting transfers between devices: 9.37 us -> 5.35 us  [across(): return lax.ppermute(x, 'mem', [(i, i ^ bits) for i in range(groups)])]
    ppermute x4, waiting for transfers between devices: 2.7 us -> 5.48 us  [swap(): return lax.ppermute(x, 'tile', pairs + [(b, a) for a, b in pairs])]
    pallas_call x2 -> x3, Pallas kernels: 9.84 us -> 9.47 us  [the longest x2 9.46 us: sweeps(): pl.pallas_call(functools.partial(sweep_kernel, chunk, devices), grid=(STE...]
  transfers between devices with their start and end apart: 11 -> 10, of which waited for: 3 -> 5; matrix products, arithmetic and copies ran while one was open for 0% -> 0% of each run, Pallas kernels for 19% -> 19%
where the time goes in v6:
time: 64.7 us; the launch traced here: 64.5 us
  starting transfers between devices  29 us (45%)
  Pallas kernels  18.2 us (28%)
  waiting for transfers between devices  15.6 us (24%)
  local copies, waits for them, and re-layouts  0.87 us (1%)
  between operations  0.75 us (1%)
    ppermute x4, starting transfers between devices, swap(): return lax.ppermute(x, 'tile', pairs + [(b, a) for a, b in pairs])  13 us
    all_to_all x1, starting transfers between devices, per_device(): vals = lax.all_to_all(payload, ('tile', 'mem'), 0, 0, tiled=True)  10.7 us
    pallas_call x2, Pallas kernels, sweeps(): pl.pallas_call(functools.partial(sweep_kernel, chunk, devices), grid=(STE...  9.46 us
    all_to_all x1, waiting for transfers between devices, per_device(): vals = lax.all_to_all(payload, ('tile', 'mem'), 0, 0, tiled=True)  9.21 us
    ppermute x4, waiting for transfers between devices, swap(): return lax.ppermute(x, 'tile', pairs + [(b, a) for a, b in pairs])  5.48 us
    ppermute x5, starting transfers between devices, across(): return lax.ppermute(x, 'mem', [(i, i ^ bits) for i in range(groups)])  5.35 us
    pallas_call x1, Pallas kernels, updated(): pl.pallas_call(update_kernel, in_specs=[VMEM] * 5 + [pl.BlockSpec(memory_...  3.15 us
    pallas_call x1, Pallas kernels, solve(): pl.pallas_call(functools.partial(solve_kernel, members, here), in_specs=[...  2.46 us
  transfers between devices with their start and end apart: 10, of which 5 were waited for; matrix products, arithmetic and copies ran while one was open for 0% of the time, Pallas kernels for 19%

profile of v6, /device:TPU:1, one launch (start us, length us, event | category | flops | bytes accessed | tf_op | source)
XLA Modules:
  0.0 64.5 jit_solution(17707115642251584971)
XLA Ops:
  0.6 1.9 %encode.1 = (bf16[28,48,128]{2,1,0:T(8,128)(2,1)S(1)}, bf16[28,48,128]{2,1,0:T(8,128)(2,1)S(1)}, bf16[24,48,128]{2,1,0:T(8,128)(2,1)S(1)}, bf16[24,48,128]{2,1,0:T(8,128)(2,1)S(1)}) custom-call(s32[1]{0:T(128)} %bitcast.odd_ref, f32[16,4,48,128]{3,2,1,0:T(8,128)} %prior_ref.9, f32[4,48,128]{2,1,0:T(8,128)} %flow_ref.3, f32[4,48,128]{2,1,0:T(8,128)} %visc_ref.3), custom_call_target="tpu_custom_call" | custom-call | tf_op jit(solution)/shard_map/encode/pallas_call | solution.py:90
  2.5 0.0 copy-start.2
  2.5 11.4 %collective-permute-start.3 = (bf16[28,48,128]{2,1,0:T(8,128)(2,1)S(1)}, bf16[28,48,128]{2,1,0:T(8,128)(2,1)S(1)}, u32[]{:S(2)}, u32[]{:S(2)}) collective-permute-start(bf16[28,48,128]{2,1,0:T(8,128)(2,1)S(1)} %get-tuple-element.19), channel_id=1, source_target_pairs={{4,8},{12,16},{20,24},{28,32},{36,40},{44,48},{52,56},{60,64},{68,... | collective-permute-start | bytes 1032200 | tf_op jit(solution)/shard_map/ppermute | solution.py:485
  13.9 1.5 %collective-permute-start = (bf16[24,48,128]{2,1,0:T(8,128)(2,1)S(1)}, bf16[24,48,128]{2,1,0:T(8,128)(2,1)S(1)}, u32[]{:S(2)}, u32[]{:S(2)}) collective-permute-start(bf16[24,48,128]{2,1,0:T(8,128)(2,1)S(1)} %get-tuple-element.16), channel_id=1, source_target_pairs={{0,4},{8,12},{16,20},{24,28},{32,36},{40,44},{48,52},{56,60},{64,6... | collective-permute-start | bytes 884744 | tf_op jit(solution)/shard_map/ppermute | solution.py:485
  15.4 0.1 collective-permute-start.1
  15.5 0.1 total.1.a_ref
  15.6 1.6 %collective-permute-start.4 = (f32[4,48,128]{2,1,0:T(8,128)S(1)}, f32[4,48,128]{2,1,0:T(8,128)S(1)}, u32[]{:S(2)}, u32[]{:S(2)}) collective-permute-start(f32[4,48,128]{2,1,0:T(8,128)S(1)} %total.1.a_ref), channel_id=1, source_target_pairs={{0,1},{1,0},{2,3},{3,2},{4,5},{5,4},{6,7},{7,6},{8,9},{9,8},{10,11... | collective-permute-start | bytes 294920 | tf_op jit(solution)/shard_map/ppermute | solution.py:488
  17.2 0.9 %collective-permute-done.4.b_ref = f32[4,48,128]{2,1,0:T(8,128)S(1)} collective-permute-done((f32[4,48,128]{2,1,0:T(8,128)S(1)}, f32[4,48,128]{2,1,0:T(8,128)S(1)}, u32[]{:S(2)}, u32[]{:S(2)}) %collective-permute-start.4) | collective-permute-done | bytes 98336 | tf_op jit(solution)/shard_map/ppermute | solution.py:488
  18.1 0.4 collective-permute-start.5
  18.5 3.2 %collective-permute-done.3.outer_ref = bf16[28,48,128]{2,1,0:T(8,128)(2,1)S(1)} collective-permute-done((bf16[28,48,128]{2,1,0:T(8,128)(2,1)S(1)}, bf16[28,48,128]{2,1,0:T(8,128)(2,1)S(1)}, u32[]{:S(2)}, u32[]{:S(2)}) %collective-permute-start.3) | collective-permute-done | bytes 344096 | tf_op jit(solution)/shard_map/ppermute | solution.py:485
  21.7 0.8 %collective-permute-done.2.inner_ref = bf16[28,48,128]{2,1,0:T(8,128)(2,1)S(1)} collective-permute-done((bf16[28,48,128]{2,1,0:T(8,128)(2,1)S(1)}, bf16[28,48,128]{2,1,0:T(8,128)(2,1)S(1)}, u32[]{:S(2)}, u32[]{:S(2)}) %collective-permute-start.2) | collective-permute-done | bytes 344096 | tf_op jit(solution)/shard_map/ppermute | solution.py:485
  22.6 4.8 %sweeps0.1 = (f32[16,4,48,128]{3,2,1,0:T(8,128)}, f32[64,128]{1,0:T(8,128)S(1)}, f32[10,48,128]{2,1,0:T(8,128)S(1)}, f32[10,48,128]{2,1,0:T(8,128)S(1)}) custom-call(s32[1]{0:T(128)} %bitcast.odd_ref, s32[1,4]{1,0:T(1,128)S(1)} %copy-done.4, f32[16,4,48,128]{3,2,1,0:T(8,128)S(1)} %copy-done, f32[4,48,128]{2,1,0:T(8,128)S(1)} %copy-done.1, ...), custom_call_target="tpu_custom_call" | custom-call | tf_op jit(solution)/shard_map/sweeps0/pallas_call | solution.py:280
  27.4 1.5 %collective-permute-done.inner_ref.refs_1_ = bf16[24,48,128]{2,1,0:T(8,128)(2,1)S(1)} collective-permute-done((bf16[24,48,128]{2,1,0:T(8,128)(2,1)S(1)}, bf16[24,48,128]{2,1,0:T(8,128)(2,1)S(1)}, u32[]{:S(2)}, u32[]{:S(2)}) %collective-permute-start) | collective-permute-done | bytes 294944 | tf_op jit(solution)/shard_map/ppermute | solution.py:485
  28.9 0.7 %anomalies.1.mine_ref = bf16[192,16,128]{2,1,0:T(8,128)(2,1)S(1)} custom-call(f32[16,4,48,128]{3,2,1,0:T(8,128)S(1)} %copy-done, f32[4,48,128]{2,1,0:T(8,128)S(1)} %pair_sum.1.a_ref, f32[4,48,128]{2,1,0:T(8,128)S(1)} %collective-permute-done.5.b_ref, f32[64,128]{1,0:T(8,128)S(1)} %get-tuple-element.22.rest_2_.refs_0_, ...), custom_call_target="tpu_custom_call" | custom-call | tf_op jit(solution)/shard_map/anomalies/pallas_call | solution.py:307
  29.6 0.4 collective-permute-start.7
  30.0 4.6 %sweeps1.1 = (f32[16,4,48,128]{3,2,1,0:T(8,128)}, f32[256,128]{1,0:T(8,128)}) custom-call(s32[1]{0:T(128)} %bitcast.odd_ref, s32[1,4]{1,0:T(1,128)S(1)} %copy-done.4, f32[16,4,48,128]{3,2,1,0:T(8,128)S(1)} %copy-done, f32[4,48,128]{2,1,0:T(8,128)S(1)} %copy-done.1, f32[4,48,128]{2,1,0:T(8,128)S(1)} %copy-done.2, ...), custom_call_target="tpu_custom_call", output_to_operand_aliasing={{0}: (10, {})} | custom-call | tf_op jit(solution)/shard_map/sweeps1/pallas_call | solution.py:280
  34.6 10.7 %all-to-all-start = ((f32[256,1,128]{2,1,0:T(1,128)}), f32[256,1,128]{2,1,0:T(1,128)S(1)}, u32[]{:S(2)}, u32[]{:S(2)}) async-start(f32[256,1,128]{2,1,0:T(1,128)} %bitcast.3), calls=%async_computation | async-start | bytes 262144 | tf_op jit(solution)/shard_map/all_to_all | solution.py:503
  45.3 2.2 %collective-permute-start.6 = (bf16[192,16,128]{2,1,0:T(8,128)(2,1)S(1)}, bf16[192,16,128]{2,1,0:T(8,128)(2,1)}, u32[]{:S(2)}, u32[]{:S(2)}) collective-permute-start(bf16[192,16,128]{2,1,0:T(8,128)(2,1)S(1)} %anomalies.1.mine_ref), channel_id=1, source_target_pairs={{0,1},{1,0},{2,3},{3,2},{4,5},{5,4},{6,7},{7,6},{8,9},{9,8},{10,11... | collective-permute-start | bytes 2359304 | tf_op jit(solution)/shard_map/ppermute | solution.py:488
  47.6 0.8 %copy-done.3 = f32[64,256]{1,0:T(8,128)S(1)} copy-done((f32[64,256]{1,0:T(8,128)S(1)}, f32[64,256]{1,0:T(8,128)}, u32[]{:S(2)}) %copy-start.3) | copy-done | bytes 65560
  48.4 0.5 slots.1
  48.9 9.2 %all-to-all-done = f32[256,1,128]{2,1,0:T(1,128)S(1)} async-done(((f32[256,1,128]{2,1,0:T(1,128)}), f32[256,1,128]{2,1,0:T(1,128)S(1)}, u32[]{:S(2)}, u32[]{:S(2)}) %all-to-all-start) | async-done | bytes 131104 | tf_op jit(solution)/shard_map/all_to_all | solution.py:503
  58.1 0.7 %collective-permute-start.8 = (bf16[192,16,128]{2,1,0:T(8,128)(2,1)S(1)}, bf16[192,16,128]{2,1,0:T(8,128)(2,1)}, u32[]{:S(2)}, u32[]{:S(2)}) collective-permute-start(bf16[192,16,128]{2,1,0:T(8,128)(2,1)S(1)} %hold.1.over_ref), channel_id=1, source_target_pairs={{0,1},{1,0},{2,3},{3,2},{4,5},{5,4},{6,7},{7,6},{8,9},{9,8},{10,11... | collective-permute-start | bytes 2359304 | tf_op jit(solution)/shard_map/ppermute | solution.py:488
  58.8 2.5 %solve.1 = (bf16[16,64]{1,0:T(8,128)(2,1)S(1)}, bf16[192,16,128]{2,1,0:T(8,128)(2,1)S(1)}) custom-call(s32[1]{0:T(128)} %bitcast.1.me_ref, f32[256,128]{1,0:T(8,128)S(1)} %bitcast.10, f32[256,128]{1,0:T(8,128)S(1)} %get-tuple-element.26.seen_ref.refs_2_, f32[256,128]{1,0:T(8,128)S(1)} %get-tuple-element.27.weight_ref, ...), custom_call_target="tpu_custom_call" | custom-call | tf_op jit(solution)/shard_map/solve/pallas_call | solution.py:404
  61.3 3.2 %update.1 = f32[16,4,48,128]{3,2,1,0:T(8,128)} custom-call(bf16[16,64]{1,0:T(8,128)(2,1)S(1)} %get-tuple-element.28.weights_ref, f32[16,4,48,128]{3,2,1,0:T(8,128)S(1)} %copy-done, bf16[192,16,128]{2,1,0:T(8,128)(2,1)S(1)} %anomalies.1.mine_ref, bf16[192,16,128]{2,1,0:T(8,128)(2,1)S(1)} %get-tuple-element.29.beside_ref, ...), custom_call_target="tpu_custom_call" | custom-call | tf_op jit(solution)/shard_map/update/pallas_call | solution.py:460
  (22 shorter events, 0.1 us)
Async XLA Ops:
  0.6 14.9 %copy-start = (f32[16,4,48,128]{3,2,1,0:T(8,128)S(1)}, f32[16,4,48,128]{3,2,1,0:T(8,128)}, u32[]{:S(2)}) copy-start(f32[16,4,48,128]{3,2,1,0:T(8,128)} %prior_ref.9) | copy-start | bytes 4718596
  2.5 20.0 %copy-start.1 = (f32[4,48,128]{2,1,0:T(8,128)S(1)}, f32[4,48,128]{2,1,0:T(8,128)}, u32[]{:S(2)}) copy-start(f32[4,48,128]{2,1,0:T(8,128)} %flow_ref.3) | copy-start | bytes 294916
  2.5 20.0 %copy-start.2 = (f32[4,48,128]{2,1,0:T(8,128)S(1)}, f32[4,48,128]{2,1,0:T(8,128)}, u32[]{:S(2)}) copy-start(f32[4,48,128]{2,1,0:T(8,128)} %visc_ref.3) | copy-start | bytes 294916
  2.5 20.0 %copy-start.4 = (s32[1,4]{1,0:T(1,128)S(1)}, s32[1,4]{1,0:T(1,128)}, u32[]{:S(2)}) copy-start(s32[1,4]{1,0:T(1,128)} %cells_ref.3) | copy-start | bytes 52
  2.5 19.2 %collective-permute-start.3 = (bf16[28,48,128]{2,1,0:T(8,128)(2,1)S(1)}, bf16[28,48,128]{2,1,0:T(8,128)(2,1)S(1)}, u32[]{:S(2)}, u32[]{:S(2)}) collective-permute-start(bf16[28,48,128]{2,1,0:T(8,128)(2,1)S(1)} %get-tuple-element.19), channel_id=1, source_target_pairs={{4,8},{12,16},{20,24},{28,32},{36,40},{44,48},{52,56},{60,64},{68,... | collective-permute-start | bytes 1032200 | tf_op jit(solution)/shard_map/ppermute | solution.py:485
  13.9 8.6 %collective-permute-start.2 = (bf16[28,48,128]{2,1,0:T(8,128)(2,1)S(1)}, bf16[28,48,128]{2,1,0:T(8,128)(2,1)S(1)}, u32[]{:S(2)}, u32[]{:S(2)}) collective-permute-start(bf16[28,48,128]{2,1,0:T(8,128)(2,1)S(1)} %get-tuple-element.18.after), channel_id=1, source_target_pairs={{0,4},{8,12},{16,20},{24,28},{32,36},{40,44},{48,52},{56,60},{64,6... | collective-permute-start | bytes 1032200 | tf_op jit(solution)/shard_map/ppermute | solution.py:485
  13.9 14.9 %collective-permute-start = (bf16[24,48,128]{2,1,0:T(8,128)(2,1)S(1)}, bf16[24,48,128]{2,1,0:T(8,128)(2,1)S(1)}, u32[]{:S(2)}, u32[]{:S(2)}) collective-permute-start(bf16[24,48,128]{2,1,0:T(8,128)(2,1)S(1)} %get-tuple-element.16), channel_id=1, source_target_pairs={{0,4},{8,12},{16,20},{24,28},{32,36},{40,44},{48,52},{56,60},{64,6... | collective-permute-start | bytes 884744 | tf_op jit(solution)/shard_map/ppermute | solution.py:485
  15.4 13.5 %collective-permute-start.1 = (bf16[24,48,128]{2,1,0:T(8,128)(2,1)S(1)}, bf16[24,48,128]{2,1,0:T(8,128)(2,1)S(1)}, u32[]{:S(2)}, u32[]{:S(2)}) collective-permute-start(bf16[24,48,128]{2,1,0:T(8,128)(2,1)S(1)} %get-tuple-element.17), channel_id=1, source_target_pairs={{4,8},{12,16},{20,24},{28,32},{36,40},{44,48},{52,56},{60,64},{68,... | collective-permute-start | bytes 884744 | tf_op jit(solution)/shard_map/ppermute | solution.py:485
  15.6 2.5 %collective-permute-start.4 = (f32[4,48,128]{2,1,0:T(8,128)S(1)}, f32[4,48,128]{2,1,0:T(8,128)S(1)}, u32[]{:S(2)}, u32[]{:S(2)}) collective-permute-start(f32[4,48,128]{2,1,0:T(8,128)S(1)} %total.1.a_ref), channel_id=1, source_target_pairs={{0,1},{1,0},{2,3},{3,2},{4,5},{5,4},{6,7},{7,6},{8,9},{9,8},{10,11... | collective-permute-start | bytes 294920 | tf_op jit(solution)/shard_map/ppermute | solution.py:488
  18.1 9.3 %collective-permute-start.5 = (f32[4,48,128]{2,1,0:T(8,128)S(1)}, f32[4,48,128]{2,1,0:T(8,128)S(1)}, u32[]{:S(2)}, u32[]{:S(2)}) collective-permute-start(f32[4,48,128]{2,1,0:T(8,128)S(1)} %pair_sum.1.a_ref), channel_id=1, source_target_pairs={{0,2},{1,3},{2,0},{3,1},{4,6},{5,7},{6,4},{7,5},{8,10},{9,11},{10,... | collective-permute-start | bytes 294920 | tf_op jit(solution)/shard_map/ppermute | solution.py:488
  29.6 28.6 %collective-permute-start.7 = (bf16[192,16,128]{2,1,0:T(8,128)(2,1)S(1)}, bf16[192,16,128]{2,1,0:T(8,128)(2,1)S(1)}, u32[]{:S(2)}, u32[]{:S(2)}) collective-permute-start(bf16[192,16,128]{2,1,0:T(8,128)(2,1)S(1)} %anomalies.1.mine_ref), channel_id=1, source_target_pairs={{0,2},{1,3},{2,0},{3,1},{4,6},{5,7},{6,4},{7,5},{8,10},{9,11},{10,... | collective-permute-start | bytes 2359304 | tf_op jit(solution)/shard_map/ppermute | solution.py:488
  30.0 17.6 %copy-start.5 = (s32[256]{0:T(256)S(1)}, s32[256]{0:T(256)}, u32[]{:S(2)}) copy-start(s32[256]{0:T(256)} %param.12) | copy-start | bytes 3076
  30.0 17.6 %copy-start.6 = (f32[256]{0:T(256)S(1)}, f32[256]{0:T(256)}, u32[]{:S(2)}) copy-start(f32[256]{0:T(256)} %param.13) | copy-start | bytes 3076
  30.0 17.6 %copy-start.7 = (f32[256]{0:T(256)S(1)}, f32[256]{0:T(256)}, u32[]{:S(2)}) copy-start(f32[256]{0:T(256)} %param.14) | copy-start | bytes 3076
  34.6 23.5 %all-to-all-start = ((f32[256,1,128]{2,1,0:T(1,128)}), f32[256,1,128]{2,1,0:T(1,128)S(1)}, u32[]{:S(2)}, u32[]{:S(2)}) async-start(f32[256,1,128]{2,1,0:T(1,128)} %bitcast.3), calls=%async_computation | async-start | bytes 262144 | tf_op jit(solution)/shard_map/all_to_all | solution.py:503
  45.3 13.5 %collective-permute-start.6 = (bf16[192,16,128]{2,1,0:T(8,128)(2,1)S(1)}, bf16[192,16,128]{2,1,0:T(8,128)(2,1)}, u32[]{:S(2)}, u32[]{:S(2)}) collective-permute-start(bf16[192,16,128]{2,1,0:T(8,128)(2,1)S(1)} %anomalies.1.mine_ref), channel_id=1, source_target_pairs={{0,1},{1,0},{2,3},{3,2},{4,5},{5,4},{6,7},{7,6},{8,9},{9,8},{10,11... | collective-permute-start | bytes 2359304 | tf_op jit(solution)/shard_map/ppermute | solution.py:488
  47.6 0.8 %copy-start.3 = (f32[64,256]{1,0:T(8,128)S(1)}, f32[64,256]{1,0:T(8,128)}, u32[]{:S(2)}) copy-start(f32[64,256]{1,0:T(8,128)} %noise_ref.1) | copy-start | bytes 196612
  58.1 3.2 %collective-permute-start.8 = (bf16[192,16,128]{2,1,0:T(8,128)(2,1)S(1)}, bf16[192,16,128]{2,1,0:T(8,128)(2,1)}, u32[]{:S(2)}, u32[]{:S(2)}) collective-permute-start(bf16[192,16,128]{2,1,0:T(8,128)(2,1)S(1)} %hold.1.over_ref), channel_id=1, source_target_pairs={{0,1},{1,0},{2,3},{3,2},{4,5},{5,4},{6,7},{7,6},{8,9},{9,8},{10,11... | collective-permute-start | bytes 2359304 | tf_op jit(solution)/shard_map/ppermute | solution.py:488

commit v7 on v6

--- a/solution.py
+++ b/solution.py
@@ -12,6 +12,8 @@
 PARTS = ((8, 0), (8, 1))
 CHUNKS = len(PARTS)
 ROWS = 8
+WINDOW = 8
+WAYS = 4
 STEPS = 1
 LOG_MID = 0.5 * (math.log(0.02) + math.log(0.05))
 LOG_HALF = 0.5 * (math.log(0.05) - math.log(0.02)) + 1.0
@@ -165,17 +167,99 @@
     buf[l, 8 + nz : 9 + nz] = value[0:1]
 
 
-def sweep_kernel(chunk, devices, odd_ref, cells_ref, prior_ref, flow_ref, visc_ref, inner_ref, outer_ref, *rest):
+def wrap(buf, l, value, nz):
+    buf[l, 8 : 8 + nz] = value
+    buf[l, 5:8] = value[nz - 3 : nz]
+    buf[l, 8 + nz : 12 + nz] = value[0:4]
+
+
+def viscosity_from(code):
+    return jnp.exp(jnp.log(code.astype(F32)) * (1.0 / (LN2 * NU_SCALE)) + LOG_MID)
+
+
+def probe_kernel(devices, odd_ref, cells_ref, prior_ref, visc_ref, inner_ref, outer_ref, lap0, adv0, rows_in, lines_ref, token_ref, nus, held_rows, rows):
+    _, layers, nz, ny = prior_ref.shape
+    part, place = PARTS[-1]
+    odd = odd_ref[0]
+    rows[...] = rows_in[...]
+    lane = lax.broadcasted_iota(jnp.int32, (WINDOW, ny), 1)
+
+    def step(slot, back, centre, front, visc):
+        held_rows[slot, 4 : 4 + WINDOW] = centre
+        sides = held_rows[slot, 3 : 3 + WINDOW] + held_rows[slot, 5 : 5 + WINDOW]
+        below = jnp.where(lane == 0, 0.0, pltpu.roll(centre, 1, 1))
+        above = jnp.where(lane == ny - 1, 0.0, pltpu.roll(centre, ny - 1, 1))
+        lap = back + front + (sides + (below + above)) - 6.0 * centre
+        return centre + visc * lap - 0.15 * (centre - back) + 0.01
+
+    def member(m, carry, way):
+        nu = nus.at[way]
+        for l in range(3):
+            for side_ref, ahead in ((inner_ref, 1 - odd), (outer_ref, odd)):
+                wrap(nu, ahead * (3 + layers) + l, viscosity_from(side_ref[m * 3 + l]), nz)
+        for l in range(layers):
+            wrap(nu, 3 + l, visc_ref[l] * jnp.exp(prior_ref[place * part + m, l]), nz)
+        for s in range(4):
+            cell = cells_ref[0, s]
+            layer, z = cell // (nz * ny), lax.rem(cell, nz * ny) // ny
+            window = pl.ds(z + 5, WINDOW)
+            reach = [layer + j for j in range(2 * ITERS - 1)]
+            visc = [nu[l, window] for l in reach]
+            speed = [adv0[l, window] + v * lap0[l, window] for l, v in zip(reach, visc)]
+            slot = (way * 4 + s) * 9
+            for _ in range(1, ITERS):
+                visc = visc[1:-1]
+                speed = [step(slot + k, *speed[k : k + 3], v) for k, v in enumerate(visc)]
+                slot += len(visc)
+            rows[pl.ds(s * 16 + place * part + m, 1), :] = speed[0][3:4]
+        return carry
+
+    def one_group(i, carry):
+        for way in range(WAYS):
+            member(i * WAYS + way, carry, way)
+        return carry
+
+    lax.fori_loop(0, part // WAYS, one_group, 0)
+    lane = lax.broadcasted_iota(jnp.int32, rows.shape, 1)
+    row = lax.broadcasted_iota(jnp.int32, rows.shape, 0)
+    y = jnp.zeros(rows.shape, jnp.int32)
+    for s in range(4):
+        y = jnp.where(row // 16 == s, lax.rem(cells_ref[0, s], ny), y)
+    picked = jnp.sum(jnp.where(lane == y, rows[...], 0.0), axis=1, keepdims=True)
+    line = jnp.sum(jnp.where(lane == row, picked, 0.0), axis=0, keepdims=True)
+    lines_ref[...] = jnp.broadcast_to(line, (devices, ny))
+    token_ref[...] = rows[0:8]
+
+
+def probes(odd, prior, visc, cells, halo, first, devices):
+    _, layers, nz, ny = prior.shape
+    _, rows, lap0, adv0 = first
+    return pl.pallas_call(
+        functools.partial(probe_kernel, devices),
+        in_specs=[SMEM] * 2 + [VMEM] * 7,
+        out_specs=[VMEM] * 2,
+        out_shape=[jax.ShapeDtypeStruct((devices, ny), F32), jax.ShapeDtypeStruct((8, ny), F32)],
+        scratch_shapes=[
+            pltpu.VMEM((WAYS,) + lap0.shape, F32),
+            pltpu.VMEM((36 * WAYS, WINDOW + 8, ny), F32),
+            pltpu.VMEM(rows.shape, F32),
+        ],
+        compiler_params=params(),
+        name="probes",
+    )(odd, cells, prior, visc, *halo, lap0, adv0, rows)
+
+
+def sweep_kernel(chunk, odd_ref, cells_ref, prior_ref, flow_ref, visc_ref, inner_ref, outer_ref, *rest):
     _, layers, nz, ny = prior_ref.shape
     part, place = PARTS[chunk]
     group = part // STEPS
     step = pl.program_id(0)
     wide = layers + 2 * ITERS
-    last = chunk == CHUNKS - 1
     odd = odd_ref[0]
     partners = ((inner_ref, 1 - odd), (outer_ref, odd))
     if chunk == 0:
-        out_ref, rows, lap0, adv0, buf0, buf1, nu = rest
+        _, out_ref, rows, lap0, adv0, buf0, buf1, nu = rest
+        prior, offset = prior_ref, place * part
 
         @pl.when(step == 0)
         def _():
@@ -188,23 +272,28 @@
             for l in range(1, wide - 1):
                 centre, back = buf0[l, 8 : 8 + nz], buf0[l - 1, 8 : 8 + nz]
                 sides = back + buf0[l + 1, 8 : 8 + nz] + neighbours(buf0, l, centre, nz, ny)
-                lap0[l - 1] = sides - 6.0 * centre
-                adv0[l - 1] = centre - 0.15 * (centre - back) + 0.01
+                wrap(lap0, l - 1, sides - 6.0 * centre, nz)
+                wrap(adv0, l - 1, centre - 0.15 * (centre - back) + 0.01, nz)
             rows[...] = jnp.zeros_like(rows)
 
-    elif not last:
-        lap0, adv0, rows_in, _, out_ref, rows, buf0, buf1, nu = rest
-
-        @pl.when(step == 0)
-        def _():
-            rows[...] = rows_in[...]
-
     else:
-        lap0, adv0, rows_in, _, out_ref, lines_ref, buf0, buf1, nu, rows = rest
-
-        @pl.when(step == 0)
-        def _():
-            rows[...] = rows_in[...]
+        sources, (_, _, out_ref, token_ref, buf0, buf1, nu), (lap0, adv0, *sides, prior, sems) = rest[:2], rest[2:9], rest[9:]
+        copies = [
+            pltpu.make_async_copy(source, target, sems.at[i])
+            for i, (source, target) in enumerate(
+                zip(
+                    (prior_ref.at[pl.ds(place * part, part)], inner_ref, outer_ref) + tuple(sources),
+                    (prior, *sides, lap0, adv0),
+                )
+            )
+        ]
+        for copy in copies:
+            copy.start()
+        for copy in copies:
+            copy.wait()
+        partners = ((sides[0], 1 - odd), (sides[1], odd))
+        offset = 0
+        token_ref[...] = jnp.zeros_like(token_ref)
 
     base_slabs = layers if chunk == 0 else 0
 
@@ -213,12 +302,12 @@
         first = base_slabs + index * 3
         for l in range(3):
             for side_ref, ahead in partners:
-                code = side_ref[first + l].astype(F32)
-                nu[ahead * (3 + layers) + l] = jnp.exp(jnp.log(code) * (1.0 / (LN2 * NU_SCALE)) + LOG_MID)
+                code = side_ref[first + l]
+                nu[ahead * (3 + layers) + l] = viscosity_from(code)
         for l in range(layers):
-            nu[3 + l] = visc_ref[l] * jnp.exp(prior_ref[place * part + index, l])
+            nu[3 + l] = visc_ref[l] * jnp.exp(prior[offset + index, l])
         for l in range(1, wide - 1):
-            put(buf1, l, adv0[l - 1] + nu[l - 1] * lap0[l - 1], nz)
+            put(buf1, l, adv0[l - 1, 8 : 8 + nz] + nu[l - 1] * lap0[l - 1, 8 : 8 + nz], nz)
         src, dst = buf1, buf0
         for sweep in range(1, ITERS):
             low, high = sweep + 1, wide - sweep - 1
@@ -233,52 +322,48 @@
                     put(dst, l, value, nz)
                 back, centre = centre, front
             src, dst = dst, src
-        for s in range(4):
-            cell = cells_ref[0, s]
-            layer, z = cell // (nz * ny), lax.rem(cell, nz * ny) // ny
-            rows[pl.ds(s * 16 + place * part + index, 1), :] = out_ref[m, layer, pl.ds(z, 1), :]
+        if chunk == 0:
+            for s in range(4):
+                cell = cells_ref[0, s]
+                layer, z = cell // (nz * ny), lax.rem(cell, nz * ny) // ny
+                rows[pl.ds(s * 16 + place * part + index, 1), :] = out_ref[m, layer, pl.ds(z, 1), :]
         return carry
 
     lax.fori_loop(0, group, member, 0)
-    if last:
-
-        @pl.when(step == STEPS - 1)
-        def _():
-            lane = lax.broadcasted_iota(jnp.int32, rows.shape, 1)
-            row = lax.broadcasted_iota(jnp.int32, rows.shape, 0)
-            y = jnp.zeros(rows.shape, jnp.int32)
-            for s in range(4):
-                y = jnp.where(row // 16 == s, lax.rem(cells_ref[0, s], ny), y)
-            picked = jnp.sum(jnp.where(lane == y, rows[...], 0.0), axis=1, keepdims=True)
-            line = jnp.sum(jnp.where(lane == row, picked, 0.0), axis=0, keepdims=True)
-            lines_ref[...] = jnp.broadcast_to(line, (devices, ny))
-
-
-def sweeps(odd, prior, flow, visc, cells, halo, chunk, before, devices):
+
+
+def sweeps(odd, prior, flow, visc, cells, halo, chunk, before=None, after=None):
     _, layers, nz, ny = prior.shape
     part, place = PARTS[chunk]
     wide = layers + 2 * ITERS
-    base_shape = (wide - 2, nz, ny)
-    args = [odd, cells, prior, flow, visc, *halo]
+    padded = (wide - 2, nz + 16, ny)
+    anywhere = pl.BlockSpec(memory_space=pl.ANY)
+    hbm = pl.BlockSpec(memory_space=pltpu.HBM)
+    args = [odd, cells, prior, flow, visc]
+    specs = [SMEM] * 2 + [VMEM] * 3
     scratch = [
         pltpu.VMEM((wide, nz + 16, ny), F32),
         pltpu.VMEM((wide, nz + 16, ny), F32),
-        pltpu.VMEM(base_shape, F32),
+        pltpu.VMEM((wide - 2, nz, ny), F32),
     ]
     alias = {}
-    specs = [SMEM] * 2 + [VMEM] * (len(args) - 2)
+    shapes = [prior.shape]
     if chunk:
-        args += [before[2], before[3], before[1], before[0]]
-        specs += [VMEM] * 3 + [pl.BlockSpec(memory_space=pltpu.HBM)]
+        velocity, _, lap0, adv0 = before
+        args += [pltpu.with_memory_space_constraint(x, pltpu.HBM) for x in (*halo, lap0, adv0)] + [after, velocity]
+        specs += [hbm] * 4 + [anywhere, hbm]
+        args[2:4] = [pltpu.with_memory_space_constraint(x, pltpu.HBM) for x in (prior, flow)]
+        specs[2:4] = [hbm, hbm]
         alias = {len(args) - 1: 0}
-    last = chunk == CHUNKS - 1
-    shapes = [prior.shape, (devices, ny) if last else (64, ny)]
-    if chunk == 0:
-        shapes += [base_shape] * 2
-    if last:
-        scratch.append(pltpu.VMEM((64, ny), F32))
-    out = pl.pallas_call(
-        functools.partial(sweep_kernel, chunk, devices),
+        scratch += [pltpu.VMEM(padded, F32)] * 2 + [pltpu.VMEM(halo[0].shape, BF16)] * 2
+        scratch += [pltpu.VMEM((part, layers, nz, ny), F32), pltpu.SemaphoreType.DMA((5,))]
+        shapes += [(8, ny)]
+    else:
+        args += [*halo, after]
+        specs += [VMEM] * 2 + [anywhere]
+        shapes += [(64, ny), padded, padded]
+    return pl.pallas_call(
+        functools.partial(sweep_kernel, chunk),
         grid=(STEPS,),
         in_specs=specs,
         out_specs=[pl.BlockSpec((part // STEPS, layers, nz, ny), lambda i: (place * STEPS + i, 0, 0, 0))] + [VMEM] * (len(shapes) - 1),
@@ -288,7 +373,6 @@
         compiler_params=params(),
         name=f"sweeps{chunk}",
     )(*args)
-    return tuple(out) + (tuple(before[2:]) if chunk else ())
 
 
 def anomaly_kernel(members_all, prior_ref, a_ref, b_ref, *refs):
@@ -353,9 +437,13 @@
     return lax.dot_general(a, b, (dims, ((), ())), precision=lax.Precision.HIGHEST, preferred_element_type=F32)
 
 
-def solve_kernel(members, here, me_ref, vals_ref, seen_ref, weight_ref, beside_any, out_ref, beside_ref, scr, sem):
-    fetch = pltpu.make_async_copy(beside_any, beside_ref, sem)
-    fetch.start()
+def solve_kernel(members, here, me_ref, vals_ref, seen_ref, weight_ref, beside_any, prior_hbm, out_ref, beside_ref, prior_ref, scr, sems):
+    fetches = [
+        pltpu.make_async_copy(beside_any, beside_ref, sems.at[0]),
+        pltpu.make_async_copy(prior_hbm, prior_ref, sems.at[1]),
+    ]
+    for fetch in fetches:
+        fetch.start()
     devices, ny = vals_ref.shape
     groups = members // here
     tiles = devices // groups
@@ -397,19 +485,24 @@
     scr[...] = jnp.concatenate(order + [jnp.zeros((ny - members, ny), F32)], axis=0).T
     mine = scr[pl.ds(pl.multiple_of(me * here, here), here), :]
     out_ref[...] = mine[:, :members].astype(BF16)
-    fetch.wait()
-
-
-def solve(vals, seen, weight, me, members, here, beside):
+    for fetch in fetches:
+        fetch.wait()
+
+
+def solve(vals, seen, weight, me, members, here, beside, prior):
     return pl.pallas_call(
         functools.partial(solve_kernel, members, here),
-        in_specs=[SMEM] + [VMEM] * 3 + [pl.BlockSpec(memory_space=pl.ANY)],
-        out_specs=[VMEM] * 2,
-        out_shape=[jax.ShapeDtypeStruct((here, members), BF16), jax.ShapeDtypeStruct(beside.shape, BF16)],
-        scratch_shapes=[pltpu.VMEM((128, 128), F32), pltpu.SemaphoreType.DMA],
+        in_specs=[SMEM] + [VMEM] * 3 + [pl.BlockSpec(memory_space=pl.ANY), pl.BlockSpec(memory_space=pltpu.HBM)],
+        out_specs=[VMEM] * 3,
+        out_shape=[
+            jax.ShapeDtypeStruct((here, members), BF16),
+            jax.ShapeDtypeStruct(beside.shape, BF16),
+            jax.ShapeDtypeStruct(prior.shape, F32),
+        ],
+        scratch_shapes=[pltpu.VMEM((128, 128), F32), pltpu.SemaphoreType.DMA((2,))],
         compiler_params=params(),
         name="solve",
-    )(me, vals, seen, weight, beside)
+    )(me, vals, seen, weight, beside, pltpu.with_memory_space_constraint(prior, pltpu.HBM))
 
 
 def update_kernel(weights_ref, prior_ref, mine_ref, beside_ref, over_ref, far_any, out_hbm, far_ref, out_ref, sems):
@@ -489,23 +582,22 @@
 
     sent = encode(odd, prior, base_flow, base_visc)
     halos = [(swap(sent[2 * c], 0), swap(sent[2 * c + 1], 1)) for c in range(CHUNKS)]
-    state, states = None, []
-    for chunk in range(CHUNKS):
-        state = sweeps(odd, prior, base_flow, base_visc, probe_cells, halos[chunk], chunk, state, tiles * groups)
-        states.append(state)
-    velocity, payload = state[:2]
+    fields = (odd, prior, base_flow, base_visc, probe_cells)
+    seen, weight = in_slots(obs_slot, obs_values, obs_var, obs_noise, probe_cells.shape[1], sent[0])
+    first = sweeps(*fields, halos[0], 0, after=seen)
+    payload, token = probes(odd, prior, base_visc, probe_cells, halos[1], first, tiles * groups)
+    velocity, done = sweeps(*fields, halos[1], 1, first, token)
     total = total_of(prior, sent[0])
     chip = pair_sum(total, across(total, 1))
     totals = [chip, across(chip, 2)]
-    mine = anomalies(prior, totals, float(members), states[0][1], *halos[1])
+    mine = anomalies(prior, totals, float(members), first[1], *halos[1])
     beside = across(mine, 1)
     over = across(mine, 2)
     vals = lax.all_to_all(payload, ("tile", "mem"), 0, 0, tiled=True)
-    seen, weight = in_slots(obs_slot, obs_values, obs_var, obs_noise, probe_cells.shape[1], payload)
-    over = held(over, vals, seen)
+    over = held(over, vals, done)
     far = across(over, 1)
-    weights, beside = solve(vals, seen, weight, me, members, here, beside)
-    return velocity, updated(weights, prior, mine, beside, over, far)
+    weights, beside, near_prior = solve(vals, seen, weight, me, members, here, beside, prior)
+    return velocity, updated(weights, near_prior, mine, beside, over, far)
 
 
 def solution(mesh):

time: 64.7 us -> 62.4 us (0.964)
  waiting for transfers between devices: 15.6 us -> 10.4 us
  Pallas kernels: 18.2 us -> 21.2 us
    all_to_all x1, waiting for transfers between devices: 9.21 us -> 4.6 us  [per_device(): vals = lax.all_to_all(payload, ('tile', 'mem'), 0, 0, tiled=True)]
    pallas_call x2 -> x3, Pallas kernels: 9.46 us -> 13.3 us  [the longest x2 10.9 us: sweeps(): pl.pallas_call(functools.partial(sweep_kernel, chunk), grid=(STEPS,), in_...]
    pallas_call x1, Pallas kernels: 3.15 us -> 2.24 us  [updated(): pl.pallas_call(update_kernel, in_specs=[VMEM] * 5 + [pl.BlockSpec(memory_...]
  transfers between devices with their start and end apart: 10 -> 10, of which waited for: 5 -> 5; matrix products, arithmetic and copies ran while one was open for 0% -> 0% of each run, Pallas kernels for 19% -> 26%
where the time goes in v7:
time: 62.4 us; the launch traced here: 62.3 us
  starting transfers between devices  29 us (46%)
  Pallas kernels  21.2 us (34%)
  waiting for transfers between devices  10.4 us (17%)
  between operations  0.85 us (1%)
  local copies, waits for them, and re-layouts  0.73 us (1%)
    ppermute x4, starting transfers between devices, swap(): return lax.ppermute(x, 'tile', pairs + [(b, a) for a, b in pairs])  13 us
    pallas_call x2, Pallas kernels, sweeps(): pl.pallas_call(functools.partial(sweep_kernel, chunk), grid=(STEPS,), in_...  10.9 us
    all_to_all x1, starting transfers between devices, per_device(): vals = lax.all_to_all(payload, ('tile', 'mem'), 0, 0, tiled=True)  10.7 us
    ppermute x5, starting transfers between devices, across(): return lax.ppermute(x, 'mem', [(i, i ^ bits) for i in range(groups)])  5.35 us
    ppermute x4, waiting for transfers between devices, swap(): return lax.ppermute(x, 'tile', pairs + [(b, a) for a, b in pairs])  4.88 us
    all_to_all x1, waiting for transfers between devices, per_device(): vals = lax.all_to_all(payload, ('tile', 'mem'), 0, 0, tiled=True)  4.6 us
    pallas_call x1, Pallas kernels, solve(): pl.pallas_call(functools.partial(solve_kernel, members, here), in_specs=[...  2.53 us
    pallas_call x1, Pallas kernels, probes(): pl.pallas_call(functools.partial(probe_kernel, devices), in_specs=[SMEM]...  2.45 us
  transfers between devices with their start and end apart: 10, of which 5 were waited for; matrix products, arithmetic and copies ran while one was open for 0% of the time, Pallas kernels for 26%

profile of v7, /device:TPU:1, one launch (start us, length us, event | category | flops | bytes accessed | tf_op | source)
XLA Modules:
  0.0 62.3 jit_solution(522151854746765075)
XLA Ops:
  0.6 1.9 %encode.1 = (bf16[28,48,128]{2,1,0:T(8,128)(2,1)S(1)}, bf16[28,48,128]{2,1,0:T(8,128)(2,1)S(1)}, bf16[24,48,128]{2,1,0:T(8,128)(2,1)S(1)}, bf16[24,48,128]{2,1,0:T(8,128)(2,1)S(1)}) custom-call(s32[1]{0:T(128)} %bitcast.odd_ref, f32[16,4,48,128]{3,2,1,0:T(8,128)} %prior_hbm.3, f32[4,48,128]{2,1,0:T(8,128)} %flow_ref.3, f32[4,48,128]{2,1,0:T(8,128)} %visc_ref.5), custom_call_target="tpu_custom_call" | custom-call | tf_op jit(solution)/shard_map/encode/pallas_call | solution.py:92
  2.6 11.4 %collective-permute-start.3 = (bf16[28,48,128]{2,1,0:T(8,128)(2,1)S(1)}, bf16[28,48,128]{2,1,0:T(8,128)(2,1)S(1)}, u32[]{:S(2)}, u32[]{:S(2)}) collective-permute-start(bf16[28,48,128]{2,1,0:T(8,128)(2,1)S(1)} %get-tuple-element.22), channel_id=1, source_target_pairs={{4,8},{12,16},{20,24},{28,32},{36,40},{44,48},{52,56},{60,64},{68,... | collective-permute-start | bytes 1032200 | tf_op jit(solution)/shard_map/ppermute | solution.py:578
  14.0 1.5 %collective-permute-start = (bf16[24,48,128]{2,1,0:T(8,128)(2,1)S(1)}, bf16[24,48,128]{2,1,0:T(8,128)(2,1)S(1)}, u32[]{:S(2)}, u32[]{:S(2)}) collective-permute-start(bf16[24,48,128]{2,1,0:T(8,128)(2,1)S(1)} %get-tuple-element.19), channel_id=1, source_target_pairs={{0,4},{8,12},{16,20},{24,28},{32,36},{40,44},{48,52},{56,60},{64,6... | collective-permute-start | bytes 884744 | tf_op jit(solution)/shard_map/ppermute | solution.py:578
  15.5 0.1 collective-permute-start.1
  15.6 0.1 total.1.a_ref
  15.6 1.6 %collective-permute-start.4 = (f32[4,48,128]{2,1,0:T(8,128)S(1)}, f32[4,48,128]{2,1,0:T(8,128)S(1)}, u32[]{:S(2)}, u32[]{:S(2)}) collective-permute-start(f32[4,48,128]{2,1,0:T(8,128)S(1)} %total.1.a_ref), channel_id=1, source_target_pairs={{0,1},{1,0},{2,3},{3,2},{4,5},{5,4},{6,7},{7,6},{8,9},{9,8},{10,11... | collective-permute-start | bytes 294920 | tf_op jit(solution)/shard_map/ppermute | solution.py:581
  17.2 0.9 %collective-permute-done.4.b_ref = f32[4,48,128]{2,1,0:T(8,128)S(1)} collective-permute-done((f32[4,48,128]{2,1,0:T(8,128)S(1)}, f32[4,48,128]{2,1,0:T(8,128)S(1)}, u32[]{:S(2)}, u32[]{:S(2)}) %collective-permute-start.4) | collective-permute-done | bytes 98336 | tf_op jit(solution)/shard_map/ppermute | solution.py:581
  18.2 0.4 collective-permute-start.5
  18.6 0.5 slots.1
  19.1 2.6 %collective-permute-done.3.outer_ref = bf16[28,48,128]{2,1,0:T(8,128)(2,1)S(1)} collective-permute-done((bf16[28,48,128]{2,1,0:T(8,128)(2,1)S(1)}, bf16[28,48,128]{2,1,0:T(8,128)(2,1)S(1)}, u32[]{:S(2)}, u32[]{:S(2)}) %collective-permute-start.3) | collective-permute-done | bytes 344096 | tf_op jit(solution)/shard_map/ppermute | solution.py:578
  21.8 0.8 %collective-permute-done.2.inner_ref = bf16[28,48,128]{2,1,0:T(8,128)(2,1)S(1)} collective-permute-done((bf16[28,48,128]{2,1,0:T(8,128)(2,1)S(1)}, bf16[28,48,128]{2,1,0:T(8,128)(2,1)S(1)}, u32[]{:S(2)}, u32[]{:S(2)}) %collective-permute-start.2) | collective-permute-done | bytes 344096 | tf_op jit(solution)/shard_map/ppermute | solution.py:578
  22.6 4.9 %sweeps0.1 = (f32[16,4,48,128]{3,2,1,0:T(8,128)}, f32[64,128]{1,0:T(8,128)S(1)}, f32[10,64,128]{2,1,0:T(8,128)S(1)}, f32[10,64,128]{2,1,0:T(8,128)S(1)}) custom-call(s32[1]{0:T(128)} %bitcast.odd_ref, s32[1,4]{1,0:T(1,128)S(1)} %copy-done.13, f32[16,4,48,128]{3,2,1,0:T(8,128)S(1)} %copy-done, f32[4,48,128]{2,1,0:T(8,128)S(1)} %copy-done.6, ...), custom_call_target="tpu_custom_call" | custom-call | tf_op jit(solution)/shard_map/sweeps0/pallas_call | solution.py:365
  27.5 1.4 %collective-permute-done.inner_ref.refs_1_ = bf16[24,48,128]{2,1,0:T(8,128)(2,1)S(1)} collective-permute-done((bf16[24,48,128]{2,1,0:T(8,128)(2,1)S(1)}, bf16[24,48,128]{2,1,0:T(8,128)(2,1)S(1)}, u32[]{:S(2)}, u32[]{:S(2)}) %collective-permute-start) | collective-permute-done | bytes 294944 | tf_op jit(solution)/shard_map/ppermute | solution.py:578
  28.9 0.7 %anomalies.1.mine_ref = bf16[192,16,128]{2,1,0:T(8,128)(2,1)S(1)} custom-call(f32[16,4,48,128]{3,2,1,0:T(8,128)S(1)} %copy-done, f32[4,48,128]{2,1,0:T(8,128)S(1)} %pair_sum.1.a_ref, f32[4,48,128]{2,1,0:T(8,128)S(1)} %collective-permute-done.5.b_ref, f32[64,128]{1,0:T(8,128)S(1)} %get-tuple-element.26.rows_in.refs_0_, ...), custom_call_target="tpu_custom_call" | custom-call | tf_op jit(solution)/shard_map/anomalies/pallas_call | solution.py:391
  29.6 0.4 collective-permute-start.7
  30.1 2.5 %probes.1 = (f32[256,128]{1,0:T(8,128)S(1)}, f32[8,128]{1,0:T(8,128)S(1)}) custom-call(s32[1]{0:T(128)} %bitcast.odd_ref, s32[1,4]{1,0:T(1,128)S(1)} %copy-done.13, f32[16,4,48,128]{3,2,1,0:T(8,128)S(1)} %copy-done, f32[4,48,128]{2,1,0:T(8,128)S(1)} %copy-done.3, bf16[24,48,128]{2,1,0:T(8,128)(2,1)S(1)} %collective-permute-done.inner_ref.refs_1_, ...), custom_call_target="tpu_custom_call" | custom-call | tf_op jit(solution)/shard_map/probes/pallas_call | solution.py:237
  32.5 0.6 %copy-done.11 = f32[256,128]{1,0:T(8,128)} copy-done((f32[256,128]{1,0:T(8,128)}, f32[256,128]{1,0:T(8,128)S(1)}, u32[]{:S(2)}) %copy-start.11) | copy-done | bytes 131096
  33.2 10.7 %all-to-all-start = ((f32[256,1,128]{2,1,0:T(1,128)}), f32[256,1,128]{2,1,0:T(1,128)S(1)}, u32[]{:S(2)}, u32[]{:S(2)}) async-start(f32[256,1,128]{2,1,0:T(1,128)} %bitcast.11), calls=%async_computation | async-start | bytes 262144 | tf_op jit(solution)/shard_map/all_to_all | solution.py:596
  43.9 2.2 %collective-permute-start.6 = (bf16[192,16,128]{2,1,0:T(8,128)(2,1)S(1)}, bf16[192,16,128]{2,1,0:T(8,128)(2,1)S(1)}, u32[]{:S(2)}, u32[]{:S(2)}) collective-permute-start(bf16[192,16,128]{2,1,0:T(8,128)(2,1)S(1)} %anomalies.1.mine_ref), channel_id=1, source_target_pairs={{0,1},{1,0},{2,3},{3,2},{4,5},{5,4},{6,7},{7,6},{8,9},{9,8},{10,11... | collective-permute-start | bytes 2359304 | tf_op jit(solution)/shard_map/ppermute | solution.py:581
  46.1 6.0 %sweeps1.1 = (f32[16,4,48,128]{3,2,1,0:T(8,128)}, f32[8,128]{1,0:T(8,128)S(1)}) custom-call(s32[1]{0:T(128)} %bitcast.odd_ref, s32[1,4]{1,0:T(1,128)S(1)} %copy-done.13, f32[16,4,48,128]{3,2,1,0:T(8,128)} %prior_hbm.3, f32[4,48,128]{2,1,0:T(8,128)} %flow_ref.3, f32[4,48,128]{2,1,0:T(8,128)S(1)} %copy-done.3, ...), custom_call_target="tpu_custom_call", output_to_operand_aliasing={{0}: (10, {})} | custom-call | tf_op jit(solution)/shard_map/sweeps1/pallas_call | solution.py:365
  52.2 4.6 %all-to-all-done = f32[256,1,128]{2,1,0:T(1,128)S(1)} async-done(((f32[256,1,128]{2,1,0:T(1,128)}), f32[256,1,128]{2,1,0:T(1,128)S(1)}, u32[]{:S(2)}, u32[]{:S(2)}) %all-to-all-start) | async-done | bytes 131104 | tf_op jit(solution)/shard_map/all_to_all | solution.py:596
  56.8 0.7 %collective-permute-start.8 = (bf16[192,16,128]{2,1,0:T(8,128)(2,1)S(1)}, bf16[192,16,128]{2,1,0:T(8,128)(2,1)S(1)}, u32[]{:S(2)}, u32[]{:S(2)}) collective-permute-start(bf16[192,16,128]{2,1,0:T(8,128)(2,1)S(1)} %hold.1.over_ref), channel_id=1, source_target_pairs={{0,1},{1,0},{2,3},{3,2},{4,5},{5,4},{6,7},{7,6},{8,9},{9,8},{10,11... | collective-permute-start | bytes 2359304 | tf_op jit(solution)/shard_map/ppermute | solution.py:581
  57.5 2.5 %solve.1 = (bf16[16,64]{1,0:T(8,128)(2,1)S(1)}, bf16[192,16,128]{2,1,0:T(8,128)(2,1)S(1)}, f32[16,4,48,128]{3,2,1,0:T(8,128)S(1)}) custom-call(s32[1]{0:T(128)} %bitcast.4.me_ref, f32[256,128]{1,0:T(8,128)S(1)} %bitcast.10, f32[256,128]{1,0:T(8,128)S(1)} %copy-done.8, f32[256,128]{1,0:T(8,128)S(1)} %copy-done.10, ...), custom_call_target="tpu_custom_call" | custom-call | tf_op jit(solution)/shard_map/solve/pallas_call | solution.py:493
  60.0 2.2 %update.1 = f32[16,4,48,128]{3,2,1,0:T(8,128)} custom-call(bf16[16,64]{1,0:T(8,128)(2,1)S(1)} %get-tuple-element.32.weights_ref, f32[16,4,48,128]{3,2,1,0:T(8,128)S(1)} %get-tuple-element.33.prior_ref, bf16[192,16,128]{2,1,0:T(8,128)(2,1)S(1)} %anomalies.1.mine_ref, bf16[192,16,128]{2,1,0:T(8,128)(2,1)S(1)} %get-tuple-element.34.beside_ref, ...), custom_call_target="tpu_custom_call" | custom-call | tf_op jit(solution)/shard_map/update/pallas_call | solution.py:553
  (41 shorter events, 0.1 us)
Async XLA Ops:
  0.6 14.9 %copy-start = (f32[16,4,48,128]{3,2,1,0:T(8,128)S(1)}, f32[16,4,48,128]{3,2,1,0:T(8,128)}, u32[]{:S(2)}) copy-start(f32[16,4,48,128]{3,2,1,0:T(8,128)} %prior_hbm.3) | copy-start | bytes 4718596
  2.5 16.1 %copy-start.12 = (f32[64,256]{1,0:T(8,128)S(1)}, f32[64,256]{1,0:T(8,128)}, u32[]{:S(2)}) copy-start(f32[64,256]{1,0:T(8,128)} %noise_ref.1) | copy-start | bytes 196612
  2.5 16.1 %copy-start.14 = (s32[256]{0:T(256)S(1)}, s32[256]{0:T(256)}, u32[]{:S(2)}) copy-start(s32[256]{0:T(256)} %param.12) | copy-start | bytes 3076
  2.5 16.1 %copy-start.15 = (f32[256]{0:T(256)S(1)}, f32[256]{0:T(256)}, u32[]{:S(2)}) copy-start(f32[256]{0:T(256)} %param.13) | copy-start | bytes 3076
  2.5 16.1 %copy-start.16 = (f32[256]{0:T(256)S(1)}, f32[256]{0:T(256)}, u32[]{:S(2)}) copy-start(f32[256]{0:T(256)} %param.14) | copy-start | bytes 3076
  2.6 20.0 %copy-start.3 = (f32[4,48,128]{2,1,0:T(8,128)S(1)}, f32[4,48,128]{2,1,0:T(8,128)}, u32[]{:S(2)}) copy-start(f32[4,48,128]{2,1,0:T(8,128)} %visc_ref.5) | copy-start | bytes 294916
  2.6 20.0 %copy-start.6 = (f32[4,48,128]{2,1,0:T(8,128)S(1)}, f32[4,48,128]{2,1,0:T(8,128)}, u32[]{:S(2)}) copy-start(f32[4,48,128]{2,1,0:T(8,128)} %flow_ref.3) | copy-start | bytes 294916
  2.6 20.0 %copy-start.13 = (s32[1,4]{1,0:T(1,128)S(1)}, s32[1,4]{1,0:T(1,128)}, u32[]{:S(2)}) copy-start(s32[1,4]{1,0:T(1,128)} %cells_ref.5) | copy-start | bytes 52
  2.6 19.2 %collective-permute-start.3 = (bf16[28,48,128]{2,1,0:T(8,128)(2,1)S(1)}, bf16[28,48,128]{2,1,0:T(8,128)(2,1)S(1)}, u32[]{:S(2)}, u32[]{:S(2)}) collective-permute-start(bf16[28,48,128]{2,1,0:T(8,128)(2,1)S(1)} %get-tuple-element.22), channel_id=1, source_target_pairs={{4,8},{12,16},{20,24},{28,32},{36,40},{44,48},{52,56},{60,64},{68,... | collective-permute-start | bytes 1032200 | tf_op jit(solution)/shard_map/ppermute | solution.py:578
  14.0 8.6 %collective-permute-start.2 = (bf16[28,48,128]{2,1,0:T(8,128)(2,1)S(1)}, bf16[28,48,128]{2,1,0:T(8,128)(2,1)S(1)}, u32[]{:S(2)}, u32[]{:S(2)}) collective-permute-start(bf16[28,48,128]{2,1,0:T(8,128)(2,1)S(1)} %get-tuple-element.21.after), channel_id=1, source_target_pairs={{0,4},{8,12},{16,20},{24,28},{32,36},{40,44},{48,52},{56,60},{64,6... | collective-permute-start | bytes 1032200 | tf_op jit(solution)/shard_map/ppermute | solution.py:578
  14.0 14.9 %collective-permute-start = (bf16[24,48,128]{2,1,0:T(8,128)(2,1)S(1)}, bf16[24,48,128]{2,1,0:T(8,128)(2,1)S(1)}, u32[]{:S(2)}, u32[]{:S(2)}) collective-permute-start(bf16[24,48,128]{2,1,0:T(8,128)(2,1)S(1)} %get-tuple-element.19), channel_id=1, source_target_pairs={{0,4},{8,12},{16,20},{24,28},{32,36},{40,44},{48,52},{56,60},{64,6... | collective-permute-start | bytes 884744 | tf_op jit(solution)/shard_map/ppermute | solution.py:578
  15.5 13.5 %collective-permute-start.1 = (bf16[24,48,128]{2,1,0:T(8,128)(2,1)S(1)}, bf16[24,48,128]{2,1,0:T(8,128)(2,1)S(1)}, u32[]{:S(2)}, u32[]{:S(2)}) collective-permute-start(bf16[24,48,128]{2,1,0:T(8,128)(2,1)S(1)} %get-tuple-element.20), channel_id=1, source_target_pairs={{4,8},{12,16},{20,24},{28,32},{36,40},{44,48},{52,56},{60,64},{68,... | collective-permute-start | bytes 884744 | tf_op jit(solution)/shard_map/ppermute | solution.py:578
  15.6 2.5 %collective-permute-start.4 = (f32[4,48,128]{2,1,0:T(8,128)S(1)}, f32[4,48,128]{2,1,0:T(8,128)S(1)}, u32[]{:S(2)}, u32[]{:S(2)}) collective-permute-start(f32[4,48,128]{2,1,0:T(8,128)S(1)} %total.1.a_ref), channel_id=1, source_target_pairs={{0,1},{1,0},{2,3},{3,2},{4,5},{5,4},{6,7},{7,6},{8,9},{9,8},{10,11... | collective-permute-start | bytes 294920 | tf_op jit(solution)/shard_map/ppermute | solution.py:581
  18.2 9.3 %collective-permute-start.5 = (f32[4,48,128]{2,1,0:T(8,128)S(1)}, f32[4,48,128]{2,1,0:T(8,128)S(1)}, u32[]{:S(2)}, u32[]{:S(2)}) collective-permute-start(f32[4,48,128]{2,1,0:T(8,128)S(1)} %pair_sum.1.a_ref), channel_id=1, source_target_pairs={{0,2},{1,3},{2,0},{3,1},{4,6},{5,7},{6,4},{7,5},{8,10},{9,11},{10,... | collective-permute-start | bytes 294920 | tf_op jit(solution)/shard_map/ppermute | solution.py:581
  19.1 10.5 %copy-start.7 = (f32[256,128]{1,0:T(8,128)}, f32[256,128]{1,0:T(8,128)S(1)}, u32[]{:S(2)}) copy-start(f32[256,128]{1,0:T(8,128)S(1)} %get-tuple-element.23.rest_0_.seen_ref) | copy-start | bytes 393220
  19.1 10.5 %copy-start.9 = (f32[256,128]{1,0:T(8,128)}, f32[256,128]{1,0:T(8,128)S(1)}, u32[]{:S(2)}) copy-start(f32[256,128]{1,0:T(8,128)S(1)} %get-tuple-element.31.weight_ref) | copy-start | bytes 393220
  27.5 2.5 %copy-start.4 = (f32[10,64,128]{2,1,0:T(8,128)}, f32[10,64,128]{2,1,0:T(8,128)S(1)}, u32[]{:S(2)}) copy-start(f32[10,64,128]{2,1,0:T(8,128)S(1)} %get-tuple-element.24.lap0.rest_0_) | copy-start | bytes 983044
  27.5 2.5 %copy-start.5 = (f32[10,64,128]{2,1,0:T(8,128)}, f32[10,64,128]{2,1,0:T(8,128)S(1)}, u32[]{:S(2)}) copy-start(f32[10,64,128]{2,1,0:T(8,128)S(1)} %get-tuple-element.25.adv0.rest_1_) | copy-start | bytes 983044
  29.6 27.1 %collective-permute-start.7 = (bf16[192,16,128]{2,1,0:T(8,128)(2,1)S(1)}, bf16[192,16,128]{2,1,0:T(8,128)(2,1)S(1)}, u32[]{:S(2)}, u32[]{:S(2)}) collective-permute-start(bf16[192,16,128]{2,1,0:T(8,128)(2,1)S(1)} %anomalies.1.mine_ref), channel_id=1, source_target_pairs={{0,2},{1,3},{2,0},{3,1},{4,6},{5,7},{6,4},{7,5},{8,10},{9,11},{10,... | collective-permute-start | bytes 2359304 | tf_op jit(solution)/shard_map/ppermute | solution.py:581
  33.2 23.6 %all-to-all-start = ((f32[256,1,128]{2,1,0:T(1,128)}), f32[256,1,128]{2,1,0:T(1,128)S(1)}, u32[]{:S(2)}, u32[]{:S(2)}) async-start(f32[256,1,128]{2,1,0:T(1,128)} %bitcast.11), calls=%async_computation | async-start | bytes 262144 | tf_op jit(solution)/shard_map/all_to_all | solution.py:596
  43.9 13.6 %collective-permute-start.6 = (bf16[192,16,128]{2,1,0:T(8,128)(2,1)S(1)}, bf16[192,16,128]{2,1,0:T(8,128)(2,1)S(1)}, u32[]{:S(2)}, u32[]{:S(2)}) collective-permute-start(bf16[192,16,128]{2,1,0:T(8,128)(2,1)S(1)} %anomalies.1.mine_ref), channel_id=1, source_target_pairs={{0,1},{1,0},{2,3},{3,2},{4,5},{5,4},{6,7},{7,6},{8,9},{9,8},{10,11... | collective-permute-start | bytes 2359304 | tf_op jit(solution)/shard_map/ppermute | solution.py:581
  52.1 5.3 %copy-start.8 = (f32[256,128]{1,0:T(8,128)S(1)}, f32[256,128]{1,0:T(8,128)}, u32[]{:S(2)}) copy-start(f32[256,128]{1,0:T(8,128)} %copy-done.7) | copy-start | bytes 393220
  52.1 5.3 %copy-start.10 = (f32[256,128]{1,0:T(8,128)S(1)}, f32[256,128]{1,0:T(8,128)}, u32[]{:S(2)}) copy-start(f32[256,128]{1,0:T(8,128)} %copy-done.9) | copy-start | bytes 393220
  56.8 3.3 %collective-permute-start.8 = (bf16[192,16,128]{2,1,0:T(8,128)(2,1)S(1)}, bf16[192,16,128]{2,1,0:T(8,128)(2,1)S(1)}, u32[]{:S(2)}, u32[]{:S(2)}) collective-permute-start(bf16[192,16,128]{2,1,0:T(8,128)(2,1)S(1)} %hold.1.over_ref), channel_id=1, source_target_pairs={{0,1},{1,0},{2,3},{3,2},{4,5},{5,4},{6,7},{7,6},{8,9},{9,8},{10,11... | collective-permute-start | bytes 2359304 | tf_op jit(solution)/shard_map/ppermute | solution.py:581
  (3 other events, 2.9 us)

commit v8 on v7

--- a/solution.py
+++ b/solution.py
@@ -13,7 +13,7 @@
 CHUNKS = len(PARTS)
 ROWS = 8
 WINDOW = 8
-WAYS = 4
+WAYS = 2
 STEPS = 1
 LOG_MID = 0.5 * (math.log(0.02) + math.log(0.05))
 LOG_HALF = 0.5 * (math.log(0.05) - math.log(0.02)) + 1.0
@@ -471,7 +471,7 @@
     error = jnp.where(diagonal, alpha * half, 0.0) - alpha * gram
 
     def more(state):
-        return (state[0] > 1e-9) & (state[1] < 40)
+        return (state[0] > 2e-6) & (state[1] < 40)
 
     def double(state):
         size, count, power_of, x = state
@@ -505,11 +505,10 @@
     )(me, vals, seen, weight, beside, pltpu.with_memory_space_constraint(prior, pltpu.HBM))
 
 
-def update_kernel(weights_ref, prior_ref, mine_ref, beside_ref, over_ref, far_any, out_hbm, far_ref, out_ref, sems):
+def update_kernel(weights_ref, prior_ref, *refs):
+    blocks, (out_hbm, out_ref, sems) = refs[:4], refs[4:]
     here, layers, nz, ny = prior_ref.shape
     members = weights_ref.shape[1]
-    fetch = pltpu.make_async_copy(far_any, far_ref, sems.at[layers])
-    fetch.start()
     tall = (here * ROWS, here)
     spread = lax.broadcasted_iota(jnp.int32, tall, 0) // ROWS == lax.broadcasted_iota(jnp.int32, tall, 1)
     wide = (members, members * ROWS)
@@ -523,27 +522,20 @@
     lhs = jnp.where(row % ROWS == column // here % ROWS, lhs, 0.0).astype(BF16)
     places = [(l, z) for l in range(layers) for z in range(0, nz, ROWS)]
     stores = []
-
-    def add(blocks, columns, base, done):
-        for p in range(0, len(places), 2):
-            pair = places[p : p + 2]
-            sides = []
-            for l, z in pair:
-                first = l * nz + z
-                sides.append(jnp.concatenate([b[first : first + ROWS].reshape(ROWS * here, ny) for b in blocks], axis=0))
-            update = jnp.dot(columns, jnp.concatenate(sides, axis=1), preferred_element_type=F32)
-            for i, (l, z) in enumerate(pair):
-                part = update[:, i * ny : (i + 1) * ny]
-                for m in range(here):
-                    out_ref[m, l, z : z + ROWS] = base[m, l, z : z + ROWS] + part[m * ROWS : (m + 1) * ROWS]
-                if done and z + ROWS == nz:
-                    stores.append(pltpu.make_async_copy(out_ref.at[:, l], out_hbm.at[:, l], sems.at[l]))
-                    stores[-1].start()
-
-    split = 3 * here * ROWS
-    add((mine_ref, beside_ref, over_ref), lhs[:, :split], prior_ref, False)
-    fetch.wait()
-    add((far_ref,), lhs[:, split:], out_ref, True)
+    for p in range(0, len(places), 2):
+        pair = places[p : p + 2]
+        sides = []
+        for l, z in pair:
+            first = l * nz + z
+            sides.append(jnp.concatenate([b[first : first + ROWS].reshape(ROWS * here, ny) for b in blocks], axis=0))
+        update = jnp.dot(lhs, jnp.concatenate(sides, axis=1), preferred_element_type=F32)
+        for i, (l, z) in enumerate(pair):
+            part = update[:, i * ny : (i + 1) * ny]
+            for m in range(here):
+                out_ref[m, l, z : z + ROWS] = prior_ref[m, l, z : z + ROWS] + part[m * ROWS : (m + 1) * ROWS]
+            if z + ROWS == nz:
+                stores.append(pltpu.make_async_copy(out_ref.at[:, l], out_hbm.at[:, l], sems.at[l]))
+                stores[-1].start()
     for store in stores:
         store.wait()
 
@@ -552,14 +544,10 @@
     layers = prior.shape[1]
     return pl.pallas_call(
         update_kernel,
-        in_specs=[VMEM] * 5 + [pl.BlockSpec(memory_space=pl.ANY)],
+        in_specs=[VMEM] * 6,
         out_specs=pl.BlockSpec(memory_space=pltpu.HBM),
         out_shape=jax.ShapeDtypeStruct(prior.shape, F32),
-        scratch_shapes=[
-            pltpu.VMEM(mine.shape, BF16),
-            pltpu.VMEM(prior.shape, F32),
-            pltpu.SemaphoreType.DMA((layers + 1,)),
-        ],
+        scratch_shapes=[pltpu.VMEM(prior.shape, F32), pltpu.SemaphoreType.DMA((layers,))],
         compiler_params=params(),
         name="update",
     )(weights, prior, mine, beside, over, far)

time: 62.4 us -> 61.4 us (0.984)
  Pallas kernels: 21.2 us -> 20 us
where the time goes in v8:
time: 61.4 us; the launch traced here: 61.1 us
  starting transfers between devices  29 us (47%)
  Pallas kernels  20 us (33%)
  waiting for transfers between devices  10.4 us (17%)
  between operations  0.85 us (1%)
  local copies, waits for them, and re-layouts  0.73 us (1%)
    ppermute x4, starting transfers between devices, swap(): return lax.ppermute(x, 'tile', pairs + [(b, a) for a, b in pairs])  13 us
    pallas_call x2, Pallas kernels, sweeps(): pl.pallas_call(functools.partial(sweep_kernel, chunk), grid=(STEPS,), in_...  10.9 us
    all_to_all x1, starting transfers between devices, per_device(): vals = lax.all_to_all(payload, ('tile', 'mem'), 0, 0, tiled=True)  10.7 us
    ppermute x5, starting transfers between devices, across(): return lax.ppermute(x, 'mem', [(i, i ^ bits) for i in range(groups)])  5.35 us
    ppermute x4, waiting for transfers between devices, swap(): return lax.ppermute(x, 'tile', pairs + [(b, a) for a, b in pairs])  4.87 us
    all_to_all x1, waiting for transfers between devices, per_device(): vals = lax.all_to_all(payload, ('tile', 'mem'), 0, 0, tiled=True)  4.6 us
    pallas_call x1, Pallas kernels, probes(): pl.pallas_call(functools.partial(probe_kernel, devices), in_specs=[SMEM]...  2.28 us
    pallas_call x1, Pallas kernels, solve(): pl.pallas_call(functools.partial(solve_kernel, members, here), in_specs=[...  2.01 us
  transfers between devices with their start and end apart: 10, of which 5 were waited for; matrix products, arithmetic and copies ran while one was open for 0% of the time, Pallas kernels for 26%

profile of v8, /device:TPU:1, one launch (start us, length us, event | category | flops | bytes accessed | tf_op | source)
XLA Modules:
  0.0 61.1 jit_solution(5595050901875870934)
XLA Ops:
  0.6 1.9 %encode.1 = (bf16[28,48,128]{2,1,0:T(8,128)(2,1)S(1)}, bf16[28,48,128]{2,1,0:T(8,128)(2,1)S(1)}, bf16[24,48,128]{2,1,0:T(8,128)(2,1)S(1)}, bf16[24,48,128]{2,1,0:T(8,128)(2,1)S(1)}) custom-call(s32[1]{0:T(128)} %bitcast.odd_ref, f32[16,4,48,128]{3,2,1,0:T(8,128)} %prior_hbm.3, f32[4,48,128]{2,1,0:T(8,128)} %flow_ref.3, f32[4,48,128]{2,1,0:T(8,128)} %visc_ref.5), custom_call_target="tpu_custom_call" | custom-call | tf_op jit(solution)/shard_map/encode/pallas_call | solution.py:92
  2.6 11.4 %collective-permute-start.3 = (bf16[28,48,128]{2,1,0:T(8,128)(2,1)S(1)}, bf16[28,48,128]{2,1,0:T(8,128)(2,1)S(1)}, u32[]{:S(2)}, u32[]{:S(2)}) collective-permute-start(bf16[28,48,128]{2,1,0:T(8,128)(2,1)S(1)} %get-tuple-element.22), channel_id=1, source_target_pairs={{4,8},{12,16},{20,24},{28,32},{36,40},{44,48},{52,56},{60,64},{68,... | collective-permute-start | bytes 1032200 | tf_op jit(solution)/shard_map/ppermute | solution.py:566
  14.0 1.5 %collective-permute-start = (bf16[24,48,128]{2,1,0:T(8,128)(2,1)S(1)}, bf16[24,48,128]{2,1,0:T(8,128)(2,1)S(1)}, u32[]{:S(2)}, u32[]{:S(2)}) collective-permute-start(bf16[24,48,128]{2,1,0:T(8,128)(2,1)S(1)} %get-tuple-element.19), channel_id=1, source_target_pairs={{0,4},{8,12},{16,20},{24,28},{32,36},{40,44},{48,52},{56,60},{64,6... | collective-permute-start | bytes 884744 | tf_op jit(solution)/shard_map/ppermute | solution.py:566
  15.5 0.1 collective-permute-start.1
  15.6 0.1 total.1.a_ref
  15.6 1.6 %collective-permute-start.4 = (f32[4,48,128]{2,1,0:T(8,128)S(1)}, f32[4,48,128]{2,1,0:T(8,128)S(1)}, u32[]{:S(2)}, u32[]{:S(2)}) collective-permute-start(f32[4,48,128]{2,1,0:T(8,128)S(1)} %total.1.a_ref), channel_id=1, source_target_pairs={{0,1},{1,0},{2,3},{3,2},{4,5},{5,4},{6,7},{7,6},{8,9},{9,8},{10,11... | collective-permute-start | bytes 294920 | tf_op jit(solution)/shard_map/ppermute | solution.py:569
  17.2 0.9 %collective-permute-done.4.b_ref = f32[4,48,128]{2,1,0:T(8,128)S(1)} collective-permute-done((f32[4,48,128]{2,1,0:T(8,128)S(1)}, f32[4,48,128]{2,1,0:T(8,128)S(1)}, u32[]{:S(2)}, u32[]{:S(2)}) %collective-permute-start.4) | collective-permute-done | bytes 98336 | tf_op jit(solution)/shard_map/ppermute | solution.py:569
  18.2 0.4 collective-permute-start.5
  18.6 0.5 slots.1
  19.1 2.6 %collective-permute-done.3.outer_ref = bf16[28,48,128]{2,1,0:T(8,128)(2,1)S(1)} collective-permute-done((bf16[28,48,128]{2,1,0:T(8,128)(2,1)S(1)}, bf16[28,48,128]{2,1,0:T(8,128)(2,1)S(1)}, u32[]{:S(2)}, u32[]{:S(2)}) %collective-permute-start.3) | collective-permute-done | bytes 344096 | tf_op jit(solution)/shard_map/ppermute | solution.py:566
  21.8 0.8 %collective-permute-done.2.inner_ref = bf16[28,48,128]{2,1,0:T(8,128)(2,1)S(1)} collective-permute-done((bf16[28,48,128]{2,1,0:T(8,128)(2,1)S(1)}, bf16[28,48,128]{2,1,0:T(8,128)(2,1)S(1)}, u32[]{:S(2)}, u32[]{:S(2)}) %collective-permute-start.2) | collective-permute-done | bytes 344096 | tf_op jit(solution)/shard_map/ppermute | solution.py:566
  22.6 4.9 %sweeps0.1 = (f32[16,4,48,128]{3,2,1,0:T(8,128)}, f32[64,128]{1,0:T(8,128)S(1)}, f32[10,64,128]{2,1,0:T(8,128)S(1)}, f32[10,64,128]{2,1,0:T(8,128)S(1)}) custom-call(s32[1]{0:T(128)} %bitcast.odd_ref, s32[1,4]{1,0:T(1,128)S(1)} %copy-done.13, f32[16,4,48,128]{3,2,1,0:T(8,128)S(1)} %copy-done, f32[4,48,128]{2,1,0:T(8,128)S(1)} %copy-done.6, ...), custom_call_target="tpu_custom_call" | custom-call | tf_op jit(solution)/shard_map/sweeps0/pallas_call | solution.py:365
  27.5 1.4 %collective-permute-done.inner_ref.refs_1_ = bf16[24,48,128]{2,1,0:T(8,128)(2,1)S(1)} collective-permute-done((bf16[24,48,128]{2,1,0:T(8,128)(2,1)S(1)}, bf16[24,48,128]{2,1,0:T(8,128)(2,1)S(1)}, u32[]{:S(2)}, u32[]{:S(2)}) %collective-permute-start) | collective-permute-done | bytes 294944 | tf_op jit(solution)/shard_map/ppermute | solution.py:566
  28.9 0.7 %anomalies.1.refs_0_ = bf16[192,16,128]{2,1,0:T(8,128)(2,1)S(1)} custom-call(f32[16,4,48,128]{3,2,1,0:T(8,128)S(1)} %copy-done, f32[4,48,128]{2,1,0:T(8,128)S(1)} %pair_sum.1.a_ref, f32[4,48,128]{2,1,0:T(8,128)S(1)} %collective-permute-done.5.b_ref, f32[64,128]{1,0:T(8,128)S(1)} %get-tuple-element.26.rows_in.refs_0_, ...), custom_call_target="tpu_custom_call" | custom-call | tf_op jit(solution)/shard_map/anomalies/pallas_call | solution.py:391
  29.6 0.4 collective-permute-start.7
  30.1 2.3 %probes.1 = (f32[256,128]{1,0:T(8,128)S(1)}, f32[8,128]{1,0:T(8,128)S(1)}) custom-call(s32[1]{0:T(128)} %bitcast.odd_ref, s32[1,4]{1,0:T(1,128)S(1)} %copy-done.13, f32[16,4,48,128]{3,2,1,0:T(8,128)S(1)} %copy-done, f32[4,48,128]{2,1,0:T(8,128)S(1)} %copy-done.3, bf16[24,48,128]{2,1,0:T(8,128)(2,1)S(1)} %collective-permute-done.inner_ref.refs_1_, ...), custom_call_target="tpu_custom_call" | custom-call | tf_op jit(solution)/shard_map/probes/pallas_call | solution.py:237
  32.4 0.6 %copy-done.11 = f32[256,128]{1,0:T(8,128)} copy-done((f32[256,128]{1,0:T(8,128)}, f32[256,128]{1,0:T(8,128)S(1)}, u32[]{:S(2)}) %copy-start.11) | copy-done | bytes 131096
  33.0 10.7 %all-to-all-start = ((f32[256,1,128]{2,1,0:T(1,128)}), f32[256,1,128]{2,1,0:T(1,128)S(1)}, u32[]{:S(2)}, u32[]{:S(2)}) async-start(f32[256,1,128]{2,1,0:T(1,128)} %bitcast.11), calls=%async_computation | async-start | bytes 262144 | tf_op jit(solution)/shard_map/all_to_all | solution.py:584
  43.7 2.2 %collective-permute-start.6 = (bf16[192,16,128]{2,1,0:T(8,128)(2,1)S(1)}, bf16[192,16,128]{2,1,0:T(8,128)(2,1)S(1)}, u32[]{:S(2)}, u32[]{:S(2)}) collective-permute-start(bf16[192,16,128]{2,1,0:T(8,128)(2,1)S(1)} %anomalies.1.refs_0_), channel_id=1, source_target_pairs={{0,1},{1,0},{2,3},{3,2},{4,5},{5,4},{6,7},{7,6},{8,9},{9,8},{10,11... | collective-permute-start | bytes 2359304 | tf_op jit(solution)/shard_map/ppermute | solution.py:569
  46.0 6.0 %sweeps1.1 = (f32[16,4,48,128]{3,2,1,0:T(8,128)}, f32[8,128]{1,0:T(8,128)S(1)}) custom-call(s32[1]{0:T(128)} %bitcast.odd_ref, s32[1,4]{1,0:T(1,128)S(1)} %copy-done.13, f32[16,4,48,128]{3,2,1,0:T(8,128)} %prior_hbm.3, f32[4,48,128]{2,1,0:T(8,128)} %flow_ref.3, f32[4,48,128]{2,1,0:T(8,128)S(1)} %copy-done.3, ...), custom_call_target="tpu_custom_call", output_to_operand_aliasing={{0}: (10, {})} | custom-call | tf_op jit(solution)/shard_map/sweeps1/pallas_call | solution.py:365
  52.0 4.6 %all-to-all-done = f32[256,1,128]{2,1,0:T(1,128)S(1)} async-done(((f32[256,1,128]{2,1,0:T(1,128)}), f32[256,1,128]{2,1,0:T(1,128)S(1)}, u32[]{:S(2)}, u32[]{:S(2)}) %all-to-all-start) | async-done | bytes 131104 | tf_op jit(solution)/shard_map/all_to_all | solution.py:584
  56.6 0.7 %collective-permute-start.8 = (bf16[192,16,128]{2,1,0:T(8,128)(2,1)S(1)}, bf16[192,16,128]{2,1,0:T(8,128)(2,1)S(1)}, u32[]{:S(2)}, u32[]{:S(2)}) collective-permute-start(bf16[192,16,128]{2,1,0:T(8,128)(2,1)S(1)} %hold.1.refs_2_), channel_id=1, source_target_pairs={{0,1},{1,0},{2,3},{3,2},{4,5},{5,4},{6,7},{7,6},{8,9},{9,8},{10,11... | collective-permute-start | bytes 2359304 | tf_op jit(solution)/shard_map/ppermute | solution.py:569
  57.3 2.0 %solve.1 = (bf16[16,64]{1,0:T(8,128)(2,1)S(1)}, bf16[192,16,128]{2,1,0:T(8,128)(2,1)S(1)}, f32[16,4,48,128]{3,2,1,0:T(8,128)S(1)}) custom-call(s32[1]{0:T(128)} %bitcast.4.me_ref, f32[256,128]{1,0:T(8,128)S(1)} %bitcast.10, f32[256,128]{1,0:T(8,128)S(1)} %copy-done.8, f32[256,128]{1,0:T(8,128)S(1)} %copy-done.10, ...), custom_call_target="tpu_custom_call" | custom-call | tf_op jit(solution)/shard_map/solve/pallas_call | solution.py:493
  59.4 1.7 %update.1 = f32[16,4,48,128]{3,2,1,0:T(8,128)} custom-call(bf16[16,64]{1,0:T(8,128)(2,1)S(1)} %get-tuple-element.32.weights_ref, f32[16,4,48,128]{3,2,1,0:T(8,128)S(1)} %get-tuple-element.33.prior_ref, bf16[192,16,128]{2,1,0:T(8,128)(2,1)S(1)} %anomalies.1.refs_0_, bf16[192,16,128]{2,1,0:T(8,128)(2,1)S(1)} %get-tuple-element.34.refs_1_, ...), custom_call_target="tpu_custom_call" | custom-call | tf_op jit(solution)/shard_map/update/pallas_call | solution.py:545
  (41 shorter events, 0.1 us)
Async XLA Ops:
  0.6 14.9 %copy-start = (f32[16,4,48,128]{3,2,1,0:T(8,128)S(1)}, f32[16,4,48,128]{3,2,1,0:T(8,128)}, u32[]{:S(2)}) copy-start(f32[16,4,48,128]{3,2,1,0:T(8,128)} %prior_hbm.3) | copy-start | bytes 4718596
  2.5 16.1 %copy-start.12 = (f32[64,256]{1,0:T(8,128)S(1)}, f32[64,256]{1,0:T(8,128)}, u32[]{:S(2)}) copy-start(f32[64,256]{1,0:T(8,128)} %noise_ref.1) | copy-start | bytes 196612
  2.5 16.1 %copy-start.14 = (s32[256]{0:T(256)S(1)}, s32[256]{0:T(256)}, u32[]{:S(2)}) copy-start(s32[256]{0:T(256)} %param.12) | copy-start | bytes 3076
  2.5 16.1 %copy-start.15 = (f32[256]{0:T(256)S(1)}, f32[256]{0:T(256)}, u32[]{:S(2)}) copy-start(f32[256]{0:T(256)} %param.13) | copy-start | bytes 3076
  2.5 16.1 %copy-start.16 = (f32[256]{0:T(256)S(1)}, f32[256]{0:T(256)}, u32[]{:S(2)}) copy-start(f32[256]{0:T(256)} %param.14) | copy-start | bytes 3076
  2.6 20.0 %copy-start.3 = (f32[4,48,128]{2,1,0:T(8,128)S(1)}, f32[4,48,128]{2,1,0:T(8,128)}, u32[]{:S(2)}) copy-start(f32[4,48,128]{2,1,0:T(8,128)} %visc_ref.5) | copy-start | bytes 294916
  2.6 20.0 %copy-start.6 = (f32[4,48,128]{2,1,0:T(8,128)S(1)}, f32[4,48,128]{2,1,0:T(8,128)}, u32[]{:S(2)}) copy-start(f32[4,48,128]{2,1,0:T(8,128)} %flow_ref.3) | copy-start | bytes 294916
  2.6 20.0 %copy-start.13 = (s32[1,4]{1,0:T(1,128)S(1)}, s32[1,4]{1,0:T(1,128)}, u32[]{:S(2)}) copy-start(s32[1,4]{1,0:T(1,128)} %cells_ref.5) | copy-start | bytes 52
  2.6 19.2 %collective-permute-start.3 = (bf16[28,48,128]{2,1,0:T(8,128)(2,1)S(1)}, bf16[28,48,128]{2,1,0:T(8,128)(2,1)S(1)}, u32[]{:S(2)}, u32[]{:S(2)}) collective-permute-start(bf16[28,48,128]{2,1,0:T(8,128)(2,1)S(1)} %get-tuple-element.22), channel_id=1, source_target_pairs={{4,8},{12,16},{20,24},{28,32},{36,40},{44,48},{52,56},{60,64},{68,... | collective-permute-start | bytes 1032200 | tf_op jit(solution)/shard_map/ppermute | solution.py:566
  14.0 8.6 %collective-permute-start.2 = (bf16[28,48,128]{2,1,0:T(8,128)(2,1)S(1)}, bf16[28,48,128]{2,1,0:T(8,128)(2,1)S(1)}, u32[]{:S(2)}, u32[]{:S(2)}) collective-permute-start(bf16[28,48,128]{2,1,0:T(8,128)(2,1)S(1)} %get-tuple-element.21.after), channel_id=1, source_target_pairs={{0,4},{8,12},{16,20},{24,28},{32,36},{40,44},{48,52},{56,60},{64,6... | collective-permute-start | bytes 1032200 | tf_op jit(solution)/shard_map/ppermute | solution.py:566
  14.0 14.9 %collective-permute-start = (bf16[24,48,128]{2,1,0:T(8,128)(2,1)S(1)}, bf16[24,48,128]{2,1,0:T(8,128)(2,1)S(1)}, u32[]{:S(2)}, u32[]{:S(2)}) collective-permute-start(bf16[24,48,128]{2,1,0:T(8,128)(2,1)S(1)} %get-tuple-element.19), channel_id=1, source_target_pairs={{0,4},{8,12},{16,20},{24,28},{32,36},{40,44},{48,52},{56,60},{64,6... | collective-permute-start | bytes 884744 | tf_op jit(solution)/shard_map/ppermute | solution.py:566
  15.5 13.5 %collective-permute-start.1 = (bf16[24,48,128]{2,1,0:T(8,128)(2,1)S(1)}, bf16[24,48,128]{2,1,0:T(8,128)(2,1)S(1)}, u32[]{:S(2)}, u32[]{:S(2)}) collective-permute-start(bf16[24,48,128]{2,1,0:T(8,128)(2,1)S(1)} %get-tuple-element.20), channel_id=1, source_target_pairs={{4,8},{12,16},{20,24},{28,32},{36,40},{44,48},{52,56},{60,64},{68,... | collective-permute-start | bytes 884744 | tf_op jit(solution)/shard_map/ppermute | solution.py:566
  15.6 2.5 %collective-permute-start.4 = (f32[4,48,128]{2,1,0:T(8,128)S(1)}, f32[4,48,128]{2,1,0:T(8,128)S(1)}, u32[]{:S(2)}, u32[]{:S(2)}) collective-permute-start(f32[4,48,128]{2,1,0:T(8,128)S(1)} %total.1.a_ref), channel_id=1, source_target_pairs={{0,1},{1,0},{2,3},{3,2},{4,5},{5,4},{6,7},{7,6},{8,9},{9,8},{10,11... | collective-permute-start | bytes 294920 | tf_op jit(solution)/shard_map/ppermute | solution.py:569
  18.2 9.3 %collective-permute-start.5 = (f32[4,48,128]{2,1,0:T(8,128)S(1)}, f32[4,48,128]{2,1,0:T(8,128)S(1)}, u32[]{:S(2)}, u32[]{:S(2)}) collective-permute-start(f32[4,48,128]{2,1,0:T(8,128)S(1)} %pair_sum.1.a_ref), channel_id=1, source_target_pairs={{0,2},{1,3},{2,0},{3,1},{4,6},{5,7},{6,4},{7,5},{8,10},{9,11},{10,... | collective-permute-start | bytes 294920 | tf_op jit(solution)/shard_map/ppermute | solution.py:569
  19.1 10.5 %copy-start.7 = (f32[256,128]{1,0:T(8,128)}, f32[256,128]{1,0:T(8,128)S(1)}, u32[]{:S(2)}) copy-start(f32[256,128]{1,0:T(8,128)S(1)} %get-tuple-element.23.rest_0_.seen_ref) | copy-start | bytes 393220
  19.1 10.5 %copy-start.9 = (f32[256,128]{1,0:T(8,128)}, f32[256,128]{1,0:T(8,128)S(1)}, u32[]{:S(2)}) copy-start(f32[256,128]{1,0:T(8,128)S(1)} %get-tuple-element.31.weight_ref) | copy-start | bytes 393220
  27.5 2.5 %copy-start.4 = (f32[10,64,128]{2,1,0:T(8,128)}, f32[10,64,128]{2,1,0:T(8,128)S(1)}, u32[]{:S(2)}) copy-start(f32[10,64,128]{2,1,0:T(8,128)S(1)} %get-tuple-element.24.lap0.rest_0_) | copy-start | bytes 983044
  27.5 2.5 %copy-start.5 = (f32[10,64,128]{2,1,0:T(8,128)}, f32[10,64,128]{2,1,0:T(8,128)S(1)}, u32[]{:S(2)}) copy-start(f32[10,64,128]{2,1,0:T(8,128)S(1)} %get-tuple-element.25.adv0.rest_1_) | copy-start | bytes 983044
  29.6 27.0 %collective-permute-start.7 = (bf16[192,16,128]{2,1,0:T(8,128)(2,1)S(1)}, bf16[192,16,128]{2,1,0:T(8,128)(2,1)S(1)}, u32[]{:S(2)}, u32[]{:S(2)}) collective-permute-start(bf16[192,16,128]{2,1,0:T(8,128)(2,1)S(1)} %anomalies.1.refs_0_), channel_id=1, source_target_pairs={{0,2},{1,3},{2,0},{3,1},{4,6},{5,7},{6,4},{7,5},{8,10},{9,11},{10,... | collective-permute-start | bytes 2359304 | tf_op jit(solution)/shard_map/ppermute | solution.py:569
  33.0 23.6 %all-to-all-start = ((f32[256,1,128]{2,1,0:T(1,128)}), f32[256,1,128]{2,1,0:T(1,128)S(1)}, u32[]{:S(2)}, u32[]{:S(2)}) async-start(f32[256,1,128]{2,1,0:T(1,128)} %bitcast.11), calls=%async_computation | async-start | bytes 262144 | tf_op jit(solution)/shard_map/all_to_all | solution.py:584
  43.7 13.6 %collective-permute-start.6 = (bf16[192,16,128]{2,1,0:T(8,128)(2,1)S(1)}, bf16[192,16,128]{2,1,0:T(8,128)(2,1)S(1)}, u32[]{:S(2)}, u32[]{:S(2)}) collective-permute-start(bf16[192,16,128]{2,1,0:T(8,128)(2,1)S(1)} %anomalies.1.refs_0_), channel_id=1, source_target_pairs={{0,1},{1,0},{2,3},{3,2},{4,5},{5,4},{6,7},{7,6},{8,9},{9,8},{10,11... | collective-permute-start | bytes 2359304 | tf_op jit(solution)/shard_map/ppermute | solution.py:569
  52.0 5.3 %copy-start.8 = (f32[256,128]{1,0:T(8,128)S(1)}, f32[256,128]{1,0:T(8,128)}, u32[]{:S(2)}) copy-start(f32[256,128]{1,0:T(8,128)} %copy-done.7) | copy-start | bytes 393220
  52.0 5.3 %copy-start.10 = (f32[256,128]{1,0:T(8,128)S(1)}, f32[256,128]{1,0:T(8,128)}, u32[]{:S(2)}) copy-start(f32[256,128]{1,0:T(8,128)} %copy-done.9) | copy-start | bytes 393220
  56.6 2.7 %collective-permute-start.8 = (bf16[192,16,128]{2,1,0:T(8,128)(2,1)S(1)}, bf16[192,16,128]{2,1,0:T(8,128)(2,1)S(1)}, u32[]{:S(2)}, u32[]{:S(2)}) collective-permute-start(bf16[192,16,128]{2,1,0:T(8,128)(2,1)S(1)} %hold.1.refs_2_), channel_id=1, source_target_pairs={{0,1},{1,0},{2,3},{3,2},{4,5},{5,4},{6,7},{7,6},{8,9},{9,8},{10,11... | collective-permute-start | bytes 2359304 | tf_op jit(solution)/shard_map/ppermute | solution.py:569
  (3 other events, 2.9 us)

commit v9 on v8

--- a/solution.py
+++ b/solution.py
@@ -468,19 +468,21 @@
     half = 0.5 * jnp.max(jnp.sum(jnp.abs(gram), axis=1))
     alpha = 1.0 / (members - 1.0 + half)
     diagonal = lax.broadcasted_iota(jnp.int32, gram.shape, 0) == lax.broadcasted_iota(jnp.int32, gram.shape, 1)
-    error = jnp.where(diagonal, alpha * half, 0.0) - alpha * gram
+    error = (jnp.where(diagonal, alpha * half, 0.0) - alpha * gram)[:members]
+    rest = jnp.zeros((ny - members, 2 * ny), F32)
 
     def more(state):
         return (state[0] > 2e-6) & (state[1] < 40)
 
     def double(state):
         size, count, power_of, x = state
-        both = dot(power_of, jnp.concatenate([power_of, x], axis=1), ((1,), (0,)))
+        right = jnp.concatenate([jnp.concatenate([power_of, x], axis=1), rest], axis=0)
+        both = dot(power_of, right, ((1,), (0,)))
         return size * size, count + 1, both[:, :ny], x + both[:, ny:]
 
-    x = lax.while_loop(more, double, (half * alpha, 0, error, alpha * rhs))[3]
+    x = lax.while_loop(more, double, (half * alpha, 0, error, alpha * rhs[:members]))[3]
     me = me_ref[0]
-    scr[...] = x
+    scr[0:members] = x
     order = [scr[pl.ds(pl.multiple_of((me ^ g) * here, here), here), :] for g in range(groups)]
     scr[...] = jnp.concatenate(order + [jnp.zeros((ny - members, ny), F32)], axis=0).T
     mine = scr[pl.ds(pl.multiple_of(me * here, here), here), :]

time: 61.4 us -> 61.2 us (level)
  no operation moved by 1% of the time
where the time goes in v9:
time: 61.2 us
  starting transfers between devices  29 us (47%)
  Pallas kernels  20.1 us (33%)
  waiting for transfers between devices  10.4 us (17%)
  between operations  0.85 us (1%)
  local copies, waits for them, and re-layouts  0.73 us (1%)
    ppermute x4, starting transfers between devices, swap(): return lax.ppermute(x, 'tile', pairs + [(b, a) for a, b in pairs])  13 us
    pallas_call x2, Pallas kernels, sweeps(): pl.pallas_call(functools.partial(sweep_kernel, chunk), grid=(STEPS,), in_...  10.9 us
    all_to_all x1, starting transfers between devices, per_device(): vals = lax.all_to_all(payload, ('tile', 'mem'), 0, 0, tiled=True)  10.7 us
    ppermute x5, starting transfers between devices, across(): return lax.ppermute(x, 'mem', [(i, i ^ bits) for i in range(groups)])  5.35 us
    ppermute x4, waiting for transfers between devices, swap(): return lax.ppermute(x, 'tile', pairs + [(b, a) for a, b in pairs])  4.88 us
    all_to_all x1, waiting for transfers between devices, per_device(): vals = lax.all_to_all(payload, ('tile', 'mem'), 0, 0, tiled=True)  4.6 us
    pallas_call x1, Pallas kernels, probes(): pl.pallas_call(functools.partial(probe_kernel, devices), in_specs=[SMEM]...  2.28 us
    pallas_call x1, Pallas kernels, solve(): pl.pallas_call(functools.partial(solve_kernel, members, here), in_specs=[...  2.11 us
  transfers between devices with their start and end apart: 10, of which 5 were waited for; matrix products, arithmetic and copies ran while one was open for 0% of the time, Pallas kernels for 26%

profile of v9, /device:TPU:1, one launch (start us, length us, event | category | flops | bytes accessed | tf_op | source)
XLA Modules:
  0.0 61.2 jit_solution(5048988997572980726)
XLA Ops:
  0.6 1.9 %encode.1 = (bf16[28,48,128]{2,1,0:T(8,128)(2,1)S(1)}, bf16[28,48,128]{2,1,0:T(8,128)(2,1)S(1)}, bf16[24,48,128]{2,1,0:T(8,128)(2,1)S(1)}, bf16[24,48,128]{2,1,0:T(8,128)(2,1)S(1)}) custom-call(s32[1]{0:T(128)} %bitcast.odd_ref, f32[16,4,48,128]{3,2,1,0:T(8,128)} %prior_hbm.3, f32[4,48,128]{2,1,0:T(8,128)} %flow_ref.3, f32[4,48,128]{2,1,0:T(8,128)} %visc_ref.5), custom_call_target="tpu_custom_call" | custom-call | tf_op jit(solution)/shard_map/encode/pallas_call | solution.py:92
  2.6 11.4 %collective-permute-start.3 = (bf16[28,48,128]{2,1,0:T(8,128)(2,1)S(1)}, bf16[28,48,128]{2,1,0:T(8,128)(2,1)S(1)}, u32[]{:S(2)}, u32[]{:S(2)}) collective-permute-start(bf16[28,48,128]{2,1,0:T(8,128)(2,1)S(1)} %get-tuple-element.22), channel_id=1, source_target_pairs={{4,8},{12,16},{20,24},{28,32},{36,40},{44,48},{52,56},{60,64},{68,... | collective-permute-start | bytes 1032200 | tf_op jit(solution)/shard_map/ppermute | solution.py:568
  14.0 1.5 %collective-permute-start = (bf16[24,48,128]{2,1,0:T(8,128)(2,1)S(1)}, bf16[24,48,128]{2,1,0:T(8,128)(2,1)S(1)}, u32[]{:S(2)}, u32[]{:S(2)}) collective-permute-start(bf16[24,48,128]{2,1,0:T(8,128)(2,1)S(1)} %get-tuple-element.19), channel_id=1, source_target_pairs={{0,4},{8,12},{16,20},{24,28},{32,36},{40,44},{48,52},{56,60},{64,6... | collective-permute-start | bytes 884744 | tf_op jit(solution)/shard_map/ppermute | solution.py:568
  15.5 0.1 collective-permute-start.1
  15.6 0.1 total.1.a_ref
  15.6 1.6 %collective-permute-start.4 = (f32[4,48,128]{2,1,0:T(8,128)S(1)}, f32[4,48,128]{2,1,0:T(8,128)S(1)}, u32[]{:S(2)}, u32[]{:S(2)}) collective-permute-start(f32[4,48,128]{2,1,0:T(8,128)S(1)} %total.1.a_ref), channel_id=1, source_target_pairs={{0,1},{1,0},{2,3},{3,2},{4,5},{5,4},{6,7},{7,6},{8,9},{9,8},{10,11... | collective-permute-start | bytes 294920 | tf_op jit(solution)/shard_map/ppermute | solution.py:571
  17.2 0.9 %collective-permute-done.4.b_ref = f32[4,48,128]{2,1,0:T(8,128)S(1)} collective-permute-done((f32[4,48,128]{2,1,0:T(8,128)S(1)}, f32[4,48,128]{2,1,0:T(8,128)S(1)}, u32[]{:S(2)}, u32[]{:S(2)}) %collective-permute-start.4) | collective-permute-done | bytes 98336 | tf_op jit(solution)/shard_map/ppermute | solution.py:571
  18.2 0.4 collective-permute-start.5
  18.6 0.5 slots.1
  19.1 2.6 %collective-permute-done.3.outer_ref = bf16[28,48,128]{2,1,0:T(8,128)(2,1)S(1)} collective-permute-done((bf16[28,48,128]{2,1,0:T(8,128)(2,1)S(1)}, bf16[28,48,128]{2,1,0:T(8,128)(2,1)S(1)}, u32[]{:S(2)}, u32[]{:S(2)}) %collective-permute-start.3) | collective-permute-done | bytes 344096 | tf_op jit(solution)/shard_map/ppermute | solution.py:568
  21.8 0.8 %collective-permute-done.2.inner_ref = bf16[28,48,128]{2,1,0:T(8,128)(2,1)S(1)} collective-permute-done((bf16[28,48,128]{2,1,0:T(8,128)(2,1)S(1)}, bf16[28,48,128]{2,1,0:T(8,128)(2,1)S(1)}, u32[]{:S(2)}, u32[]{:S(2)}) %collective-permute-start.2) | collective-permute-done | bytes 344096 | tf_op jit(solution)/shard_map/ppermute | solution.py:568
  22.6 4.9 %sweeps0.1 = (f32[16,4,48,128]{3,2,1,0:T(8,128)}, f32[64,128]{1,0:T(8,128)S(1)}, f32[10,64,128]{2,1,0:T(8,128)S(1)}, f32[10,64,128]{2,1,0:T(8,128)S(1)}) custom-call(s32[1]{0:T(128)} %bitcast.odd_ref, s32[1,4]{1,0:T(1,128)S(1)} %copy-done.13, f32[16,4,48,128]{3,2,1,0:T(8,128)S(1)} %copy-done, f32[4,48,128]{2,1,0:T(8,128)S(1)} %copy-done.6, ...), custom_call_target="tpu_custom_call" | custom-call | tf_op jit(solution)/shard_map/sweeps0/pallas_call | solution.py:365
  27.5 1.4 %collective-permute-done.inner_ref.refs_1_ = bf16[24,48,128]{2,1,0:T(8,128)(2,1)S(1)} collective-permute-done((bf16[24,48,128]{2,1,0:T(8,128)(2,1)S(1)}, bf16[24,48,128]{2,1,0:T(8,128)(2,1)S(1)}, u32[]{:S(2)}, u32[]{:S(2)}) %collective-permute-start) | collective-permute-done | bytes 294944 | tf_op jit(solution)/shard_map/ppermute | solution.py:568
  28.9 0.7 %anomalies.1.refs_0_ = bf16[192,16,128]{2,1,0:T(8,128)(2,1)S(1)} custom-call(f32[16,4,48,128]{3,2,1,0:T(8,128)S(1)} %copy-done, f32[4,48,128]{2,1,0:T(8,128)S(1)} %pair_sum.1.a_ref, f32[4,48,128]{2,1,0:T(8,128)S(1)} %collective-permute-done.5.b_ref, f32[64,128]{1,0:T(8,128)S(1)} %get-tuple-element.26.rows_in.refs_0_, ...), custom_call_target="tpu_custom_call" | custom-call | tf_op jit(solution)/shard_map/anomalies/pallas_call | solution.py:391
  29.6 0.4 collective-permute-start.7
  30.1 2.3 %probes.1 = (f32[256,128]{1,0:T(8,128)S(1)}, f32[8,128]{1,0:T(8,128)S(1)}) custom-call(s32[1]{0:T(128)} %bitcast.odd_ref, s32[1,4]{1,0:T(1,128)S(1)} %copy-done.13, f32[16,4,48,128]{3,2,1,0:T(8,128)S(1)} %copy-done, f32[4,48,128]{2,1,0:T(8,128)S(1)} %copy-done.3, bf16[24,48,128]{2,1,0:T(8,128)(2,1)S(1)} %collective-permute-done.inner_ref.refs_1_, ...), custom_call_target="tpu_custom_call" | custom-call | tf_op jit(solution)/shard_map/probes/pallas_call | solution.py:237
  32.4 0.6 %copy-done.11 = f32[256,128]{1,0:T(8,128)} copy-done((f32[256,128]{1,0:T(8,128)}, f32[256,128]{1,0:T(8,128)S(1)}, u32[]{:S(2)}) %copy-start.11) | copy-done | bytes 131096
  33.0 10.7 %all-to-all-start = ((f32[256,1,128]{2,1,0:T(1,128)}), f32[256,1,128]{2,1,0:T(1,128)S(1)}, u32[]{:S(2)}, u32[]{:S(2)}) async-start(f32[256,1,128]{2,1,0:T(1,128)} %bitcast.11), calls=%async_computation | async-start | bytes 262144 | tf_op jit(solution)/shard_map/all_to_all | solution.py:586
  43.7 2.2 %collective-permute-start.6 = (bf16[192,16,128]{2,1,0:T(8,128)(2,1)S(1)}, bf16[192,16,128]{2,1,0:T(8,128)(2,1)S(1)}, u32[]{:S(2)}, u32[]{:S(2)}) collective-permute-start(bf16[192,16,128]{2,1,0:T(8,128)(2,1)S(1)} %anomalies.1.refs_0_), channel_id=1, source_target_pairs={{0,1},{1,0},{2,3},{3,2},{4,5},{5,4},{6,7},{7,6},{8,9},{9,8},{10,11... | collective-permute-start | bytes 2359304 | tf_op jit(solution)/shard_map/ppermute | solution.py:571
  46.0 6.0 %sweeps1.1 = (f32[16,4,48,128]{3,2,1,0:T(8,128)}, f32[8,128]{1,0:T(8,128)S(1)}) custom-call(s32[1]{0:T(128)} %bitcast.odd_ref, s32[1,4]{1,0:T(1,128)S(1)} %copy-done.13, f32[16,4,48,128]{3,2,1,0:T(8,128)} %prior_hbm.3, f32[4,48,128]{2,1,0:T(8,128)} %flow_ref.3, f32[4,48,128]{2,1,0:T(8,128)S(1)} %copy-done.3, ...), custom_call_target="tpu_custom_call", output_to_operand_aliasing={{0}: (10, {})} | custom-call | tf_op jit(solution)/shard_map/sweeps1/pallas_call | solution.py:365
  52.0 4.6 %all-to-all-done = f32[256,1,128]{2,1,0:T(1,128)S(1)} async-done(((f32[256,1,128]{2,1,0:T(1,128)}), f32[256,1,128]{2,1,0:T(1,128)S(1)}, u32[]{:S(2)}, u32[]{:S(2)}) %all-to-all-start) | async-done | bytes 131104 | tf_op jit(solution)/shard_map/all_to_all | solution.py:586
  56.6 0.7 %collective-permute-start.8 = (bf16[192,16,128]{2,1,0:T(8,128)(2,1)S(1)}, bf16[192,16,128]{2,1,0:T(8,128)(2,1)S(1)}, u32[]{:S(2)}, u32[]{:S(2)}) collective-permute-start(bf16[192,16,128]{2,1,0:T(8,128)(2,1)S(1)} %hold.1.refs_2_), channel_id=1, source_target_pairs={{0,1},{1,0},{2,3},{3,2},{4,5},{5,4},{6,7},{7,6},{8,9},{9,8},{10,11... | collective-permute-start | bytes 2359304 | tf_op jit(solution)/shard_map/ppermute | solution.py:571
  57.3 2.1 %solve.1 = (bf16[16,64]{1,0:T(8,128)(2,1)S(1)}, bf16[192,16,128]{2,1,0:T(8,128)(2,1)S(1)}, f32[16,4,48,128]{3,2,1,0:T(8,128)S(1)}) custom-call(s32[1]{0:T(128)} %bitcast.4.me_ref, f32[256,128]{1,0:T(8,128)S(1)} %bitcast.10, f32[256,128]{1,0:T(8,128)S(1)} %copy-done.8, f32[256,128]{1,0:T(8,128)S(1)} %copy-done.10, ...), custom_call_target="tpu_custom_call" | custom-call | tf_op jit(solution)/shard_map/solve/pallas_call | solution.py:495
  59.4 1.7 %update.1 = f32[16,4,48,128]{3,2,1,0:T(8,128)} custom-call(bf16[16,64]{1,0:T(8,128)(2,1)S(1)} %get-tuple-element.32.weights_ref, f32[16,4,48,128]{3,2,1,0:T(8,128)S(1)} %get-tuple-element.33.prior_ref, bf16[192,16,128]{2,1,0:T(8,128)(2,1)S(1)} %anomalies.1.refs_0_, bf16[192,16,128]{2,1,0:T(8,128)(2,1)S(1)} %get-tuple-element.34.refs_1_, ...), custom_call_target="tpu_custom_call" | custom-call | tf_op jit(solution)/shard_map/update/pallas_call | solution.py:547
  (41 shorter events, 0.1 us)
Async XLA Ops:
  0.6 14.9 %copy-start = (f32[16,4,48,128]{3,2,1,0:T(8,128)S(1)}, f32[16,4,48,128]{3,2,1,0:T(8,128)}, u32[]{:S(2)}) copy-start(f32[16,4,48,128]{3,2,1,0:T(8,128)} %prior_hbm.3) | copy-start | bytes 4718596
  2.5 16.1 %copy-start.12 = (f32[64,256]{1,0:T(8,128)S(1)}, f32[64,256]{1,0:T(8,128)}, u32[]{:S(2)}) copy-start(f32[64,256]{1,0:T(8,128)} %noise_ref.1) | copy-start | bytes 196612
  2.5 16.1 %copy-start.14 = (s32[256]{0:T(256)S(1)}, s32[256]{0:T(256)}, u32[]{:S(2)}) copy-start(s32[256]{0:T(256)} %param.12) | copy-start | bytes 3076
  2.5 16.1 %copy-start.15 = (f32[256]{0:T(256)S(1)}, f32[256]{0:T(256)}, u32[]{:S(2)}) copy-start(f32[256]{0:T(256)} %param.13) | copy-start | bytes 3076
  2.5 16.1 %copy-start.16 = (f32[256]{0:T(256)S(1)}, f32[256]{0:T(256)}, u32[]{:S(2)}) copy-start(f32[256]{0:T(256)} %param.14) | copy-start | bytes 3076
  2.6 20.0 %copy-start.3 = (f32[4,48,128]{2,1,0:T(8,128)S(1)}, f32[4,48,128]{2,1,0:T(8,128)}, u32[]{:S(2)}) copy-start(f32[4,48,128]{2,1,0:T(8,128)} %visc_ref.5) | copy-start | bytes 294916
  2.6 20.0 %copy-start.6 = (f32[4,48,128]{2,1,0:T(8,128)S(1)}, f32[4,48,128]{2,1,0:T(8,128)}, u32[]{:S(2)}) copy-start(f32[4,48,128]{2,1,0:T(8,128)} %flow_ref.3) | copy-start | bytes 294916
  2.6 20.0 %copy-start.13 = (s32[1,4]{1,0:T(1,128)S(1)}, s32[1,4]{1,0:T(1,128)}, u32[]{:S(2)}) copy-start(s32[1,4]{1,0:T(1,128)} %cells_ref.5) | copy-start | bytes 52
  2.6 19.2 %collective-permute-start.3 = (bf16[28,48,128]{2,1,0:T(8,128)(2,1)S(1)}, bf16[28,48,128]{2,1,0:T(8,128)(2,1)S(1)}, u32[]{:S(2)}, u32[]{:S(2)}) collective-permute-start(bf16[28,48,128]{2,1,0:T(8,128)(2,1)S(1)} %get-tuple-element.22), channel_id=1, source_target_pairs={{4,8},{12,16},{20,24},{28,32},{36,40},{44,48},{52,56},{60,64},{68,... | collective-permute-start | bytes 1032200 | tf_op jit(solution)/shard_map/ppermute | solution.py:568
  14.0 8.6 %collective-permute-start.2 = (bf16[28,48,128]{2,1,0:T(8,128)(2,1)S(1)}, bf16[28,48,128]{2,1,0:T(8,128)(2,1)S(1)}, u32[]{:S(2)}, u32[]{:S(2)}) collective-permute-start(bf16[28,48,128]{2,1,0:T(8,128)(2,1)S(1)} %get-tuple-element.21.after), channel_id=1, source_target_pairs={{0,4},{8,12},{16,20},{24,28},{32,36},{40,44},{48,52},{56,60},{64,6... | collective-permute-start | bytes 1032200 | tf_op jit(solution)/shard_map/ppermute | solution.py:568
  14.0 14.9 %collective-permute-start = (bf16[24,48,128]{2,1,0:T(8,128)(2,1)S(1)}, bf16[24,48,128]{2,1,0:T(8,128)(2,1)S(1)}, u32[]{:S(2)}, u32[]{:S(2)}) collective-permute-start(bf16[24,48,128]{2,1,0:T(8,128)(2,1)S(1)} %get-tuple-element.19), channel_id=1, source_target_pairs={{0,4},{8,12},{16,20},{24,28},{32,36},{40,44},{48,52},{56,60},{64,6... | collective-permute-start | bytes 884744 | tf_op jit(solution)/shard_map/ppermute | solution.py:568
  15.5 13.5 %collective-permute-start.1 = (bf16[24,48,128]{2,1,0:T(8,128)(2,1)S(1)}, bf16[24,48,128]{2,1,0:T(8,128)(2,1)S(1)}, u32[]{:S(2)}, u32[]{:S(2)}) collective-permute-start(bf16[24,48,128]{2,1,0:T(8,128)(2,1)S(1)} %get-tuple-element.20), channel_id=1, source_target_pairs={{4,8},{12,16},{20,24},{28,32},{36,40},{44,48},{52,56},{60,64},{68,... | collective-permute-start | bytes 884744 | tf_op jit(solution)/shard_map/ppermute | solution.py:568
  15.6 2.5 %collective-permute-start.4 = (f32[4,48,128]{2,1,0:T(8,128)S(1)}, f32[4,48,128]{2,1,0:T(8,128)S(1)}, u32[]{:S(2)}, u32[]{:S(2)}) collective-permute-start(f32[4,48,128]{2,1,0:T(8,128)S(1)} %total.1.a_ref), channel_id=1, source_target_pairs={{0,1},{1,0},{2,3},{3,2},{4,5},{5,4},{6,7},{7,6},{8,9},{9,8},{10,11... | collective-permute-start | bytes 294920 | tf_op jit(solution)/shard_map/ppermute | solution.py:571
  18.2 9.3 %collective-permute-start.5 = (f32[4,48,128]{2,1,0:T(8,128)S(1)}, f32[4,48,128]{2,1,0:T(8,128)S(1)}, u32[]{:S(2)}, u32[]{:S(2)}) collective-permute-start(f32[4,48,128]{2,1,0:T(8,128)S(1)} %pair_sum.1.a_ref), channel_id=1, source_target_pairs={{0,2},{1,3},{2,0},{3,1},{4,6},{5,7},{6,4},{7,5},{8,10},{9,11},{10,... | collective-permute-start | bytes 294920 | tf_op jit(solution)/shard_map/ppermute | solution.py:571
  19.1 10.5 %copy-start.7 = (f32[256,128]{1,0:T(8,128)}, f32[256,128]{1,0:T(8,128)S(1)}, u32[]{:S(2)}) copy-start(f32[256,128]{1,0:T(8,128)S(1)} %get-tuple-element.23.rest_0_.seen_ref) | copy-start | bytes 393220
  19.1 10.5 %copy-start.9 = (f32[256,128]{1,0:T(8,128)}, f32[256,128]{1,0:T(8,128)S(1)}, u32[]{:S(2)}) copy-start(f32[256,128]{1,0:T(8,128)S(1)} %get-tuple-element.31.weight_ref) | copy-start | bytes 393220
  27.5 2.5 %copy-start.4 = (f32[10,64,128]{2,1,0:T(8,128)}, f32[10,64,128]{2,1,0:T(8,128)S(1)}, u32[]{:S(2)}) copy-start(f32[10,64,128]{2,1,0:T(8,128)S(1)} %get-tuple-element.24.lap0.rest_0_) | copy-start | bytes 983044
  27.5 2.5 %copy-start.5 = (f32[10,64,128]{2,1,0:T(8,128)}, f32[10,64,128]{2,1,0:T(8,128)S(1)}, u32[]{:S(2)}) copy-start(f32[10,64,128]{2,1,0:T(8,128)S(1)} %get-tuple-element.25.adv0.rest_1_) | copy-start | bytes 983044
  29.6 26.9 %collective-permute-start.7 = (bf16[192,16,128]{2,1,0:T(8,128)(2,1)S(1)}, bf16[192,16,128]{2,1,0:T(8,128)(2,1)S(1)}, u32[]{:S(2)}, u32[]{:S(2)}) collective-permute-start(bf16[192,16,128]{2,1,0:T(8,128)(2,1)S(1)} %anomalies.1.refs_0_), channel_id=1, source_target_pairs={{0,2},{1,3},{2,0},{3,1},{4,6},{5,7},{6,4},{7,5},{8,10},{9,11},{10,... | collective-permute-start | bytes 2359304 | tf_op jit(solution)/shard_map/ppermute | solution.py:571
  33.0 23.6 %all-to-all-start = ((f32[256,1,128]{2,1,0:T(1,128)}), f32[256,1,128]{2,1,0:T(1,128)S(1)}, u32[]{:S(2)}, u32[]{:S(2)}) async-start(f32[256,1,128]{2,1,0:T(1,128)} %bitcast.11), calls=%async_computation | async-start | bytes 262144 | tf_op jit(solution)/shard_map/all_to_all | solution.py:586
  43.7 13.6 %collective-permute-start.6 = (bf16[192,16,128]{2,1,0:T(8,128)(2,1)S(1)}, bf16[192,16,128]{2,1,0:T(8,128)(2,1)S(1)}, u32[]{:S(2)}, u32[]{:S(2)}) collective-permute-start(bf16[192,16,128]{2,1,0:T(8,128)(2,1)S(1)} %anomalies.1.refs_0_), channel_id=1, source_target_pairs={{0,1},{1,0},{2,3},{3,2},{4,5},{5,4},{6,7},{7,6},{8,9},{9,8},{10,11... | collective-permute-start | bytes 2359304 | tf_op jit(solution)/shard_map/ppermute | solution.py:571
  52.0 5.3 %copy-start.8 = (f32[256,128]{1,0:T(8,128)S(1)}, f32[256,128]{1,0:T(8,128)}, u32[]{:S(2)}) copy-start(f32[256,128]{1,0:T(8,128)} %copy-done.7) | copy-start | bytes 393220
  52.0 5.3 %copy-start.10 = (f32[256,128]{1,0:T(8,128)S(1)}, f32[256,128]{1,0:T(8,128)}, u32[]{:S(2)}) copy-start(f32[256,128]{1,0:T(8,128)} %copy-done.9) | copy-start | bytes 393220
  56.6 2.8 %collective-permute-start.8 = (bf16[192,16,128]{2,1,0:T(8,128)(2,1)S(1)}, bf16[192,16,128]{2,1,0:T(8,128)(2,1)S(1)}, u32[]{:S(2)}, u32[]{:S(2)}) collective-permute-start(bf16[192,16,128]{2,1,0:T(8,128)(2,1)S(1)} %hold.1.refs_2_), channel_id=1, source_target_pairs={{0,1},{1,0},{2,3},{3,2},{4,5},{5,4},{6,7},{7,6},{8,9},{9,8},{10,11... | collective-permute-start | bytes 2359304 | tf_op jit(solution)/shard_map/ppermute | solution.py:571
  (3 other events, 2.9 us)

commit v10 on v9

--- a/solution.py
+++ b/solution.py
@@ -580,7 +580,7 @@
     total = total_of(prior, sent[0])
     chip = pair_sum(total, across(total, 1))
     totals = [chip, across(chip, 2)]
-    mine = anomalies(prior, totals, float(members), first[1], *halos[1])
+    mine = anomalies(prior, totals, float(members), token, *halos[1])
     beside = across(mine, 1)
     over = across(mine, 2)
     vals = lax.all_to_all(payload, ("tile", "mem"), 0, 0, tiled=True)

time: 61.2 us -> 61.3 us (level)
    pallas_call x1, Pallas kernels: 2.28 us -> 2.94 us  [probes(): pl.pallas_call(functools.partial(probe_kernel, devices), in_specs=[SMEM]...]
  transfers between devices with their start and end apart: 10 -> 10, of which waited for: 5 -> 5; matrix products, arithmetic and copies ran while one was open for 0% -> 0% of each run, Pallas kernels for 26% -> 27%
where the time goes in v10:
time: 61.3 us; the launch traced here: 61 us
  starting transfers between devices  29 us (47%)
  Pallas kernels  20.5 us (33%)
  waiting for transfers between devices  9.85 us (16%)
  between operations  0.84 us (1%)
  local copies, waits for them, and re-layouts  0.74 us (1%)
    ppermute x4, starting transfers between devices, swap(): return lax.ppermute(x, 'tile', pairs + [(b, a) for a, b in pairs])  13 us
    pallas_call x2, Pallas kernels, sweeps(): pl.pallas_call(functools.partial(sweep_kernel, chunk), grid=(STEPS,), in_...  10.8 us
    all_to_all x1, starting transfers between devices, per_device(): vals = lax.all_to_all(payload, ('tile', 'mem'), 0, 0, tiled=True)  10.7 us
    ppermute x5, starting transfers between devices, across(): return lax.ppermute(x, 'mem', [(i, i ^ bits) for i in range(groups)])  5.35 us
    all_to_all x1, waiting for transfers between devices, per_device(): vals = lax.all_to_all(payload, ('tile', 'mem'), 0, 0, tiled=True)  4.6 us
    ppermute x4, waiting for transfers between devices, swap(): return lax.ppermute(x, 'tile', pairs + [(b, a) for a, b in pairs])  4.29 us
    pallas_call x1, Pallas kernels, probes(): pl.pallas_call(functools.partial(probe_kernel, devices), in_specs=[SMEM]...  2.94 us
    pallas_call x1, Pallas kernels, solve(): pl.pallas_call(functools.partial(solve_kernel, members, here), in_specs=[...  1.91 us
  transfers between devices with their start and end apart: 10, of which 5 were waited for; matrix products, arithmetic and copies ran while one was open for 0% of the time, Pallas kernels for 27%

profile of v10, /device:TPU:1, one launch (start us, length us, event | category | flops | bytes accessed | tf_op | source)
XLA Modules:
  0.0 61.0 jit_solution(1947206121634725186)
XLA Ops:
  0.6 1.9 %encode.1 = (bf16[28,48,128]{2,1,0:T(8,128)(2,1)S(1)}, bf16[28,48,128]{2,1,0:T(8,128)(2,1)S(1)}, bf16[24,48,128]{2,1,0:T(8,128)(2,1)S(1)}, bf16[24,48,128]{2,1,0:T(8,128)(2,1)S(1)}) custom-call(s32[1]{0:T(128)} %bitcast.odd_ref, f32[16,4,48,128]{3,2,1,0:T(8,128)} %prior_hbm.3, f32[4,48,128]{2,1,0:T(8,128)} %flow_ref.3, f32[4,48,128]{2,1,0:T(8,128)} %visc_ref.5), custom_call_target="tpu_custom_call" | custom-call | tf_op jit(solution)/shard_map/encode/pallas_call | solution.py:92
  2.6 11.4 %collective-permute-start.3 = (bf16[28,48,128]{2,1,0:T(8,128)(2,1)S(1)}, bf16[28,48,128]{2,1,0:T(8,128)(2,1)S(1)}, u32[]{:S(2)}, u32[]{:S(2)}) collective-permute-start(bf16[28,48,128]{2,1,0:T(8,128)(2,1)S(1)} %get-tuple-element.22), channel_id=1, source_target_pairs={{4,8},{12,16},{20,24},{28,32},{36,40},{44,48},{52,56},{60,64},{68,... | collective-permute-start | bytes 1032200 | tf_op jit(solution)/shard_map/ppermute | solution.py:568
  14.0 1.5 %collective-permute-start = (bf16[24,48,128]{2,1,0:T(8,128)(2,1)S(1)}, bf16[24,48,128]{2,1,0:T(8,128)(2,1)S(1)}, u32[]{:S(2)}, u32[]{:S(2)}) collective-permute-start(bf16[24,48,128]{2,1,0:T(8,128)(2,1)S(1)} %get-tuple-element.19), channel_id=1, source_target_pairs={{0,4},{8,12},{16,20},{24,28},{32,36},{40,44},{48,52},{56,60},{64,6... | collective-permute-start | bytes 884744 | tf_op jit(solution)/shard_map/ppermute | solution.py:568
  15.5 0.1 collective-permute-start.1
  15.6 0.1 total.1.a_ref
  15.6 1.6 %collective-permute-start.4 = (f32[4,48,128]{2,1,0:T(8,128)S(1)}, f32[4,48,128]{2,1,0:T(8,128)S(1)}, u32[]{:S(2)}, u32[]{:S(2)}) collective-permute-start(f32[4,48,128]{2,1,0:T(8,128)S(1)} %total.1.a_ref), channel_id=1, source_target_pairs={{0,1},{1,0},{2,3},{3,2},{4,5},{5,4},{6,7},{7,6},{8,9},{9,8},{10,11... | collective-permute-start | bytes 294920 | tf_op jit(solution)/shard_map/ppermute | solution.py:571
  17.2 0.9 %collective-permute-done.4.b_ref = f32[4,48,128]{2,1,0:T(8,128)S(1)} collective-permute-done((f32[4,48,128]{2,1,0:T(8,128)S(1)}, f32[4,48,128]{2,1,0:T(8,128)S(1)}, u32[]{:S(2)}, u32[]{:S(2)}) %collective-permute-start.4) | collective-permute-done | bytes 98336 | tf_op jit(solution)/shard_map/ppermute | solution.py:571
  18.2 0.4 collective-permute-start.5
  18.6 0.5 slots.1
  19.1 0.7 %copy-done.9 = f32[256,128]{1,0:T(8,128)} copy-done((f32[256,128]{1,0:T(8,128)}, f32[256,128]{1,0:T(8,128)S(1)}, u32[]{:S(2)}) %copy-start.9) | copy-done | bytes 131096
  19.8 2.0 %collective-permute-done.3.outer_ref = bf16[28,48,128]{2,1,0:T(8,128)(2,1)S(1)} collective-permute-done((bf16[28,48,128]{2,1,0:T(8,128)(2,1)S(1)}, bf16[28,48,128]{2,1,0:T(8,128)(2,1)S(1)}, u32[]{:S(2)}, u32[]{:S(2)}) %collective-permute-start.3) | collective-permute-done | bytes 344096 | tf_op jit(solution)/shard_map/ppermute | solution.py:568
  21.8 0.8 %collective-permute-done.2.inner_ref = bf16[28,48,128]{2,1,0:T(8,128)(2,1)S(1)} collective-permute-done((bf16[28,48,128]{2,1,0:T(8,128)(2,1)S(1)}, bf16[28,48,128]{2,1,0:T(8,128)(2,1)S(1)}, u32[]{:S(2)}, u32[]{:S(2)}) %collective-permute-start.2) | collective-permute-done | bytes 344096 | tf_op jit(solution)/shard_map/ppermute | solution.py:568
  22.6 4.8 %sweeps0.1 = (f32[16,4,48,128]{3,2,1,0:T(8,128)}, f32[64,128]{1,0:T(8,128)S(1)}, f32[10,64,128]{2,1,0:T(8,128)S(1)}, f32[10,64,128]{2,1,0:T(8,128)S(1)}) custom-call(s32[1]{0:T(128)} %bitcast.odd_ref, s32[1,4]{1,0:T(1,128)S(1)} %copy-done.12, f32[16,4,48,128]{3,2,1,0:T(8,128)S(1)} %copy-done, f32[4,48,128]{2,1,0:T(8,128)S(1)} %copy-done.6, ...), custom_call_target="tpu_custom_call" | custom-call | tf_op jit(solution)/shard_map/sweeps0/pallas_call | solution.py:365
  27.4 1.5 %collective-permute-done.inner_ref.refs_1_ = bf16[24,48,128]{2,1,0:T(8,128)(2,1)S(1)} collective-permute-done((bf16[24,48,128]{2,1,0:T(8,128)(2,1)S(1)}, bf16[24,48,128]{2,1,0:T(8,128)(2,1)S(1)}, u32[]{:S(2)}, u32[]{:S(2)}) %collective-permute-start) | collective-permute-done | bytes 294944 | tf_op jit(solution)/shard_map/ppermute | solution.py:568
  28.9 2.9 %probes.1 = (f32[256,128]{1,0:T(8,128)}, f32[8,128]{1,0:T(8,128)S(1)}) custom-call(s32[1]{0:T(128)} %bitcast.odd_ref, s32[1,4]{1,0:T(1,128)S(1)} %copy-done.12, f32[16,4,48,128]{3,2,1,0:T(8,128)S(1)} %copy-done, f32[4,48,128]{2,1,0:T(8,128)S(1)} %copy-done.3, bf16[24,48,128]{2,1,0:T(8,128)(2,1)S(1)} %collective-permute-done.inner_ref.refs_1_, ...), custom_call_target="tpu_custom_call" | custom-call | tf_op jit(solution)/shard_map/probes/pallas_call | solution.py:237
  31.9 0.7 %anomalies.1.refs_0_ = bf16[192,16,128]{2,1,0:T(8,128)(2,1)S(1)} custom-call(f32[16,4,48,128]{3,2,1,0:T(8,128)S(1)} %copy-done, f32[4,48,128]{2,1,0:T(8,128)S(1)} %pair_sum.1.a_ref, f32[4,48,128]{2,1,0:T(8,128)S(1)} %collective-permute-done.5.b_ref, f32[8,128]{1,0:T(8,128)S(1)} %get-tuple-element.27.rest_2_.refs_0_, ...), custom_call_target="tpu_custom_call" | custom-call | tf_op jit(solution)/shard_map/anomalies/pallas_call | solution.py:391
  32.6 0.4 collective-permute-start.7
  33.0 10.7 %all-to-all-start = ((f32[256,1,128]{2,1,0:T(1,128)}), f32[256,1,128]{2,1,0:T(1,128)S(1)}, u32[]{:S(2)}, u32[]{:S(2)}) async-start(f32[256,1,128]{2,1,0:T(1,128)} %bitcast.6), calls=%async_computation | async-start | bytes 262144 | tf_op jit(solution)/shard_map/all_to_all | solution.py:586
  43.7 2.2 %collective-permute-start.6 = (bf16[192,16,128]{2,1,0:T(8,128)(2,1)S(1)}, bf16[192,16,128]{2,1,0:T(8,128)(2,1)S(1)}, u32[]{:S(2)}, u32[]{:S(2)}) collective-permute-start(bf16[192,16,128]{2,1,0:T(8,128)(2,1)S(1)} %anomalies.1.refs_0_), channel_id=1, source_target_pairs={{0,1},{1,0},{2,3},{3,2},{4,5},{5,4},{6,7},{7,6},{8,9},{9,8},{10,11... | collective-permute-start | bytes 2359304 | tf_op jit(solution)/shard_map/ppermute | solution.py:571
  46.0 6.0 %sweeps1.1 = (f32[16,4,48,128]{3,2,1,0:T(8,128)}, f32[8,128]{1,0:T(8,128)S(1)}) custom-call(s32[1]{0:T(128)} %bitcast.odd_ref, s32[1,4]{1,0:T(1,128)S(1)} %copy-done.12, f32[16,4,48,128]{3,2,1,0:T(8,128)} %prior_hbm.3, f32[4,48,128]{2,1,0:T(8,128)} %flow_ref.3, f32[4,48,128]{2,1,0:T(8,128)S(1)} %copy-done.3, ...), custom_call_target="tpu_custom_call", output_to_operand_aliasing={{0}: (10, {})} | custom-call | tf_op jit(solution)/shard_map/sweeps1/pallas_call | solution.py:365
  52.0 4.6 %all-to-all-done = f32[256,1,128]{2,1,0:T(1,128)S(1)} async-done(((f32[256,1,128]{2,1,0:T(1,128)}), f32[256,1,128]{2,1,0:T(1,128)S(1)}, u32[]{:S(2)}, u32[]{:S(2)}) %all-to-all-start) | async-done | bytes 131104 | tf_op jit(solution)/shard_map/all_to_all | solution.py:586
  56.6 0.7 %collective-permute-start.8 = (bf16[192,16,128]{2,1,0:T(8,128)(2,1)S(1)}, bf16[192,16,128]{2,1,0:T(8,128)(2,1)S(1)}, u32[]{:S(2)}, u32[]{:S(2)}) collective-permute-start(bf16[192,16,128]{2,1,0:T(8,128)(2,1)S(1)} %hold.1.refs_2_), channel_id=1, source_target_pairs={{0,1},{1,0},{2,3},{3,2},{4,5},{5,4},{6,7},{7,6},{8,9},{9,8},{10,11... | collective-permute-start | bytes 2359304 | tf_op jit(solution)/shard_map/ppermute | solution.py:571
  57.3 1.9 %solve.1 = (bf16[16,64]{1,0:T(8,128)(2,1)S(1)}, bf16[192,16,128]{2,1,0:T(8,128)(2,1)S(1)}, f32[16,4,48,128]{3,2,1,0:T(8,128)S(1)}) custom-call(s32[1]{0:T(128)} %bitcast.4.me_ref, f32[256,128]{1,0:T(8,128)S(1)} %bitcast.10, f32[256,128]{1,0:T(8,128)S(1)} %copy-done.8, f32[256,128]{1,0:T(8,128)S(1)} %copy-done.10, ...), custom_call_target="tpu_custom_call" | custom-call | tf_op jit(solution)/shard_map/solve/pallas_call | solution.py:495
  59.3 1.7 %update.1 = f32[16,4,48,128]{3,2,1,0:T(8,128)} custom-call(bf16[16,64]{1,0:T(8,128)(2,1)S(1)} %get-tuple-element.32.weights_ref, f32[16,4,48,128]{3,2,1,0:T(8,128)S(1)} %get-tuple-element.33.prior_ref, bf16[192,16,128]{2,1,0:T(8,128)(2,1)S(1)} %anomalies.1.refs_0_, bf16[192,16,128]{2,1,0:T(8,128)(2,1)S(1)} %get-tuple-element.34.refs_1_, ...), custom_call_target="tpu_custom_call" | custom-call | tf_op jit(solution)/shard_map/update/pallas_call | solution.py:547
  (39 shorter events, 0.1 us)
Async XLA Ops:
  0.6 14.9 %copy-start = (f32[16,4,48,128]{3,2,1,0:T(8,128)S(1)}, f32[16,4,48,128]{3,2,1,0:T(8,128)}, u32[]{:S(2)}) copy-start(f32[16,4,48,128]{3,2,1,0:T(8,128)} %prior_hbm.3) | copy-start | bytes 4718596
  2.5 16.1 %copy-start.11 = (f32[64,256]{1,0:T(8,128)S(1)}, f32[64,256]{1,0:T(8,128)}, u32[]{:S(2)}) copy-start(f32[64,256]{1,0:T(8,128)} %noise_ref.1) | copy-start | bytes 196612
  2.5 16.1 %copy-start.13 = (s32[256]{0:T(256)S(1)}, s32[256]{0:T(256)}, u32[]{:S(2)}) copy-start(s32[256]{0:T(256)} %param.12) | copy-start | bytes 3076
  2.5 16.1 %copy-start.14 = (f32[256]{0:T(256)S(1)}, f32[256]{0:T(256)}, u32[]{:S(2)}) copy-start(f32[256]{0:T(256)} %param.13) | copy-start | bytes 3076
  2.5 16.1 %copy-start.15 = (f32[256]{0:T(256)S(1)}, f32[256]{0:T(256)}, u32[]{:S(2)}) copy-start(f32[256]{0:T(256)} %param.14) | copy-start | bytes 3076
  2.6 20.0 %copy-start.3 = (f32[4,48,128]{2,1,0:T(8,128)S(1)}, f32[4,48,128]{2,1,0:T(8,128)}, u32[]{:S(2)}) copy-start(f32[4,48,128]{2,1,0:T(8,128)} %visc_ref.5) | copy-start | bytes 294916
  2.6 20.0 %copy-start.6 = (f32[4,48,128]{2,1,0:T(8,128)S(1)}, f32[4,48,128]{2,1,0:T(8,128)}, u32[]{:S(2)}) copy-start(f32[4,48,128]{2,1,0:T(8,128)} %flow_ref.3) | copy-start | bytes 294916
  2.6 20.0 %copy-start.12 = (s32[1,4]{1,0:T(1,128)S(1)}, s32[1,4]{1,0:T(1,128)}, u32[]{:S(2)}) copy-start(s32[1,4]{1,0:T(1,128)} %cells_ref.5) | copy-start | bytes 52
  2.6 19.2 %collective-permute-start.3 = (bf16[28,48,128]{2,1,0:T(8,128)(2,1)S(1)}, bf16[28,48,128]{2,1,0:T(8,128)(2,1)S(1)}, u32[]{:S(2)}, u32[]{:S(2)}) collective-permute-start(bf16[28,48,128]{2,1,0:T(8,128)(2,1)S(1)} %get-tuple-element.22), channel_id=1, source_target_pairs={{4,8},{12,16},{20,24},{28,32},{36,40},{44,48},{52,56},{60,64},{68,... | collective-permute-start | bytes 1032200 | tf_op jit(solution)/shard_map/ppermute | solution.py:568
  14.0 8.6 %collective-permute-start.2 = (bf16[28,48,128]{2,1,0:T(8,128)(2,1)S(1)}, bf16[28,48,128]{2,1,0:T(8,128)(2,1)S(1)}, u32[]{:S(2)}, u32[]{:S(2)}) collective-permute-start(bf16[28,48,128]{2,1,0:T(8,128)(2,1)S(1)} %get-tuple-element.21.after), channel_id=1, source_target_pairs={{0,4},{8,12},{16,20},{24,28},{32,36},{40,44},{48,52},{56,60},{64,6... | collective-permute-start | bytes 1032200 | tf_op jit(solution)/shard_map/ppermute | solution.py:568
  14.0 14.9 %collective-permute-start = (bf16[24,48,128]{2,1,0:T(8,128)(2,1)S(1)}, bf16[24,48,128]{2,1,0:T(8,128)(2,1)S(1)}, u32[]{:S(2)}, u32[]{:S(2)}) collective-permute-start(bf16[24,48,128]{2,1,0:T(8,128)(2,1)S(1)} %get-tuple-element.19), channel_id=1, source_target_pairs={{0,4},{8,12},{16,20},{24,28},{32,36},{40,44},{48,52},{56,60},{64,6... | collective-permute-start | bytes 884744 | tf_op jit(solution)/shard_map/ppermute | solution.py:568
  15.5 13.5 %collective-permute-start.1 = (bf16[24,48,128]{2,1,0:T(8,128)(2,1)S(1)}, bf16[24,48,128]{2,1,0:T(8,128)(2,1)S(1)}, u32[]{:S(2)}, u32[]{:S(2)}) collective-permute-start(bf16[24,48,128]{2,1,0:T(8,128)(2,1)S(1)} %get-tuple-element.20), channel_id=1, source_target_pairs={{4,8},{12,16},{20,24},{28,32},{36,40},{44,48},{52,56},{60,64},{68,... | collective-permute-start | bytes 884744 | tf_op jit(solution)/shard_map/ppermute | solution.py:568
  15.6 2.5 %collective-permute-start.4 = (f32[4,48,128]{2,1,0:T(8,128)S(1)}, f32[4,48,128]{2,1,0:T(8,128)S(1)}, u32[]{:S(2)}, u32[]{:S(2)}) collective-permute-start(f32[4,48,128]{2,1,0:T(8,128)S(1)} %total.1.a_ref), channel_id=1, source_target_pairs={{0,1},{1,0},{2,3},{3,2},{4,5},{5,4},{6,7},{7,6},{8,9},{9,8},{10,11... | collective-permute-start | bytes 294920 | tf_op jit(solution)/shard_map/ppermute | solution.py:571
  18.2 13.7 %collective-permute-start.5 = (f32[4,48,128]{2,1,0:T(8,128)S(1)}, f32[4,48,128]{2,1,0:T(8,128)S(1)}, u32[]{:S(2)}, u32[]{:S(2)}) collective-permute-start(f32[4,48,128]{2,1,0:T(8,128)S(1)} %pair_sum.1.a_ref), channel_id=1, source_target_pairs={{0,2},{1,3},{2,0},{3,1},{4,6},{5,7},{6,4},{7,5},{8,10},{9,11},{10,... | collective-permute-start | bytes 294920 | tf_op jit(solution)/shard_map/ppermute | solution.py:571
  19.8 12.1 %copy-start.7 = (f32[256,128]{1,0:T(8,128)}, f32[256,128]{1,0:T(8,128)S(1)}, u32[]{:S(2)}) copy-start(f32[256,128]{1,0:T(8,128)S(1)} %get-tuple-element.23.rest_0_.seen_ref) | copy-start | bytes 393220
  27.4 5.1 %copy-start.4 = (f32[10,64,128]{2,1,0:T(8,128)}, f32[10,64,128]{2,1,0:T(8,128)S(1)}, u32[]{:S(2)}) copy-start(f32[10,64,128]{2,1,0:T(8,128)S(1)} %get-tuple-element.24.lap0.rest_0_) | copy-start | bytes 983044
  27.4 5.1 %copy-start.5 = (f32[10,64,128]{2,1,0:T(8,128)}, f32[10,64,128]{2,1,0:T(8,128)S(1)}, u32[]{:S(2)}) copy-start(f32[10,64,128]{2,1,0:T(8,128)S(1)} %get-tuple-element.25.adv0.rest_1_) | copy-start | bytes 983044
  28.9 3.7 %copy-start.2 = (bf16[24,48,128]{2,1,0:T(8,128)(2,1)}, bf16[24,48,128]{2,1,0:T(8,128)(2,1)S(1)}, u32[]{:S(2)}) copy-start(bf16[24,48,128]{2,1,0:T(8,128)(2,1)S(1)} %collective-permute-done.1.outer_ref.refs_2_) | copy-start | bytes 884740
  32.6 24.0 %collective-permute-start.7 = (bf16[192,16,128]{2,1,0:T(8,128)(2,1)S(1)}, bf16[192,16,128]{2,1,0:T(8,128)(2,1)S(1)}, u32[]{:S(2)}, u32[]{:S(2)}) collective-permute-start(bf16[192,16,128]{2,1,0:T(8,128)(2,1)S(1)} %anomalies.1.refs_0_), channel_id=1, source_target_pairs={{0,2},{1,3},{2,0},{3,1},{4,6},{5,7},{6,4},{7,5},{8,10},{9,11},{10,... | collective-permute-start | bytes 2359304 | tf_op jit(solution)/shard_map/ppermute | solution.py:571
  33.0 23.6 %all-to-all-start = ((f32[256,1,128]{2,1,0:T(1,128)}), f32[256,1,128]{2,1,0:T(1,128)S(1)}, u32[]{:S(2)}, u32[]{:S(2)}) async-start(f32[256,1,128]{2,1,0:T(1,128)} %bitcast.6), calls=%async_computation | async-start | bytes 262144 | tf_op jit(solution)/shard_map/all_to_all | solution.py:586
  43.7 13.6 %collective-permute-start.6 = (bf16[192,16,128]{2,1,0:T(8,128)(2,1)S(1)}, bf16[192,16,128]{2,1,0:T(8,128)(2,1)S(1)}, u32[]{:S(2)}, u32[]{:S(2)}) collective-permute-start(bf16[192,16,128]{2,1,0:T(8,128)(2,1)S(1)} %anomalies.1.refs_0_), channel_id=1, source_target_pairs={{0,1},{1,0},{2,3},{3,2},{4,5},{5,4},{6,7},{7,6},{8,9},{9,8},{10,11... | collective-permute-start | bytes 2359304 | tf_op jit(solution)/shard_map/ppermute | solution.py:571
  52.0 5.3 %copy-start.8 = (f32[256,128]{1,0:T(8,128)S(1)}, f32[256,128]{1,0:T(8,128)}, u32[]{:S(2)}) copy-start(f32[256,128]{1,0:T(8,128)} %copy-done.7) | copy-start | bytes 393220
  52.0 5.3 %copy-start.10 = (f32[256,128]{1,0:T(8,128)S(1)}, f32[256,128]{1,0:T(8,128)}, u32[]{:S(2)}) copy-start(f32[256,128]{1,0:T(8,128)} %copy-done.9) | copy-start | bytes 393220
  56.6 2.7 %collective-permute-start.8 = (bf16[192,16,128]{2,1,0:T(8,128)(2,1)S(1)}, bf16[192,16,128]{2,1,0:T(8,128)(2,1)S(1)}, u32[]{:S(2)}, u32[]{:S(2)}) collective-permute-start(bf16[192,16,128]{2,1,0:T(8,128)(2,1)S(1)} %hold.1.refs_2_), channel_id=1, source_target_pairs={{0,1},{1,0},{2,3},{3,2},{4,5},{5,4},{6,7},{7,6},{8,9},{9,8},{10,11... | collective-permute-start | bytes 2359304 | tf_op jit(solution)/shard_map/ppermute | solution.py:571
  (2 other events, 4.3 us)

commit v11 on v10

--- a/solution.py
+++ b/solution.py
@@ -89,13 +89,13 @@
     for c, (part, _) in enumerate(PARTS):
         slabs = 3 * part + (layers if c == 0 else 0)
         shapes += [jax.ShapeDtypeStruct((slabs, nz, ny), BF16)] * 2
+    shapes.append(jax.ShapeDtypeStruct(prior.shape, F32))
     return pl.pallas_call(
         encode_kernel,
         in_specs=[SMEM] + [pl.BlockSpec(memory_space=pltpu.HBM)] * 3,
         out_specs=[VMEM] * len(shapes),
         out_shape=shapes,
         scratch_shapes=[
-            pltpu.VMEM(prior.shape, F32),
             pltpu.VMEM(flow.shape, F32),
             pltpu.VMEM(visc.shape, F32),
             pltpu.VMEM(visc.shape, F32),
@@ -570,17 +570,17 @@
     def across(x, bits):
         return lax.ppermute(x, "mem", [(i, i ^ bits) for i in range(groups)])
 
-    sent = encode(odd, prior, base_flow, base_visc)
+    *sent, near = encode(odd, prior, base_flow, base_visc)
     halos = [(swap(sent[2 * c], 0), swap(sent[2 * c + 1], 1)) for c in range(CHUNKS)]
-    fields = (odd, prior, base_flow, base_visc, probe_cells)
+    fields = (odd, near, base_flow, base_visc, probe_cells)
     seen, weight = in_slots(obs_slot, obs_values, obs_var, obs_noise, probe_cells.shape[1], sent[0])
     first = sweeps(*fields, halos[0], 0, after=seen)
-    payload, token = probes(odd, prior, base_visc, probe_cells, halos[1], first, tiles * groups)
-    velocity, done = sweeps(*fields, halos[1], 1, first, token)
-    total = total_of(prior, sent[0])
+    payload, token = probes(odd, near, base_visc, probe_cells, halos[1], first, tiles * groups)
+    velocity, done = sweeps(odd, prior, *fields[2:], halos[1], 1, first, token)
+    total = total_of(near, sent[0])
     chip = pair_sum(total, across(total, 1))
     totals = [chip, across(chip, 2)]
-    mine = anomalies(prior, totals, float(members), token, *halos[1])
+    mine = anomalies(near, totals, float(members), first[1], *halos[1])
     beside = across(mine, 1)
     over = across(mine, 2)
     vals = lax.all_to_all(payload, ("tile", "mem"), 0, 0, tiled=True)

time: 61.3 us -> 62.3 us (1.016)
  Pallas kernels: 20.5 us -> 21.5 us
  waiting for transfers between devices: 9.85 us -> 10.7 us
  local copies, waits for them, and re-layouts: 0.74 us -> 0.06 us
    pallas_call x1, Pallas kernels: 1.74 us -> 2.85 us  [updated(): pl.pallas_call(update_kernel, in_specs=[VMEM] * 6, out_specs=pl.BlockSpec...]
    ppermute x4, waiting for transfers between devices: 4.29 us -> 5.02 us  [swap(): return lax.ppermute(x, 'tile', pairs + [(b, a) for a, b in pairs])]
    unnamed x32 -> x22, local copies, waits for them, and re-layouts: 0.74 us -> 0.06 us
  transfers between devices with their start and end apart: 10 -> 10, of which waited for: 5 -> 6; matrix products, arithmetic and copies ran while one was open for 0% -> 0% of each run, Pallas kernels for 27% -> 26%
where the time goes in v11:
time: 62.3 us; the launch traced here: 62.1 us
  starting transfers between devices  29 us (47%)
  Pallas kernels  21.5 us (35%)
  waiting for transfers between devices  10.7 us (17%)
  between operations  0.77 us (1%)
    ppermute x4, starting transfers between devices, swap(): return lax.ppermute(x, 'tile', pairs + [(b, a) for a, b in pairs])  13 us
    pallas_call x2, Pallas kernels, sweeps(): pl.pallas_call(functools.partial(sweep_kernel, chunk), grid=(STEPS,), in_...  10.8 us
    all_to_all x1, starting transfers between devices, per_device(): vals = lax.all_to_all(payload, ('tile', 'mem'), 0, 0, tiled=True)  10.7 us
    ppermute x5, starting transfers between devices, across(): return lax.ppermute(x, 'mem', [(i, i ^ bits) for i in range(groups)])  5.34 us
    ppermute x4, waiting for transfers between devices, swap(): return lax.ppermute(x, 'tile', pairs + [(b, a) for a, b in pairs])  5.02 us
    all_to_all x1, waiting for transfers between devices, per_device(): vals = lax.all_to_all(payload, ('tile', 'mem'), 0, 0, tiled=True)  4.62 us
    pallas_call x1, Pallas kernels, probes(): pl.pallas_call(functools.partial(probe_kernel, devices), in_specs=[SMEM]...  2.95 us
    pallas_call x1, Pallas kernels, updated(): pl.pallas_call(update_kernel, in_specs=[VMEM] * 6, out_specs=pl.BlockSpec...  2.85 us
  transfers between devices with their start and end apart: 10, of which 6 were waited for; matrix products, arithmetic and copies ran while one was open for 0% of the time, Pallas kernels for 26%

profile of v11, /device:TPU:1, one launch (start us, length us, event | category | flops | bytes accessed | tf_op | source)
XLA Modules:
  0.0 62.1 jit_solution(16834437971215169069)
XLA Ops:
  0.6 1.8 %encode.1 = (bf16[28,48,128]{2,1,0:T(8,128)(2,1)S(1)}, bf16[28,48,128]{2,1,0:T(8,128)(2,1)S(1)}, bf16[24,48,128]{2,1,0:T(8,128)(2,1)S(1)}, bf16[24,48,128]{2,1,0:T(8,128)(2,1)S(1)}, f32[16,4,48,128]{3,2,1,0:T(8,128)S(1)}) custom-call(s32[1]{0:T(128)} %bitcast.odd_ref, f32[16,4,48,128]{3,2,1,0:T(8,128)} %prior_hbm.3, f32[4,48,128]{2,1,0:T(8,128)} %flow_ref.3, ...), custom_call_target="tpu_custom_call" | custom-call | tf_op jit(solution)/shard_map/encode/pallas_call | solution.py:93
  2.5 11.4 %collective-permute-start.3 = (bf16[28,48,128]{2,1,0:T(8,128)(2,1)S(1)}, bf16[28,48,128]{2,1,0:T(8,128)(2,1)S(1)}, u32[]{:S(2)}, u32[]{:S(2)}) collective-permute-start(bf16[28,48,128]{2,1,0:T(8,128)(2,1)S(1)} %get-tuple-element.24), channel_id=1, source_target_pairs={{4,8},{12,16},{20,24},{28,32},{36,40},{44,48},{52,56},{60,64},{68,... | collective-permute-start | bytes 1032200 | tf_op jit(solution)/shard_map/ppermute | solution.py:568
  13.9 1.5 %collective-permute-start = (bf16[24,48,128]{2,1,0:T(8,128)(2,1)S(1)}, bf16[24,48,128]{2,1,0:T(8,128)(2,1)S(1)}, u32[]{:S(2)}, u32[]{:S(2)}) collective-permute-start(bf16[24,48,128]{2,1,0:T(8,128)(2,1)S(1)} %get-tuple-element.20), channel_id=1, source_target_pairs={{0,4},{8,12},{16,20},{24,28},{32,36},{40,44},{48,52},{56,60},{64,6... | collective-permute-start | bytes 884744 | tf_op jit(solution)/shard_map/ppermute | solution.py:568
  15.4 0.1 collective-permute-start.1
  15.5 0.1 total.1.a_ref
  15.6 1.6 %collective-permute-start.4 = (f32[4,48,128]{2,1,0:T(8,128)S(1)}, f32[4,48,128]{2,1,0:T(8,128)S(1)}, u32[]{:S(2)}, u32[]{:S(2)}) collective-permute-start(f32[4,48,128]{2,1,0:T(8,128)S(1)} %total.1.a_ref), channel_id=1, source_target_pairs={{0,1},{1,0},{2,3},{3,2},{4,5},{5,4},{6,7},{7,6},{8,9},{9,8},{10,11... | collective-permute-start | bytes 294920 | tf_op jit(solution)/shard_map/ppermute | solution.py:571
  17.2 0.9 %collective-permute-done.4.b_ref = f32[4,48,128]{2,1,0:T(8,128)S(1)} collective-permute-done((f32[4,48,128]{2,1,0:T(8,128)S(1)}, f32[4,48,128]{2,1,0:T(8,128)S(1)}, u32[]{:S(2)}, u32[]{:S(2)}) %collective-permute-start.4) | collective-permute-done | bytes 98336 | tf_op jit(solution)/shard_map/ppermute | solution.py:571
  18.1 0.4 collective-permute-start.5
  18.5 0.5 slots.1
  19.0 2.7 %collective-permute-done.3.outer_ref = bf16[28,48,128]{2,1,0:T(8,128)(2,1)S(1)} collective-permute-done((bf16[28,48,128]{2,1,0:T(8,128)(2,1)S(1)}, bf16[28,48,128]{2,1,0:T(8,128)(2,1)S(1)}, u32[]{:S(2)}, u32[]{:S(2)}) %collective-permute-start.3) | collective-permute-done | bytes 344096 | tf_op jit(solution)/shard_map/ppermute | solution.py:568
  21.7 0.8 %collective-permute-done.2.inner_ref = bf16[28,48,128]{2,1,0:T(8,128)(2,1)S(1)} collective-permute-done((bf16[28,48,128]{2,1,0:T(8,128)(2,1)S(1)}, bf16[28,48,128]{2,1,0:T(8,128)(2,1)S(1)}, u32[]{:S(2)}, u32[]{:S(2)}) %collective-permute-start.2) | collective-permute-done | bytes 344096 | tf_op jit(solution)/shard_map/ppermute | solution.py:568
  22.5 4.8 %sweeps0.1 = (f32[16,4,48,128]{3,2,1,0:T(8,128)}, f32[64,128]{1,0:T(8,128)S(1)}, f32[10,64,128]{2,1,0:T(8,128)S(1)}, f32[10,64,128]{2,1,0:T(8,128)S(1)}) custom-call(s32[1]{0:T(128)} %bitcast.odd_ref, s32[1,4]{1,0:T(1,128)S(1)} %copy-done.7, f32[16,4,48,128]{3,2,1,0:T(8,128)S(1)} %get-tuple-element.22.prior_ref, f32[4,48,128]{2,1,0:T(8,128)S(1)} %copy-done.5, ...), custom_call_target="tpu_custom_call" | custom-call | tf_op jit(solution)/shard_map/sweeps0/pallas_call | solution.py:365
  27.3 1.5 %collective-permute-done.inner_ref.refs_1_ = bf16[24,48,128]{2,1,0:T(8,128)(2,1)S(1)} collective-permute-done((bf16[24,48,128]{2,1,0:T(8,128)(2,1)S(1)}, bf16[24,48,128]{2,1,0:T(8,128)(2,1)S(1)}, u32[]{:S(2)}, u32[]{:S(2)}) %collective-permute-start) | collective-permute-done | bytes 294944 | tf_op jit(solution)/shard_map/ppermute | solution.py:568
  28.8 0.7 %anomalies.1.refs_0_ = bf16[192,16,128]{2,1,0:T(8,128)(2,1)S(1)} custom-call(f32[16,4,48,128]{3,2,1,0:T(8,128)S(1)} %get-tuple-element.22.prior_ref, f32[4,48,128]{2,1,0:T(8,128)S(1)} %pair_sum.1.a_ref, f32[4,48,128]{2,1,0:T(8,128)S(1)} %collective-permute-done.5.b_ref, f32[64,128]{1,0:T(8,128)S(1)} %get-tuple-element.28.rows_in.refs_0_, ...), custom_call_target="tpu_custom_call" | custom-call | tf_op jit(solution)/shard_map/anomalies/pallas_call | solution.py:391
  29.5 0.4 collective-permute-start.7
  30.0 2.9 %probes.1 = (f32[256,128]{1,0:T(8,128)}, f32[8,128]{1,0:T(8,128)S(1)}) custom-call(s32[1]{0:T(128)} %bitcast.odd_ref, s32[1,4]{1,0:T(1,128)S(1)} %copy-done.7, f32[16,4,48,128]{3,2,1,0:T(8,128)S(1)} %get-tuple-element.22.prior_ref, f32[4,48,128]{2,1,0:T(8,128)S(1)} %copy-done.2, bf16[24,48,128]{2,1,0:T(8,128)(2,1)S(1)} %collective-permute-done.inner_ref.refs_1_, ...), custom_call_target="tpu_custom_call" | custom-call | tf_op jit(solution)/shard_map/probes/pallas_call | solution.py:237
  32.9 10.7 %all-to-all-start = ((f32[256,1,128]{2,1,0:T(1,128)}), f32[256,1,128]{2,1,0:T(1,128)S(1)}, u32[]{:S(2)}, u32[]{:S(2)}) async-start(f32[256,1,128]{2,1,0:T(1,128)} %bitcast.6), calls=%async_computation | async-start | bytes 262144 | tf_op jit(solution)/shard_map/all_to_all | solution.py:586
  43.6 2.2 %collective-permute-start.6 = (bf16[192,16,128]{2,1,0:T(8,128)(2,1)S(1)}, bf16[192,16,128]{2,1,0:T(8,128)(2,1)S(1)}, u32[]{:S(2)}, u32[]{:S(2)}) collective-permute-start(bf16[192,16,128]{2,1,0:T(8,128)(2,1)S(1)} %anomalies.1.refs_0_), channel_id=1, source_target_pairs={{0,1},{1,0},{2,3},{3,2},{4,5},{5,4},{6,7},{7,6},{8,9},{9,8},{10,11... | collective-permute-start | bytes 2359304 | tf_op jit(solution)/shard_map/ppermute | solution.py:571
  45.9 6.0 %sweeps1.1 = (f32[16,4,48,128]{3,2,1,0:T(8,128)}, f32[8,128]{1,0:T(8,128)S(1)}) custom-call(s32[1]{0:T(128)} %bitcast.odd_ref, s32[1,4]{1,0:T(1,128)S(1)} %copy-done.7, f32[16,4,48,128]{3,2,1,0:T(8,128)} %prior_hbm.3, f32[4,48,128]{2,1,0:T(8,128)} %flow_ref.3, f32[4,48,128]{2,1,0:T(8,128)S(1)} %copy-done.2, ...), custom_call_target="tpu_custom_call", output_to_operand_aliasing={{0}: (10, {})} | custom-call | tf_op jit(solution)/shard_map/sweeps1/pallas_call | solution.py:365
  51.9 4.6 %all-to-all-done = f32[256,1,128]{2,1,0:T(1,128)S(1)} async-done(((f32[256,1,128]{2,1,0:T(1,128)}), f32[256,1,128]{2,1,0:T(1,128)S(1)}, u32[]{:S(2)}, u32[]{:S(2)}) %all-to-all-start) | async-done | bytes 131104 | tf_op jit(solution)/shard_map/all_to_all | solution.py:586
  56.5 0.7 %collective-permute-start.8 = (bf16[192,16,128]{2,1,0:T(8,128)(2,1)S(1)}, bf16[192,16,128]{2,1,0:T(8,128)(2,1)}, u32[]{:S(2)}, u32[]{:S(2)}) collective-permute-start(bf16[192,16,128]{2,1,0:T(8,128)(2,1)S(1)} %hold.1.refs_2_), channel_id=1, source_target_pairs={{0,1},{1,0},{2,3},{3,2},{4,5},{5,4},{6,7},{7,6},{8,9},{9,8},{10,11... | collective-permute-start | bytes 2359304 | tf_op jit(solution)/shard_map/ppermute | solution.py:571
  57.2 1.9 %solve.1 = (bf16[16,64]{1,0:T(8,128)(2,1)S(1)}, bf16[192,16,128]{2,1,0:T(8,128)(2,1)S(1)}, f32[16,4,48,128]{3,2,1,0:T(8,128)S(1)}) custom-call(s32[1]{0:T(128)} %bitcast.4.me_ref, f32[256,128]{1,0:T(8,128)S(1)} %bitcast.10, f32[256,128]{1,0:T(8,128)S(1)} %get-tuple-element.25.rest_0_.seen_ref, f32[256,128]{1,0:T(8,128)S(1)} %get-tuple-element.33.weight_ref, ...), custom_call_target="tpu_custom_call" | custom-call | tf_op jit(solution)/shard_map/solve/pallas_call | solution.py:495
  59.1 0.1 collective-permute-done.8.refs_3_
  59.3 2.9 %update.1 = f32[16,4,48,128]{3,2,1,0:T(8,128)} custom-call(bf16[16,64]{1,0:T(8,128)(2,1)S(1)} %get-tuple-element.34.weights_ref, f32[16,4,48,128]{3,2,1,0:T(8,128)S(1)} %get-tuple-element.35.prior_ref, bf16[192,16,128]{2,1,0:T(8,128)(2,1)S(1)} %anomalies.1.refs_0_, bf16[192,16,128]{2,1,0:T(8,128)(2,1)S(1)} %get-tuple-element.36.refs_1_, ...), custom_call_target="tpu_custom_call" | custom-call | tf_op jit(solution)/shard_map/update/pallas_call | solution.py:547
  (29 shorter events, 0.1 us)
Async XLA Ops:
  2.4 16.1 %copy-start.6 = (f32[64,256]{1,0:T(8,128)S(1)}, f32[64,256]{1,0:T(8,128)}, u32[]{:S(2)}) copy-start(f32[64,256]{1,0:T(8,128)} %noise_ref.1) | copy-start | bytes 196612
  2.4 16.1 %copy-start.8 = (s32[256]{0:T(256)S(1)}, s32[256]{0:T(256)}, u32[]{:S(2)}) copy-start(s32[256]{0:T(256)} %param.12) | copy-start | bytes 3076
  2.4 16.1 %copy-start.9 = (f32[256]{0:T(256)S(1)}, f32[256]{0:T(256)}, u32[]{:S(2)}) copy-start(f32[256]{0:T(256)} %param.13) | copy-start | bytes 3076
  2.5 16.1 %copy-start.10 = (f32[256]{0:T(256)S(1)}, f32[256]{0:T(256)}, u32[]{:S(2)}) copy-start(f32[256]{0:T(256)} %param.14) | copy-start | bytes 3076
  2.5 20.0 %copy-start.2 = (f32[4,48,128]{2,1,0:T(8,128)S(1)}, f32[4,48,128]{2,1,0:T(8,128)}, u32[]{:S(2)}) copy-start(f32[4,48,128]{2,1,0:T(8,128)} %visc_ref.5) | copy-start | bytes 294916
  2.5 20.0 %copy-start.5 = (f32[4,48,128]{2,1,0:T(8,128)S(1)}, f32[4,48,128]{2,1,0:T(8,128)}, u32[]{:S(2)}) copy-start(f32[4,48,128]{2,1,0:T(8,128)} %flow_ref.3) | copy-start | bytes 294916
  2.5 20.0 %copy-start.7 = (s32[1,4]{1,0:T(1,128)S(1)}, s32[1,4]{1,0:T(1,128)}, u32[]{:S(2)}) copy-start(s32[1,4]{1,0:T(1,128)} %cells_ref.5) | copy-start | bytes 52
  2.5 19.2 %collective-permute-start.3 = (bf16[28,48,128]{2,1,0:T(8,128)(2,1)S(1)}, bf16[28,48,128]{2,1,0:T(8,128)(2,1)S(1)}, u32[]{:S(2)}, u32[]{:S(2)}) collective-permute-start(bf16[28,48,128]{2,1,0:T(8,128)(2,1)S(1)} %get-tuple-element.24), channel_id=1, source_target_pairs={{4,8},{12,16},{20,24},{28,32},{36,40},{44,48},{52,56},{60,64},{68,... | collective-permute-start | bytes 1032200 | tf_op jit(solution)/shard_map/ppermute | solution.py:568
  13.9 8.6 %collective-permute-start.2 = (bf16[28,48,128]{2,1,0:T(8,128)(2,1)S(1)}, bf16[28,48,128]{2,1,0:T(8,128)(2,1)S(1)}, u32[]{:S(2)}, u32[]{:S(2)}) collective-permute-start(bf16[28,48,128]{2,1,0:T(8,128)(2,1)S(1)} %get-tuple-element.23.after), channel_id=1, source_target_pairs={{0,4},{8,12},{16,20},{24,28},{32,36},{40,44},{48,52},{56,60},{64,6... | collective-permute-start | bytes 1032200 | tf_op jit(solution)/shard_map/ppermute | solution.py:568
  13.9 14.9 %collective-permute-start = (bf16[24,48,128]{2,1,0:T(8,128)(2,1)S(1)}, bf16[24,48,128]{2,1,0:T(8,128)(2,1)S(1)}, u32[]{:S(2)}, u32[]{:S(2)}) collective-permute-start(bf16[24,48,128]{2,1,0:T(8,128)(2,1)S(1)} %get-tuple-element.20), channel_id=1, source_target_pairs={{0,4},{8,12},{16,20},{24,28},{32,36},{40,44},{48,52},{56,60},{64,6... | collective-permute-start | bytes 884744 | tf_op jit(solution)/shard_map/ppermute | solution.py:568
  15.4 13.5 %collective-permute-start.1 = (bf16[24,48,128]{2,1,0:T(8,128)(2,1)S(1)}, bf16[24,48,128]{2,1,0:T(8,128)(2,1)S(1)}, u32[]{:S(2)}, u32[]{:S(2)}) collective-permute-start(bf16[24,48,128]{2,1,0:T(8,128)(2,1)S(1)} %get-tuple-element.21), channel_id=1, source_target_pairs={{4,8},{12,16},{20,24},{28,32},{36,40},{44,48},{52,56},{60,64},{68,... | collective-permute-start | bytes 884744 | tf_op jit(solution)/shard_map/ppermute | solution.py:568
  15.6 2.5 %collective-permute-start.4 = (f32[4,48,128]{2,1,0:T(8,128)S(1)}, f32[4,48,128]{2,1,0:T(8,128)S(1)}, u32[]{:S(2)}, u32[]{:S(2)}) collective-permute-start(f32[4,48,128]{2,1,0:T(8,128)S(1)} %total.1.a_ref), channel_id=1, source_target_pairs={{0,1},{1,0},{2,3},{3,2},{4,5},{5,4},{6,7},{7,6},{8,9},{9,8},{10,11... | collective-permute-start | bytes 294920 | tf_op jit(solution)/shard_map/ppermute | solution.py:571
  18.1 9.2 %collective-permute-start.5 = (f32[4,48,128]{2,1,0:T(8,128)S(1)}, f32[4,48,128]{2,1,0:T(8,128)S(1)}, u32[]{:S(2)}, u32[]{:S(2)}) collective-permute-start(f32[4,48,128]{2,1,0:T(8,128)S(1)} %pair_sum.1.a_ref), channel_id=1, source_target_pairs={{0,2},{1,3},{2,0},{3,1},{4,6},{5,7},{6,4},{7,5},{8,10},{9,11},{10,... | collective-permute-start | bytes 294920 | tf_op jit(solution)/shard_map/ppermute | solution.py:571
  27.3 2.6 %copy-start.3 = (f32[10,64,128]{2,1,0:T(8,128)}, f32[10,64,128]{2,1,0:T(8,128)S(1)}, u32[]{:S(2)}) copy-start(f32[10,64,128]{2,1,0:T(8,128)S(1)} %get-tuple-element.26.lap0.rest_0_) | copy-start | bytes 983044
  27.3 2.6 %copy-start.4 = (f32[10,64,128]{2,1,0:T(8,128)}, f32[10,64,128]{2,1,0:T(8,128)S(1)}, u32[]{:S(2)}) copy-start(f32[10,64,128]{2,1,0:T(8,128)S(1)} %get-tuple-element.27.adv0.rest_1_) | copy-start | bytes 983044
  28.8 1.1 %copy-start = (bf16[24,48,128]{2,1,0:T(8,128)(2,1)}, bf16[24,48,128]{2,1,0:T(8,128)(2,1)S(1)}, u32[]{:S(2)}) copy-start(bf16[24,48,128]{2,1,0:T(8,128)(2,1)S(1)} %collective-permute-done.inner_ref.refs_1_) | copy-start | bytes 884740
  28.8 1.1 %copy-start.1 = (bf16[24,48,128]{2,1,0:T(8,128)(2,1)}, bf16[24,48,128]{2,1,0:T(8,128)(2,1)S(1)}, u32[]{:S(2)}) copy-start(bf16[24,48,128]{2,1,0:T(8,128)(2,1)S(1)} %collective-permute-done.1.outer_ref.refs_2_) | copy-start | bytes 884740
  29.5 27.0 %collective-permute-start.7 = (bf16[192,16,128]{2,1,0:T(8,128)(2,1)S(1)}, bf16[192,16,128]{2,1,0:T(8,128)(2,1)S(1)}, u32[]{:S(2)}, u32[]{:S(2)}) collective-permute-start(bf16[192,16,128]{2,1,0:T(8,128)(2,1)S(1)} %anomalies.1.refs_0_), channel_id=1, source_target_pairs={{0,2},{1,3},{2,0},{3,1},{4,6},{5,7},{6,4},{7,5},{8,10},{9,11},{10,... | collective-permute-start | bytes 2359304 | tf_op jit(solution)/shard_map/ppermute | solution.py:571
  32.9 23.6 %all-to-all-start = ((f32[256,1,128]{2,1,0:T(1,128)}), f32[256,1,128]{2,1,0:T(1,128)S(1)}, u32[]{:S(2)}, u32[]{:S(2)}) async-start(f32[256,1,128]{2,1,0:T(1,128)} %bitcast.6), calls=%async_computation | async-start | bytes 262144 | tf_op jit(solution)/shard_map/all_to_all | solution.py:586
  43.6 13.6 %collective-permute-start.6 = (bf16[192,16,128]{2,1,0:T(8,128)(2,1)S(1)}, bf16[192,16,128]{2,1,0:T(8,128)(2,1)S(1)}, u32[]{:S(2)}, u32[]{:S(2)}) collective-permute-start(bf16[192,16,128]{2,1,0:T(8,128)(2,1)S(1)} %anomalies.1.refs_0_), channel_id=1, source_target_pairs={{0,1},{1,0},{2,3},{3,2},{4,5},{5,4},{6,7},{7,6},{8,9},{9,8},{10,11... | collective-permute-start | bytes 2359304 | tf_op jit(solution)/shard_map/ppermute | solution.py:571
  56.5 2.7 %collective-permute-start.8 = (bf16[192,16,128]{2,1,0:T(8,128)(2,1)S(1)}, bf16[192,16,128]{2,1,0:T(8,128)(2,1)}, u32[]{:S(2)}, u32[]{:S(2)}) collective-permute-start(bf16[192,16,128]{2,1,0:T(8,128)(2,1)S(1)} %hold.1.refs_2_), channel_id=1, source_target_pairs={{0,1},{1,0},{2,3},{3,2},{4,5},{5,4},{6,7},{7,6},{8,9},{9,8},{10,11... | collective-permute-start | bytes 2359304 | tf_op jit(solution)/shard_map/ppermute | solution.py:571
